TPU v7x, 512 devices: a whole 4x4x16 slice. The times are simulated.
512 devices in a mesh: tok: 32 (over x_lo, z), feat: 16 (over y, x_hi, core).
Axes of the slice: x: 4 (x_hi: 2, x_lo: 2; x = x_hi * 2 + x_lo), y: 4, z: 16, core: 2. Of those that a mesh axis runs over, the one named last changes fastest.
Arguments:
- activations: float32 [65536, 8192], P('tok', 'feat'), may hold values from -200 to 200, as said below
- sketch: float32 [8192, 128], P('feat'), may hold values from -0.0625 to 0.0625
Outputs:
- first_basis: float32 [65536, 128], P(('tok', 'feat'))
- range_basis: float32 [65536, 128], P(('tok', 'feat'))
- triangle: float32 [128, 128], replicated
Inputs may be any that keep to these rules, and one draw needn't show every extreme that they name: activations of one layer, real valued.
All inputs are finite; a program needn't handle non-finite values.
Results may differ from a plain program's by a relative error of at most 0.000078.
Values sent between devices are 32-bit elements; how exact they have to be, the bound alone decides.
No kernel may reach another device: no remote copies, remote signals or barrier semaphores. Data moves between devices by JAX's collectives and lax.ppermute only.
A program may use at most 64 MiB of HBM per device.

v0:
```python
import jax
import jax.numpy as jnp
from jax import lax
from jax.sharding import PartitionSpec as P

TOP = lax.Precision.HIGHEST


def product(left_side, right_side):
    return jnp.dot(left_side, right_side, precision=TOP, preferred_element_type=jnp.float32)


def inner_product(left_side, right_side):
    return lax.dot_general(
        left_side,
        right_side,
        (((0,), (0,)), ((), ())),
        precision=TOP,
        preferred_element_type=jnp.float32,
    )


def factor(gram_matrix):
    lower_factor = jnp.linalg.cholesky(gram_matrix)
    identity = jnp.eye(gram_matrix.shape[0], dtype=jnp.float32)
    inverse = jax.scipy.linalg.solve_triangular(lower_factor, identity, lower=True)
    return (lower_factor, inverse)


def per_device(activations, sketch):
    row_count = activations.shape[0]
    tok_count = lax.axis_size("tok")
    feat_count = lax.axis_size("feat")
    row_block = row_count // feat_count
    feat_index = lax.axis_index("feat")
    image = lax.psum(product(activations, sketch), "feat")
    gram_first = lax.psum(inner_product(image, image), "tok")
    unused_first, inverse_first = factor(gram_first)
    first_basis = product(image, inverse_first.T)
    first_block = lax.dynamic_slice_in_dim(first_basis, feat_index * row_block, row_block, 0)
    back_image = lax.psum(inner_product(activations, first_basis), "tok")
    gram_back = lax.psum(inner_product(back_image, back_image), "feat")
    unused_back, inverse_back = factor(gram_back)
    weights = product(back_image, inverse_back.T)
    range_image = lax.psum(product(activations, weights), "feat")
    gram_last = lax.psum(inner_product(range_image, range_image), "tok")
    lower_factor, inverse_last = factor(gram_last)
    range_block = lax.dynamic_slice_in_dim(range_image, feat_index * row_block, row_block, 0)
    range_basis = product(range_block, inverse_last.T)
    triangle = lower_factor / jnp.sqrt(jnp.float32(row_count * tok_count))
    return (first_block, range_basis, triangle)


def solution(mesh):
    return jax.shard_map(
        per_device,
        mesh=mesh,
        in_specs=(P("tok", "feat"), P("feat", None)),
        out_specs=(P(("tok", "feat"), None), P(("tok", "feat"), None), P()),
        check_vma=False,
    )
```

profile of v0, /device:TPU:1, one launch (start us, length us, event | category | flops | bytes accessed | tf_op | source)
XLA Modules:
  0.0 1286.0 jit_solution(15755723937095555969)
XLA Ops:
  7.2 0.0 copy-start
  7.2 0.0 all-reduce.7.cloned.1.call-start
  7.2 0.9 copy-done
  8.1 6.7 fusion.18
  14.8 0.0 all-reduce.7.cloned.1.call-update
  14.8 0.0 all-reduce.9.cloned.1.call-start
  14.9 161.0 %all-reduce.7.cloned.1.call-done = f32[2048,128]{1,0:T(8,128)} async-done(((f32[2048,128]{1,0:T(8,128)}), f32[2048,128]{1,0:T(8,128)}) %all-reduce.7.cloned.1.call-update) | async-done | bytes 1048592 | tf_op jit(solution)/shard_map/psum | solution.py:36
  175.9 4.0 fusion.19
  179.9 0.0 all-reduce.9.cloned.1.call-update
  179.9 0.2 all-reduce.11.cloned.1.call-start
  180.1 216.7 %all-reduce.9.cloned.1.call-done = f32[128,128]{0,1:T(8,128)} async-done(((f32[128,128]{0,1:T(8,128)}), f32[128,128]{0,1:T(8,128)}) %all-reduce.9.cloned.1.call-update) | async-done | bytes 65552 | tf_op jit(solution)/shard_map/psum | solution.py:37
  396.8 0.9 copy.6
  397.7 0.9 fusion.13
  398.6 11.7 cholesky.59
  410.3 0.6 compare_reduce_fusion.2
  411.0 0.7 fusion.6
  411.6 9.8 custom-call.7
  421.4 0.3 fusion.4
  421.7 2.2 fusion.20
  424.0 5.5 convolution_bitcast_fusion.1
  429.5 0.0 all-reduce.11.cloned.1.call-update
  429.5 0.0 all-reduce.13.cloned.1.call-start
  429.5 253.1 %all-reduce.11.cloned.1.call-done = f32[512,128]{0,1:T(8,128)} async-done(((f32[512,128]{0,1:T(8,128)}), f32[512,128]{0,1:T(8,128)}) %all-reduce.11.cloned.1.call-update) | async-done | bytes 262160 | tf_op jit(solution)/shard_map/psum | solution.py:41
  682.6 2.0 fusion.21
  684.7 0.0 all-reduce.13.cloned.1.call-update
  684.7 0.3 all-reduce.15.cloned.1.call-start
  685.0 156.6 %all-reduce.13.cloned.1.call-done = f32[128,128]{0,1:T(8,128)} async-done(((f32[128,128]{0,1:T(8,128)}), f32[128,128]{0,1:T(8,128)}) %all-reduce.13.cloned.1.call-update) | async-done | bytes 65552 | tf_op jit(solution)/shard_map/psum | solution.py:42
  841.6 0.9 copy.8
  842.5 0.9 fusion.11
  843.4 11.7 cholesky.70
  855.1 0.6 compare_reduce_fusion.1
  855.8 0.7 fusion.7
  856.4 9.8 custom-call.8
  866.3 0.3 fusion.2
  866.6 1.5 fusion.22
  868.1 7.8 convolution_bitcast_fusion
  875.9 0.0 all-reduce.15.cloned.1.call-update
  875.9 0.3 all-reduce.17.cloned.1.call-start
  876.2 155.2 %all-reduce.15.cloned.1.call-done = f32[2048,128]{0,1:T(8,128)} async-done(((f32[2048,128]{0,1:T(8,128)}), f32[2048,128]{0,1:T(8,128)}) %all-reduce.15.cloned.1.call-update) | async-done | bytes 1048592 | tf_op jit(solution)/shard_map/psum | solution.py:45
  1031.4 3.2 fusion.23
  1034.6 0.0 all-reduce.17.cloned.1.call-update
  1034.6 0.6 constant_dynamic-slice_fusion
  1035.3 216.5 %all-reduce.17.cloned.1.call-done = f32[128,128]{0,1:T(8,128)} async-done(((f32[128,128]{0,1:T(8,128)}), f32[128,128]{0,1:T(8,128)}) %all-reduce.17.cloned.1.call-update) | async-done | bytes 65552 | tf_op jit(solution)/shard_map/psum | solution.py:46
  1251.8 0.9 copy.10
  1252.7 0.9 fusion.9
  1253.6 11.7 cholesky.81
  1265.3 0.6 compare_reduce_fusion
  1266.0 1.3 fusion.16
  1267.3 9.8 custom-call.9
  1277.1 0.3 fusion
  1277.4 1.8 fusion.14
  (3 shorter events, 0.1 us)
Async XLA Ops:
  7.2 1.0 copy-start
  7.2 168.7 %all-reduce.7.cloned.1.call-start = ((), (), s32[]{:S(2)}) async-start(), calls=%async_computation | async-start | bytes 2097152 | tf_op jit(solution)/shard_map/psum | solution.py:36
  14.8 382.0 %all-reduce.9.cloned.1.call-start = ((), (), s32[]{:S(2)}) async-start(), calls=%async_computation.1 | async-start | bytes 131072 | tf_op jit(solution)/shard_map/psum | solution.py:37
  179.9 502.8 %all-reduce.11.cloned.1.call-start = ((), (), s32[]{:S(2)}) async-start(), calls=%async_computation.2 | async-start | bytes 524288 | tf_op jit(solution)/shard_map/psum | solution.py:41
  429.5 412.1 %all-reduce.13.cloned.1.call-start = ((), (), s32[]{:S(2)}) async-start(), calls=%async_computation.3 | async-start | bytes 131072 | tf_op jit(solution)/shard_map/psum | solution.py:42
  684.7 346.7 %all-reduce.15.cloned.1.call-start = ((), (), s32[]{:S(2)}) async-start(), calls=%async_computation.4 | async-start | bytes 2097152 | tf_op jit(solution)/shard_map/psum | solution.py:45
  875.9 375.9 %all-reduce.17.cloned.1.call-start = ((), (), s32[]{:S(2)}) async-start(), calls=%async_computation.5 | async-start | bytes 131072 | tf_op jit(solution)/shard_map/psum | solution.py:46
Sparse Core Ops, SparseCore 0:
  14.9 160.8 all-reduce.6
  180.0 216.7 all-reduce.8
  429.6 253.0 all-reduce.10
  686.2 155.3 all-reduce.12
  876.0 155.3 all-reduce.14
  1035.0 216.7 all-reduce.16
where the time goes:
time: 1310 us; the launch traced here: 1290 us
  waiting for transfers between devices  1160 us (89%)
  other arithmetic  71.8 us (5%)
  matrix products  35.5 us (3%)
  between operations  14.2 us (1%)
    psum x1, waiting for transfers between devices, per_device(): back_image = lax.psum(inner_product(activations, first_basis), 'tok')  253 us
    psum x1, waiting for transfers between devices, per_device(): gram_first = lax.psum(inner_product(image, image), 'tok')  217 us
    psum x1, waiting for transfers between devices, per_device(): gram_last = lax.psum(inner_product(range_image, range_image), 'tok')  217 us
    psum x1, waiting for transfers between devices, per_device(): image = lax.psum(product(activations, sketch), 'feat')  161 us
    psum x1, waiting for transfers between devices, per_device(): gram_back = lax.psum(inner_product(back_image, back_image), 'feat')  157 us
    psum x1, waiting for transfers between devices, per_device(): range_image = lax.psum(product(activations, weights), 'feat')  155 us
    another operation x9, other arithmetic, factor(): lower_factor = jnp.linalg.cholesky(gram_matrix)  37.2 us
    another operation x5, other arithmetic, factor(): jax.scipy.linalg.solve_triangular(lower_factor, identity, lower=True)  30.7 us
  transfers between devices with their start and end apart: 6, of which 6 were waited for; matrix products, arithmetic and copies ran while one was open for 0% of the time, Pallas kernels for 0%

commit v1 on v0

--- a/solution.py
+++ b/solution.py
@@ -27,25 +27,47 @@
     return (lower_factor, inverse)
 
 
+def scatter_sum(parts, axis):
+    return jnp.sum(lax.all_to_all(parts, axis, 0, 0), axis=0)
+
+
+def gather(block, axis):
+    count = lax.axis_size(axis)
+    return lax.all_to_all(jnp.broadcast_to(block[None], (count,) + block.shape), axis, 0, 0)
+
+
 def per_device(activations, sketch):
-    row_count = activations.shape[0]
+    row_count, column_count = activations.shape
+    width = sketch.shape[1]
     tok_count = lax.axis_size("tok")
     feat_count = lax.axis_size("feat")
     row_block = row_count // feat_count
-    feat_index = lax.axis_index("feat")
-    image = lax.psum(product(activations, sketch), "feat")
-    gram_first = lax.psum(inner_product(image, image), "tok")
+    image_part = product(activations, sketch)
+    image_block = scatter_sum(image_part.reshape(feat_count, row_block, width), "feat")
+    image = gather(image_block, "feat").reshape(row_count, width)
+    back_part = inner_product(activations, image).reshape(tok_count, -1, width)
+    gram_part = inner_product(image, image).reshape(tok_count, -1, width)
+    back_rows = back_part.shape[1]
+    gram_rows = gram_part.shape[1]
+    sums = scatter_sum(jnp.concatenate([back_part, gram_part], axis=1), "tok")
+    both = gather(sums, "tok")
+    back_raw = both[:, :back_rows].reshape(column_count, width)
+    gram_first = both[:, back_rows:].reshape(width, width)
     unused_first, inverse_first = factor(gram_first)
-    first_basis = product(image, inverse_first.T)
-    first_block = lax.dynamic_slice_in_dim(first_basis, feat_index * row_block, row_block, 0)
-    back_image = lax.psum(inner_product(activations, first_basis), "tok")
-    gram_back = lax.psum(inner_product(back_image, back_image), "feat")
+    first_block = product(image_block, inverse_first.T)
+    back_image = product(back_raw, inverse_first.T)
+    range_part = product(activations, back_image).reshape(feat_count, row_block, width)
+    gram_part = inner_product(back_image, back_image).reshape(feat_count, -1, width)
+    gram_rows = gram_part.shape[1]
+    sums = scatter_sum(jnp.concatenate([range_part, gram_part], axis=1), "feat")
+    gram_back = gather(sums[row_block:], "feat").reshape(width, width)
     unused_back, inverse_back = factor(gram_back)
-    weights = product(back_image, inverse_back.T)
-    range_image = lax.psum(product(activations, weights), "feat")
-    gram_last = lax.psum(inner_product(range_image, range_image), "tok")
+    range_block = product(sums[:row_block], inverse_back.T)
+    gram_part = inner_product(range_block, range_block).reshape(feat_count, -1, width)
+    gram_slice = scatter_sum(gram_part, "feat")
+    gram_slice = jnp.sum(gather(gram_slice, "tok"), axis=0)
+    gram_last = gather(gram_slice, "feat").reshape(width, width)
     lower_factor, inverse_last = factor(gram_last)
-    range_block = lax.dynamic_slice_in_dim(range_image, feat_index * row_block, row_block, 0)
     range_basis = product(range_block, inverse_last.T)
     triangle = lower_factor / jnp.sqrt(jnp.float32(row_count * tok_count))
     return (first_block, range_basis, triangle)

time: 1310 us -> 289 us (0.22); the launches traced: 1290 us -> 289 us
  waiting for transfers between devices: 1160 us -> 6.49 us
  blocking collectives: 0 us -> 180 us
  between operations: 14.2 us -> 0.9 us
    psum x6 -> x0, waiting for transfers between devices: 1160 us -> none  [the longest x1 253 us: per_device(): back_image = lax.psum(inner_product(activations, first_basis), 'tok')]
    all_to_all x0 -> x8, blocking collectives: none -> 180 us  [the longest x4 99.3 us: scatter_sum(): return jnp.sum(lax.all_to_all(parts, axis, 0, 0), axis=0)]
  transfers between devices with their start and end apart: 6 -> 1, of which waited for: 6 -> 1; matrix products, arithmetic and copies ran while one was open for 0% -> 0% of each run, Pallas kernels for 0% -> 0%
where the time goes in v1:
time: 289 us
  blocking collectives  180 us (62%)
  other arithmetic  69.6 us (24%)
  matrix products  22.6 us (8%)
  waiting for transfers between devices  6.49 us (2%)
  starting transfers between devices  6.04 us (2%)
  local copies, waits for them, and re-layouts  3.15 us (1%)
    all_to_all x4, blocking collectives, scatter_sum(): return jnp.sum(lax.all_to_all(parts, axis, 0, 0), axis=0)  99.3 us
    all_to_all x4, blocking collectives, gather(): lax.all_to_all(jnp.broadcast_to(block[None], (count,) + block.shape), axi...  80.6 us
    another operation x9, other arithmetic, factor(): lower_factor = jnp.linalg.cholesky(gram_matrix)  37.2 us
    another operation x5, other arithmetic, factor(): jax.scipy.linalg.solve_triangular(lower_factor, identity, lower=True)  30.7 us
    dot_general x6, matrix products, product(): jnp.dot(left_side, right_side, precision=TOP, preferred_element_type=jnp....  14.4 us
    dot_general x4, matrix products, inner_product(): lax.dot_general(left_side, right_side, (((0,), (0,)), ((), ())), precisio...  7.34 us
    all_to_all x1, waiting for transfers between devices, gather(): lax.all_to_all(jnp.broadcast_to(block[None], (count,) + block.shape), axi...  6.49 us
    all_to_all x1, starting transfers between devices, gather(): lax.all_to_all(jnp.broadcast_to(block[None], (count,) + block.shape), axi...  6.04 us
  transfers between devices with their start and end apart: 1, of which 1 were waited for; matrix products, arithmetic and copies ran while one was open for 0% of the time, Pallas kernels for 0%

profile of v1, /device:TPU:1, one launch (start us, length us, event | category | flops | bytes accessed | tf_op | source)
XLA Modules:
  0.0 288.7 jit_solution(12046573767262628874)
XLA Ops:
  0.6 0.0 copy-start
  0.6 0.9 copy-done
  1.6 5.2 %fusion.19 = f32[2048,128]{1,0:T(8,128)S(1)} fusion(f32[2048,512]{1,0:T(8,128)} %param.5, f32[512,128]{1,0:T(8,128)S(1)} %copy-done), kind=kOutput, calls=%fused_computation.40 | convolution fusion | flops 1610612736 | bytes 5505024 | tf_op jit(solution)/shard_map/dot_general | solution.py:10
  6.8 26.3 %all_to_all.45 = f32[16,128,128]{2,1,0:T(8,128)S(1)} all-to-all(f32[16,128,128]{2,1,0:T(8,128)S(1)} %bitcast.71), channel_id=1, replica_groups=mesh['tok'=32,'feat'=16] {'feat'}, dimensions={0} | all-to-all | bytes 2097152 | tf_op jit(solution)/shard_map/all_to_all | solution.py:31
  33.1 0.1 reduce_sum.45
  33.2 0.1 broadcast_in_dim.11
  33.3 20.6 %all_to_all.46 = f32[16,128,128]{2,1,0:T(8,128)S(1)} all-to-all(f32[16,128,128]{2,1,0:T(8,128)S(1)} %broadcast_in_dim.11), channel_id=1, replica_groups=mesh['tok'=32,'feat'=16] {'feat'}, dimensions={0} | all-to-all | bytes 2097152 | tf_op jit(solution)/shard_map/all_to_all | solution.py:36
  53.9 0.3 copy.30
  54.2 0.3 dot_general.42
  54.5 1.7 fusion
  56.3 4.8 %convolution_bitcast_fusion.1 = f32[512,128]{0,1:T(8,128)S(1)} fusion(f32[2048,128]{1,0:T(8,128)S(1)} %bitcast.69, f32[2048,512]{1,0:T(8,128)} %param.5), kind=kOutput, calls=%fused_computation.1 | convolution fusion | flops 1610612736 | bytes 5505024 | tf_op jit(solution)/shard_map/dot_general | solution.py:14
  61.1 0.1 copy.29
  61.2 38.1 %all_to_all.47 = f32[32,20,128]{2,1,0:T(8,128)S(1)} all-to-all(f32[32,20,128]{2,1,0:T(8,128)S(1)} %pad_maximum_fusion.1), channel_id=1, replica_groups=mesh['tok'=32,'feat'=16] {'tok'}, dimensions={0} | all-to-all | bytes 655360 | tf_op jit(solution)/shard_map/all_to_all | solution.py:31
  99.4 31.5 %all_to_all.48 = f32[32,20,128]{2,1,0:T(8,128)S(1)} all-to-all(f32[32,20,128]{2,1,0:T(8,128)S(1)} %broadcast_in_dim.12), channel_id=1, replica_groups=mesh['tok'=32,'feat'=16] {'tok'}, dimensions={0} | all-to-all | bytes 655360 | tf_op jit(solution)/shard_map/all_to_all | solution.py:36
  130.9 0.1 copy.33
  131.0 11.7 %cholesky.59 = f32[128,128]{1,0:T(8,128)S(1)} custom-call(f32[128,128]{1,0:T(8,128)S(1)} %fusion.17), custom_call_target="Cholesky" | custom-call | tf_op jit(solution)/shard_map/jit(cholesky)/cholesky | solution.py:24
  142.8 0.6 compare_reduce_fusion.2
  143.4 0.7 fusion.8
  144.1 9.8 %custom-call.7 = f32[1,128,128]{1,2,0:T(8,128)S(1)} custom-call(f32[1,128,128]{2,1,0:T(8,128)S(1)} %fusion.8), custom_call_target="InvertDiagBlocksLowerTriangular" | custom-call | tf_op jit(solution)/shard_map/jit(_solve_triangular)/triangular_solve | solution.py:26
  153.9 0.3 fusion.6
  154.2 0.4 fusion.21
  154.6 6.8 %convolution_bitcast_fusion = f32[2048,128]{0,1:T(8,128)S(1)} fusion(f32[512,128]{1,0:T(8,128)S(1)} %fusion.21, f32[2048,512]{1,0:T(8,128)} %param.5), kind=kOutput, calls=%fused_computation | convolution fusion | flops 1610612736 | bytes 5505024 | tf_op jit(solution)/shard_map/dot_general | solution.py:10
  161.4 0.6 convolution_bitcast_fusion.3
  162.0 0.3 copy.39
  162.3 0.1 pad_maximum_fusion
  162.4 24.7 %all_to_all.49 = f32[16,136,128]{2,1,0:T(8,128)S(1)} all-to-all(f32[16,136,128]{2,1,0:T(8,128)S(1)} %pad_maximum_fusion), channel_id=1, replica_groups=mesh['tok'=32,'feat'=16] {'feat'}, dimensions={0} | all-to-all | bytes 2228224 | tf_op jit(solution)/shard_map/all_to_all | solution.py:31
  187.1 0.1 reduce_sum.47
  187.2 10.2 %all_to_all.50 = f32[16,8,128]{2,1,0:T(8,128)S(1)} all-to-all(f32[16,8,128]{2,1,0:T(8,128)S(1)} %broadcast_in_dim.13), channel_id=1, replica_groups=mesh['tok'=32,'feat'=16] {'feat'}, dimensions={0} | all-to-all | bytes 131072 | tf_op jit(solution)/shard_map/all_to_all | solution.py:36
  197.4 0.1 copy.37
  197.5 11.7 %cholesky.70 = f32[128,128]{1,0:T(8,128)S(1)} custom-call(f32[128,128]{1,0:T(8,128)S(1)} %fusion.15), custom_call_target="Cholesky" | custom-call | tf_op jit(solution)/shard_map/jit(cholesky)/cholesky | solution.py:24
  209.3 0.6 compare_reduce_fusion.1
  209.9 0.7 fusion.9
  210.6 9.8 %custom-call.8 = f32[1,128,128]{1,2,0:T(8,128)S(1)} custom-call(f32[1,128,128]{2,1,0:T(8,128)S(1)} %fusion.9), custom_call_target="InvertDiagBlocksLowerTriangular" | custom-call | tf_op jit(solution)/shard_map/jit(_solve_triangular)/triangular_solve | solution.py:26
  220.4 0.3 fusion.4
  220.7 0.3 fusion.10
  220.9 0.3 convolution_bitcast_fusion.2
  221.2 10.2 %all_to_all.51 = f32[16,8,128]{2,1,0:T(8,128)S(1)} all-to-all(f32[16,8,128]{2,1,0:T(8,128)S(1)} %convolution_bitcast_fusion.2), channel_id=1, replica_groups=mesh['tok'=32,'feat'=16] {'feat'}, dimensions={0} | all-to-all | bytes 131072 | tf_op jit(solution)/shard_map/all_to_all | solution.py:31
  231.5 18.3 %all_to_all.52 = f32[32,8,128]{2,1,0:T(8,128)S(1)} all-to-all(f32[32,8,128]{2,1,0:T(8,128)S(1)} %broadcast_in_dim.14), channel_id=1, replica_groups=mesh['tok'=32,'feat'=16] {'tok'}, dimensions={0} | all-to-all | bytes 262144 | tf_op jit(solution)/shard_map/all_to_all | solution.py:36
  249.8 0.6 broadcast_in_dim.15
  250.5 6.0 %all-to-all-start.8 = ((f32[16,8,128]{2,1,0:T(8,128)}), f32[16,8,128]{2,1,0:T(8,128)S(1)}, u32[]{:S(2)}, u32[]{:S(2)}) async-start(f32[16,8,128]{2,1,0:T(8,128)} %broadcast_in_dim.15), calls=%async_computation.8 | async-start | bytes 131072 | tf_op jit(solution)/shard_map/all_to_all | solution.py:36
  256.5 0.9 fusion.20
  257.4 6.5 %all-to-all-done.8 = f32[16,8,128]{2,1,0:T(8,128)S(1)} async-done(((f32[16,8,128]{2,1,0:T(8,128)}), f32[16,8,128]{2,1,0:T(8,128)S(1)}, u32[]{:S(2)}, u32[]{:S(2)}) %all-to-all-start.8) | async-done | bytes 65568 | tf_op jit(solution)/shard_map/all_to_all | solution.py:36
  263.9 0.1 copy.38
  264.0 11.7 %cholesky.81 = f32[128,128]{1,0:T(8,128)S(1)} custom-call(f32[128,128]{1,0:T(8,128)S(1)} %fusion.13), custom_call_target="Cholesky" | custom-call | tf_op jit(solution)/shard_map/jit(cholesky)/cholesky | solution.py:24
  275.8 0.6 compare_reduce_fusion
  276.4 1.3 fusion.18
  277.7 9.8 %custom-call.9 = f32[1,128,128]{1,2,0:T(8,128)S(1)} custom-call(f32[1,128,128]{2,1,0:T(8,128)S(1)} %get-tuple-element.6), custom_call_target="InvertDiagBlocksLowerTriangular" | custom-call | tf_op jit(solution)/shard_map/jit(_solve_triangular)/triangular_solve | solution.py:26
  287.5 0.3 fusion.2
  287.8 0.9 fusion.22
  (17 shorter events, 0.4 us)
Async XLA Ops:
  0.6 1.0 copy-start
  250.5 13.4 %all-to-all-start.8 = ((f32[16,8,128]{2,1,0:T(8,128)}), f32[16,8,128]{2,1,0:T(8,128)S(1)}, u32[]{:S(2)}, u32[]{:S(2)}) async-start(f32[16,8,128]{2,1,0:T(8,128)} %broadcast_in_dim.15), calls=%async_computation.8 | async-start | bytes 131072 | tf_op jit(solution)/shard_map/all_to_all | solution.py:36

commit v2 on v0

v2 whole, which is shorter than its diff:
```python
import jax
import jax.numpy as jnp
from jax import lax
from jax.experimental import pallas as pl
from jax.sharding import Mesh, PartitionSpec as P

TOP = lax.Precision.HIGHEST
PANEL = 8
SWAP = [(0, 1), (1, 0)]


def product(left_side, right_side):
    return jnp.dot(left_side, right_side, precision=TOP, preferred_element_type=jnp.float32)


def inner_product(left_side, right_side):
    return lax.dot_general(
        left_side,
        right_side,
        (((0,), (0,)), ((), ())),
        precision=TOP,
        preferred_element_type=jnp.float32,
    )


def outer_product(left_side, right_side):
    return lax.dot_general(
        left_side,
        right_side,
        (((1,), (1,)), ((), ())),
        precision=TOP,
        preferred_element_type=jnp.float32,
    )


def eliminate(gram):
    n = gram.shape[0]
    count = n // 8
    tile = (8, n)
    row = lax.broadcasted_iota(jnp.int32, tile, 0)
    lane = lax.broadcasted_iota(jnp.int32, tile, 1)
    left = [gram[8 * u : 8 * u + 8, :] for u in range(count)]
    right = [jnp.where(lane == row + 8 * u, 1.0, 0.0).astype(jnp.float32) for u in range(count)]
    for v in range(count):
        start = 8 * v
        rows = [jnp.broadcast_to(left[v][i : i + 1, :], tile) for i in range(PANEL)]
        more = [jnp.broadcast_to(right[v][i : i + 1, :], tile) for i in range(PANEL)]
        columns = [
            [jnp.broadcast_to(left[u][:, start + i : start + i + 1], tile) for u in range(v, count)]
            for i in range(PANEL)
        ]
        corner = [
            [jnp.broadcast_to(rows[i][:, start + m : start + m + 1], tile) for m in range(PANEL)]
            for i in range(PANEL)
        ]
        factors = []
        for i in range(PANEL):
            inverse = 1.0 / corner[i][i]
            factor = [c * inverse for c in columns[i]]
            for m in range(i + 1, PANEL):
                weight = corner[i][m] * inverse
                for q in range(m, PANEL):
                    corner[m][q] = corner[m][q] - weight * corner[i][q]
                rows[m] = rows[m] - weight * rows[i]
                more[m] = more[m] - weight * more[i]
                columns[m] = [c - f * corner[i][m] for c, f in zip(columns[m], factor)]
            factor[0] = jnp.where(row > i, factor[0], 0.0)
            factors.append(factor)
        for u in range(v, count):
            a, b = left[u], right[u]
            for i in range(PANEL):
                a = a - factors[i][u - v] * rows[i]
                b = b - factors[i][u - v] * more[i]
            left[u], right[u] = a, b
    upper, inverse = [], []
    for u in range(count):
        pivots = jnp.sum(jnp.where(lane == row + 8 * u, left[u], 0.0), axis=1, keepdims=True)
        scale = lax.rsqrt(pivots)
        upper.append(jnp.where(lane >= row + 8 * u, left[u] * scale, 0.0))
        inverse.append(right[u] * scale)
    return jnp.concatenate(upper, 0), jnp.concatenate(inverse, 0)


def factor_kernel(gram_ref, upper_ref, inverse_ref):
    upper_ref[...], inverse_ref[...] = eliminate(gram_ref[...])


def factor(gram_matrix):
    like = jax.ShapeDtypeStruct(gram_matrix.shape, jnp.float32)
    return pl.pallas_call(
        factor_kernel,
        out_shape=[like, like],
        name="factor",
        cost_estimate=pl.CostEstimate(flops=20_000_000, bytes_accessed=200_000, transcendentals=0),
    )(gram_matrix)


def scatter_sum(parts, axis):
    return jnp.sum(lax.all_to_all(parts, axis, 0, 0), axis=0)


def gather(block, axis):
    count = lax.axis_size(axis)
    return lax.all_to_all(jnp.broadcast_to(block[None], (count,) + block.shape), axis, 0, 0)


def take(array, index, axis):
    return lax.dynamic_index_in_dim(array, index, axis, keepdims=False)


def per_device(activations, sketch):
    row_count, column_count = activations.shape
    width = sketch.shape[1]
    core = lax.axis_index("core")
    side = lax.axis_index("x_lo")
    plane = ("y", "x_hi")
    plane_count = lax.axis_size("y") * lax.axis_size("x_hi")
    z_count = lax.axis_size("z")
    row_block = row_count // (2 * plane_count)
    half = column_count // 2
    parts = product(activations, sketch).reshape(plane_count, 2, row_block, width)
    received = lax.ppermute(take(parts, 1 - core, 1), "core", SWAP)
    image_block = scatter_sum(take(parts, core, 1) + received, plane)
    mine = gather(image_block, plane)
    other = lax.ppermute(mine, "core", SWAP)
    is_first = core == 0
    image = jnp.stack([jnp.where(is_first, mine, other), jnp.where(is_first, other, mine)], axis=1)
    image = image.reshape(row_count, width)
    back_part = inner_product(activations, image).reshape(2, half, width)
    gram_part = inner_product(image, image)
    received = lax.ppermute(jnp.concatenate([take(back_part, 1 - side, 0), gram_part], axis=0), "x_lo", SWAP)
    back_sum = (take(back_part, side, 0) + received[:half]).reshape(z_count, -1, width)
    gram_sum = (gram_part + received[half:]).reshape(z_count, -1, width)
    back_rows = back_sum.shape[1]
    sums = scatter_sum(jnp.concatenate([back_sum, gram_sum], axis=1), "z")
    both = gather(sums, "z")
    gram_first = both[:, back_rows:].reshape(width, width)
    back_mine = both[:, :back_rows].reshape(half, width)
    back_other = lax.ppermute(back_mine, "x_lo", SWAP)
    unused_first, inverse_first = factor(gram_first)
    is_low = side == 0
    back_raw = jnp.concatenate(
        [jnp.where(is_low, back_mine, back_other), jnp.where(is_low, back_other, back_mine)], axis=0
    )
    first_block = outer_product(image_block, inverse_first)
    back_image = outer_product(back_raw, inverse_first)
    parts = product(activations, back_image).reshape(plane_count, 2, row_block, width)
    gram_part = inner_product(back_image, back_image)[None]
    received = lax.ppermute(jnp.concatenate([take(parts, 1 - core, 1), gram_part], axis=0), "core", SWAP)
    gram_part = jnp.broadcast_to(gram_part + received[plane_count:], (plane_count, width, width))
    parts = jnp.concatenate([take(parts, core, 1) + received[:plane_count], gram_part], axis=1)
    sums = scatter_sum(parts, plane)
    unused_back, inverse_back = factor(sums[row_block:])
    range_block = outer_product(sums[:row_block], inverse_back)
    feat = ("y", "x_hi", "core")
    gram_part = inner_product(range_block, range_block).reshape(2 * plane_count, -1, width)
    gram_slice = scatter_sum(gram_part, feat)
    gram_slice = jnp.sum(gather(gram_slice, ("x_lo", "z")), axis=0)
    gram_last = gather(gram_slice, feat).reshape(width, width)
    upper_factor, inverse_last = factor(gram_last)
    range_basis = outer_product(range_block, inverse_last)
    tokens = row_count * lax.axis_size("x_lo") * z_count
    triangle = upper_factor.T / jnp.sqrt(jnp.float32(tokens))
    return (first_block, range_basis, triangle)


def solution(mesh):
    fine = Mesh(mesh.devices.reshape(2, 16, 4, 2, 2), ("x_lo", "z", "y", "x_hi", "core"))
    tok, feat = ("x_lo", "z"), ("y", "x_hi", "core")
    return jax.shard_map(
        per_device,
        mesh=fine,
        in_specs=(P(tok, feat), P(feat, None)),
        out_specs=(P(tok + feat, None), P(tok + feat, None), P()),
        check_vma=False,
    )
```

time: 1310 us -> 224 us (0.17); the launches traced: 1290 us -> 223 us
  waiting for transfers between devices: 1160 us -> 29 us
  blocking collectives: 0 us -> 103 us
  other arithmetic: 71.8 us -> 1.48 us
  starting transfers between devices: 0.91 us -> 39.4 us
  Pallas kernels: 0 us -> 19 us
  between operations: 14.2 us -> 0.97 us
  matrix products: 35.5 us -> 22.4 us
    psum x6 -> x0, waiting for transfers between devices: 1160 us -> none  [the longest x1 253 us: per_device(): back_image = lax.psum(inner_product(activations, first_basis), 'tok')]
    all_to_all x0 -> x6, blocking collectives: none -> 103 us  [the longest x4 70.2 us: scatter_sum(): return jnp.sum(lax.all_to_all(parts, axis, 0, 0), axis=0)]
    another operation x14 -> x2, other arithmetic: 67.9 us -> 0.15 us  [per_device(): jnp.stack([jnp.where(is_first, mine, other), jnp.where(is_first, other, m...]
    ppermute x0 -> x5, starting transfers between devices: none -> 24.8 us  [the longest x1 8.79 us: per_device(): received = lax.ppermute(take(parts, 1 - core, 1), 'core', SWAP)]
    pallas_call x0 -> x3, Pallas kernels: none -> 19 us  [factor(): pl.pallas_call(factor_kernel, out_shape=[like, like], name='factor', cost...]
    all_to_all x0 -> x2, waiting for transfers between devices: none -> 18.8 us  [gather(): lax.all_to_all(jnp.broadcast_to(block[None], (count,) + block.shape), axi...]
    all_to_all x0 -> x2, starting transfers between devices: none -> 14.7 us  [gather(): lax.all_to_all(jnp.broadcast_to(block[None], (count,) + block.shape), axi...]
  transfers between devices with their start and end apart: 6 -> 7, of which waited for: 6 -> 6; matrix products, arithmetic and copies ran while one was open for 0% -> 1% of each run, Pallas kernels for 0% -> 3%
where the time goes in v2:
time: 224 us; the launch traced here: 223 us
  blocking collectives  103 us (46%)
  starting transfers between devices  39.4 us (18%)
  waiting for transfers between devices  29 us (13%)
  matrix products  22.4 us (10%)
  Pallas kernels  19 us (8%)
  local copies, waits for them, and re-layouts  8.21 us (4%)
    all_to_all x4, blocking collectives, scatter_sum(): return jnp.sum(lax.all_to_all(parts, axis, 0, 0), axis=0)  70.2 us
    all_to_all x2, blocking collectives, gather(): lax.all_to_all(jnp.broadcast_to(block[None], (count,) + block.shape), axi...  32.6 us
    pallas_call x3, Pallas kernels, factor(): pl.pallas_call(factor_kernel, out_shape=[like, like], name='factor', cost...  19 us
    all_to_all x2, waiting for transfers between devices, gather(): lax.all_to_all(jnp.broadcast_to(block[None], (count,) + block.shape), axi...  18.8 us
    all_to_all x2, starting transfers between devices, gather(): lax.all_to_all(jnp.broadcast_to(block[None], (count,) + block.shape), axi...  14.7 us
    dot_general x2, matrix products, product(): jnp.dot(left_side, right_side, precision=TOP, preferred_element_type=jnp....  12 us
    ppermute x1, starting transfers between devices, per_device(): received = lax.ppermute(take(parts, 1 - core, 1), 'core', SWAP)  8.79 us
    ppermute x1, starting transfers between devices, per_device(): lax.ppermute(jnp.concatenate([take(parts, 1 - core, 1), gram_part], axis=...  7.28 us
  transfers between devices with their start and end apart: 7, of which 6 were waited for; matrix products, arithmetic and copies ran while one was open for 1% of the time, Pallas kernels for 3%

profile of v2, /device:TPU:1, one launch (start us, length us, event | category | flops | bytes accessed | tf_op | source)
XLA Modules:
  0.0 223.4 jit_solution(6093228233462333137)
XLA Ops:
  0.6 0.0 copy-start
  0.7 0.9 copy-done
  1.6 5.2 %fusion.9 = f32[2048,128]{1,0:T(8,128)S(1)} fusion(f32[2048,512]{1,0:T(8,128)} %param.2, f32[512,128]{1,0:T(8,128)S(1)} %copy-done), kind=kOutput, calls=%fused_computation.35 | convolution fusion | flops 1610612736 | bytes 5505024 | tf_op jit(solution)/shard_map/dot_general | solution.py:13
  6.9 8.8 %collective-permute-start = (f32[8,128,128]{2,1,0:T(8,128)S(1)}, f32[8,128,128]{2,1,0:T(8,128)S(1)}, u32[]{:S(2)}, u32[]{:S(2)}) collective-permute-start(f32[8,128,128]{2,1,0:T(8,128)S(1)} %dynamic-slice_bitcast_fusion), channel_id=1, source_target_pairs={{0,1},{1,0},{2,3},{3,2},{4,5},{5,4},{6,7},{7,6},{8,9},{9,8},{10,11... | collective-permute-start | bytes 1572872 | tf_op jit(solution)/shard_map/ppermute | solution.py:122
  15.6 1.5 collective-permute-done
  17.2 0.1 bitcast_add_fusion
  17.2 13.8 %all_to_all.40 = f32[8,128,128]{2,1,0:T(8,128)S(1)} all-to-all(f32[8,128,128]{2,1,0:T(8,128)S(1)} %bitcast_add_fusion), channel_id=1, replica_groups=mesh['x_lo'=2,'z'=16,'y'=4,'x_hi'=2,'core'=2] {'y','x_hi'}, dimensions={0} | all-to-all | bytes 1048576 | tf_op jit(solution)/shard_map/all_to_all | solution.py:99
  31.1 12.5 %all_to_all.41 = f32[8,128,128]{2,1,0:T(8,128)S(1)} all-to-all(f32[8,128,128]{2,1,0:T(8,128)S(1)} %broadcast_in_dim.14), channel_id=1, replica_groups=mesh['x_lo'=2,'z'=16,'y'=4,'x_hi'=2,'core'=2] {'y','x_hi'}, dimensions={0} | all-to-all | bytes 1048576 | tf_op jit(solution)/shard_map/all_to_all | solution.py:104
  43.5 4.4 %collective-permute-start.1 = (f32[8,128,128]{2,1,0:T(8,128)S(1)}, f32[8,128,128]{2,1,0:T(8,128)S(1)}, u32[]{:S(2)}, u32[]{:S(2)}) collective-permute-start(f32[8,128,128]{2,1,0:T(8,128)S(1)} %all_to_all.41), channel_id=1, source_target_pairs={{0,1},{1,0},{2,3},{3,2},{4,5},{5,4},{6,7},{7,6},{8,9},{9,8},{10,11... | collective-permute-start | bytes 1572872 | tf_op jit(solution)/shard_map/ppermute | solution.py:125
  47.9 0.0 copy-start.1
  47.9 1.5 collective-permute-done.1
  49.4 0.1 select_bitcast_fusion.1
  49.5 1.8 convolution_bitcast_fusion.3
  51.3 0.1 pad_maximum_fusion
  51.4 0.0 copy-done.1
  51.4 2.8 %convolution_bitcast_fusion.1 = f32[512,128]{0,1:T(8,128)S(1)} fusion(f32[2048,128]{1,0:T(8,128)S(1)} %bitcast.65, f32[2048,512]{1,0:T(8,128)S(1)} %copy-done.1), kind=kOutput, calls=%fused_computation.1 | convolution fusion | flops 1610612736 | bytes 5505024 | tf_op jit(solution)/shard_map/dot_general | solution.py:17
  54.2 0.2 reshape.42
  54.4 0.2 constant_dynamic-slice_fusion.3
  54.6 0.1 copy.14
  54.8 1.9 collective-permute-start.2
  56.7 0.1 copy.13
  56.8 6.0 %collective-permute-done.2 = f32[384,128]{1,0:T(8,128)S(1)} collective-permute-done((f32[384,128]{1,0:T(8,128)S(1)}, f32[384,128]{1,0:T(8,128)S(1)}, u32[]{:S(2)}, u32[]{:S(2)}) %collective-permute-start.2) | collective-permute-done | bytes 196640 | tf_op jit(solution)/shard_map/ppermute | solution.py:131
  62.8 25.6 %all_to_all.42 = f32[16,24,128]{2,1,0:T(8,128)S(1)} all-to-all(f32[16,24,128]{2,1,0:T(8,128)S(1)} %pad_maximum_fusion.4), channel_id=1, replica_groups=mesh['x_lo'=2,'z'=16,'y'=4,'x_hi'=2,'core'=2] {'z'}, dimensions={0} | all-to-all | bytes 393216 | tf_op jit(solution)/shard_map/all_to_all | solution.py:99
  88.4 0.7 broadcast_in_dim.15
  89.1 8.6 %all-to-all-start.3 = ((f32[16,24,128]{2,1,0:T(8,128)}), f32[16,24,128]{2,1,0:T(8,128)S(1)}, u32[]{:S(2)}, u32[]{:S(2)}) async-start(f32[16,24,128]{2,1,0:T(8,128)} %broadcast_in_dim.15), calls=%async_computation.3 | async-start | bytes 393216 | tf_op jit(solution)/shard_map/all_to_all | solution.py:104
  97.8 12.4 %all-to-all-done.3 = f32[16,24,128]{2,1,0:T(8,128)S(1)} async-done(((f32[16,24,128]{2,1,0:T(8,128)}), f32[16,24,128]{2,1,0:T(8,128)S(1)}, u32[]{:S(2)}, u32[]{:S(2)}) %all-to-all-start.3) | async-done | bytes 196640 | tf_op jit(solution)/shard_map/all_to_all | solution.py:104
  110.1 2.4 %collective-permute-start.3 = (f32[256,128]{1,0:T(8,128)S(1)}, f32[256,128]{1,0:T(8,128)S(1)}, u32[]{:S(2)}, u32[]{:S(2)}) collective-permute-start(f32[256,128]{1,0:T(8,128)S(1)} %bitcast.68), channel_id=1, source_target_pairs={{0,256},{256,0},{1,257},{257,1},{2,258},{258,2},{3,259},{259,3},{4... | collective-permute-start | bytes 393224 | tf_op jit(solution)/shard_map/ppermute | solution.py:139
  112.5 0.6 slice_bitcast_fusion.gram_ref
  113.2 6.3 %factor.3 = (f32[128,128]{1,0:T(8,128)}, f32[128,128]{1,0:T(8,128)}) custom-call(f32[128,128]{1,0:T(8,128)} %slice_bitcast_fusion.gram_ref), custom_call_target="tpu_custom_call" | custom-call | flops 20000000 | bytes 200000 | tf_op jit(solution)/shard_map/factor/pallas_call | solution.py:90
  119.5 0.0 collective-permute-done.3
  119.5 1.2 fusion
  120.8 0.6 convolution_bitcast_fusion.4
  121.4 6.8 %convolution_bitcast_fusion = f32[2048,128]{0,1:T(8,128)S(1)} fusion(f32[512,128]{1,0:T(8,128)S(1)} %fusion, f32[2048,512]{1,0:T(8,128)} %param.2), kind=kOutput, calls=%fused_computation | convolution fusion | flops 1610612736 | bytes 5505024 | tf_op jit(solution)/shard_map/dot_general | solution.py:13
  128.1 0.9 reshape.47
  129.0 0.9 constant_dynamic-slice_fusion.1
  130.0 0.4 copy.17
  130.4 7.3 %collective-permute-start.4 = (f32[9,128,128]{2,1,0:T(8,128)S(1)}, f32[9,128,128]{2,1,0:T(8,128)S(1)}, u32[]{:S(2)}, u32[]{:S(2)}) collective-permute-start(f32[9,128,128]{2,1,0:T(8,128)S(1)} %pad_maximum_fusion.2), channel_id=1, source_target_pairs={{0,1},{1,0},{2,3},{3,2},{4,5},{5,4},{6,7},{7,6},{8,9},{9,8},{10,11... | collective-permute-start | bytes 1769480 | tf_op jit(solution)/shard_map/ppermute | solution.py:149
  137.7 0.4 copy.16
  138.1 1.2 collective-permute-done.4
  139.3 0.0 copy-start.2
  139.3 0.1 slice_add_fusion
  139.4 0.1 pad_maximum_fusion.1
  139.5 19.2 %all_to_all.43 = f32[8,256,128]{2,1,0:T(8,128)S(1)} all-to-all(f32[8,256,128]{2,1,0:T(8,128)S(1)} %pad_maximum_fusion.1), channel_id=1, replica_groups=mesh['x_lo'=2,'z'=16,'y'=4,'x_hi'=2,'core'=2] {'y','x_hi'}, dimensions={0} | all-to-all | bytes 2097152 | tf_op jit(solution)/shard_map/all_to_all | solution.py:99
  158.7 0.1 reduce_sum.47
  158.8 0.6 slice.39.gram_ref
  159.4 6.3 %factor.4 = (f32[128,128]{1,0:T(8,128)}, f32[128,128]{1,0:T(8,128)}) custom-call(f32[128,128]{1,0:T(8,128)} %slice.39.gram_ref), custom_call_target="tpu_custom_call" | custom-call | flops 20000000 | bytes 200000 | tf_op jit(solution)/shard_map/factor/pallas_call | solution.py:90
  165.7 1.1 fusion.4
  166.8 0.3 convolution_bitcast_fusion.2
  167.1 11.7 %all_to_all.44 = f32[16,8,128]{2,1,0:T(8,128)S(1)} all-to-all(f32[16,8,128]{2,1,0:T(8,128)S(1)} %convolution_bitcast_fusion.2), channel_id=1, replica_groups=mesh['x_lo'=2,'z'=16,'y'=4,'x_hi'=2,'core'=2] {'y','x_hi','core'}, dimensions={0} | all-to-all | bytes 131072 | tf_op jit(solution)/shard_map/all_to_all | solution.py:99
  178.9 20.1 %all_to_all.45 = f32[32,8,128]{2,1,0:T(8,128)S(1)} all-to-all(f32[32,8,128]{2,1,0:T(8,128)S(1)} %broadcast_in_dim.19), channel_id=1, replica_groups=mesh['x_lo'=2,'z'=16,'y'=4,'x_hi'=2,'core'=2] {'x_lo','z'}, dimensions={0} | all-to-all | bytes 262144 | tf_op jit(solution)/shard_map/all_to_all | solution.py:104
  199.0 0.6 broadcast_in_dim.40
  199.7 6.0 %all-to-all-start.7 = ((f32[16,8,128]{2,1,0:T(8,128)}), f32[16,8,128]{2,1,0:T(8,128)S(1)}, u32[]{:S(2)}, u32[]{:S(2)}) async-start(f32[16,8,128]{2,1,0:T(8,128)} %broadcast_in_dim.40), calls=%async_computation.7 | async-start | bytes 131072 | tf_op jit(solution)/shard_map/all_to_all | solution.py:104
  205.7 0.0 copy-done.2
  205.7 0.9 fusion.10
  206.6 6.5 %all-to-all-done.7 = f32[16,8,128]{2,1,0:T(8,128)S(1)} async-done(((f32[16,8,128]{2,1,0:T(8,128)}), f32[16,8,128]{2,1,0:T(8,128)S(1)}, u32[]{:S(2)}, u32[]{:S(2)}) %all-to-all-start.7) | async-done | bytes 65568 | tf_op jit(solution)/shard_map/all_to_all | solution.py:104
  213.1 0.0 copy-start.3
  213.1 0.6 copy-done.3
  213.7 6.3 %factor.5 = (f32[128,128]{1,0:T(8,128)}, f32[128,128]{1,0:T(8,128)}) custom-call(f32[128,128]{1,0:T(8,128)} %bitcast.70), custom_call_target="tpu_custom_call" | custom-call | flops 20000000 | bytes 200000 | tf_op jit(solution)/shard_map/factor/pallas_call | solution.py:90
  220.1 1.7 fusion.11
  221.8 0.8 multiply_bitcast_fusion
  222.6 0.7 copy.18
  (16 shorter events, 0.4 us)
Async XLA Ops:
  0.6 1.0 copy-start
  6.9 10.3 %collective-permute-start = (f32[8,128,128]{2,1,0:T(8,128)S(1)}, f32[8,128,128]{2,1,0:T(8,128)S(1)}, u32[]{:S(2)}, u32[]{:S(2)}) collective-permute-start(f32[8,128,128]{2,1,0:T(8,128)S(1)} %dynamic-slice_bitcast_fusion), channel_id=1, source_target_pairs={{0,1},{1,0},{2,3},{3,2},{4,5},{5,4},{6,7},{7,6},{8,9},{9,8},{10,11... | collective-permute-start | bytes 1572872 | tf_op jit(solution)/shard_map/ppermute | solution.py:122
  43.5 5.9 %collective-permute-start.1 = (f32[8,128,128]{2,1,0:T(8,128)S(1)}, f32[8,128,128]{2,1,0:T(8,128)S(1)}, u32[]{:S(2)}, u32[]{:S(2)}) collective-permute-start(f32[8,128,128]{2,1,0:T(8,128)S(1)} %all_to_all.41), channel_id=1, source_target_pairs={{0,1},{1,0},{2,3},{3,2},{4,5},{5,4},{6,7},{7,6},{8,9},{9,8},{10,11... | collective-permute-start | bytes 1572872 | tf_op jit(solution)/shard_map/ppermute | solution.py:125
  47.9 3.5 %copy-start.1 = (f32[2048,512]{1,0:T(8,128)S(1)}, f32[2048,512]{1,0:T(8,128)}, u32[]{:S(2)}) copy-start(f32[2048,512]{1,0:T(8,128)} %param.2) | copy-start | bytes 12582916
  54.8 8.0 %collective-permute-start.2 = (f32[384,128]{1,0:T(8,128)S(1)}, f32[384,128]{1,0:T(8,128)S(1)}, u32[]{:S(2)}, u32[]{:S(2)}) collective-permute-start(f32[384,128]{1,0:T(8,128)S(1)} %pad_maximum_fusion.3), channel_id=1, source_target_pairs={{0,256},{256,0},{1,257},{257,1},{2,258},{258,2},{3,259},{259,3},{4... | collective-permute-start | bytes 589832 | tf_op jit(solution)/shard_map/ppermute | solution.py:131
  89.1 21.0 %all-to-all-start.3 = ((f32[16,24,128]{2,1,0:T(8,128)}), f32[16,24,128]{2,1,0:T(8,128)S(1)}, u32[]{:S(2)}, u32[]{:S(2)}) async-start(f32[16,24,128]{2,1,0:T(8,128)} %broadcast_in_dim.15), calls=%async_computation.3 | async-start | bytes 393216 | tf_op jit(solution)/shard_map/all_to_all | solution.py:104
  110.1 9.4 %collective-permute-start.3 = (f32[256,128]{1,0:T(8,128)S(1)}, f32[256,128]{1,0:T(8,128)S(1)}, u32[]{:S(2)}, u32[]{:S(2)}) collective-permute-start(f32[256,128]{1,0:T(8,128)S(1)} %bitcast.68), channel_id=1, source_target_pairs={{0,256},{256,0},{1,257},{257,1},{2,258},{258,2},{3,259},{259,3},{4... | collective-permute-start | bytes 393224 | tf_op jit(solution)/shard_map/ppermute | solution.py:139
  130.4 8.9 %collective-permute-start.4 = (f32[9,128,128]{2,1,0:T(8,128)S(1)}, f32[9,128,128]{2,1,0:T(8,128)S(1)}, u32[]{:S(2)}, u32[]{:S(2)}) collective-permute-start(f32[9,128,128]{2,1,0:T(8,128)S(1)} %pad_maximum_fusion.2), channel_id=1, source_target_pairs={{0,1},{1,0},{2,3},{3,2},{4,5},{5,4},{6,7},{7,6},{8,9},{9,8},{10,11... | collective-permute-start | bytes 1769480 | tf_op jit(solution)/shard_map/ppermute | solution.py:149
  139.3 66.4 %copy-start.2 = (f32[128,128]{1,0:T(8,128)S(1)}, f32[128,128]{1,0:T(8,128)}, u32[]{:S(2)}) copy-start(f32[128,128]{1,0:T(8,128)} %get-tuple-element.7) | copy-start | bytes 196612
  199.7 13.4 %all-to-all-start.7 = ((f32[16,8,128]{2,1,0:T(8,128)}), f32[16,8,128]{2,1,0:T(8,128)S(1)}, u32[]{:S(2)}, u32[]{:S(2)}) async-start(f32[16,8,128]{2,1,0:T(8,128)} %broadcast_in_dim.40), calls=%async_computation.7 | async-start | bytes 131072 | tf_op jit(solution)/shard_map/all_to_all | solution.py:104
  213.1 0.6 copy-start.3

commit v3 on v2

v3 whole, which is shorter than its diff:
```python
import jax
import jax.numpy as jnp
from jax import lax
from jax.experimental import pallas as pl
from jax.experimental.pallas import tpu as pltpu
from jax.sharding import Mesh, PartitionSpec as P

PANEL = 8
SWAP = [(0, 1), (1, 0)]
ROWS = 256
PLANE = ("y", "x_hi")
NEAR = ("x_lo", "z_lo")
CROSS = ("x_lo", "y", "x_hi", "core")
BIG = pltpu.CompilerParams(vmem_limit_bytes=40 * 1024 * 1024)


def terms(value):
    first = value.astype(jnp.bfloat16)
    rest = value - first.astype(jnp.float32)
    second = rest.astype(jnp.bfloat16)
    third = (rest - second.astype(jnp.float32)).astype(jnp.bfloat16)
    return first, second, third


def dot(left_side, right_side):
    return lax.dot_general(
        left_side, right_side, (((1,), (0,)), ((), ())), preferred_element_type=jnp.float32
    )


def product_wide(left_side, wide, third):
    n = third.shape[1]
    l1, l2, l3 = terms(left_side)
    p = dot(l1, wide)
    q = dot(l2, wide)
    low = dot(l1, third) + dot(l3, wide[:, :n])
    return p[:, :n] + ((p[:, n:] + q[:, :n]) + (q[:, n:] + low))


def product(left_side, right_side):
    r1, r2, r3 = terms(right_side)
    return product_wide(left_side, jnp.concatenate([r1, r2], axis=1), r3)


def product_tall(left_side, right_side):
    n = left_side.shape[0]
    l1, l2, l3 = terms(left_side)
    r1, r2, r3 = terms(right_side)
    p = dot(jnp.concatenate([l1, l2, l3], axis=0), r1)
    q = dot(jnp.concatenate([l1, l2], axis=0), r2)
    low = (p[2 * n :] + q[n:]) + dot(l1, r3)
    return p[:n] + ((p[n : 2 * n] + q[:n]) + low)


def eliminate(gram):
    n = gram.shape[0]
    count = n // 8
    tile = (8, n)
    row = lax.broadcasted_iota(jnp.int32, tile, 0)
    lane = lax.broadcasted_iota(jnp.int32, tile, 1)
    left = [gram[8 * u : 8 * u + 8, :] for u in range(count)]
    right = [jnp.where(lane == row + 8 * u, 1.0, 0.0).astype(jnp.float32) for u in range(count)]
    for v in range(count):
        start = 8 * v
        rows = [jnp.broadcast_to(left[v][i : i + 1, :], tile) for i in range(PANEL)]
        more = [jnp.broadcast_to(right[v][i : i + 1, :], tile) for i in range(PANEL)]
        columns = [
            [jnp.broadcast_to(left[u][:, start + i : start + i + 1], tile) for u in range(v, count)]
            for i in range(PANEL)
        ]
        corner = [
            [jnp.broadcast_to(rows[i][:, start + m : start + m + 1], tile) for m in range(PANEL)]
            for i in range(PANEL)
        ]
        factors = []
        for i in range(PANEL):
            inverse = 1.0 / corner[i][i]
            factor = [c * inverse for c in columns[i]]
            for m in range(i + 1, PANEL):
                weight = corner[i][m] * inverse
                for q in range(m, PANEL):
                    corner[m][q] = corner[m][q] - weight * corner[i][q]
                rows[m] = rows[m] - weight * rows[i]
                more[m] = more[m] - weight * more[i]
                columns[m] = [c - f * corner[i][m] for c, f in zip(columns[m], factor)]
            factor[0] = jnp.where(row > i, factor[0], 0.0)
            factors.append(factor)
        for u in range(v, count):
            a, b = left[u], right[u]
            for i in range(PANEL):
                a = a - factors[i][u - v] * rows[i]
                b = b - factors[i][u - v] * more[i]
            left[u], right[u] = a, b
    upper, inverse = [], []
    for u in range(count):
        pivots = jnp.sum(jnp.where(lane == row + 8 * u, left[u], 0.0), axis=1, keepdims=True)
        scale = lax.rsqrt(pivots)
        upper.append(jnp.where(lane >= row + 8 * u, left[u] * scale, 0.0))
        inverse.append(right[u] * scale)
    return jnp.concatenate(upper, 0), jnp.concatenate(inverse, 0)


def part_store(core_ref, value, keep_ref, send_ref):
    half = value.shape[0] // 2
    low, high = value[:half], value[half:]
    is_first = core_ref[0] == 0
    keep_ref[...] = jnp.where(is_first, low, high)[None]
    send_ref[...] = jnp.where(is_first, high, low)[None]


def image_kernel(core_ref, a_ref, s_ref, keep_ref, send_ref, wide_ref, third_ref):
    @pl.when(pl.program_id(0) == 0)
    def _():
        s1, s2, s3 = terms(s_ref[...])
        wide_ref[...] = jnp.concatenate([s1, s2], axis=1)
        third_ref[...] = s3

    part_store(core_ref, product_wide(a_ref[...], wide_ref[...], third_ref[...]), keep_ref, send_ref)


def back_kernel(core_ref, a_ref, mine_ref, other_ref, out_ref, back_ref, gram_ref):
    step = pl.program_id(0)

    @pl.when(step == 0)
    def _():
        back_ref[...] = jnp.zeros_like(back_ref)
        gram_ref[...] = jnp.zeros_like(gram_ref)

    is_first = core_ref[0] == 0
    mine, other = mine_ref[0], other_ref[0]
    y = jnp.concatenate([jnp.where(is_first, mine, other), jnp.where(is_first, other, mine)], axis=0)
    turned = y.T
    back_ref[...] += product_tall(turned, a_ref[...])
    gram_ref[...] += product_tall(turned, y)

    @pl.when(step == pl.num_programs(0) - 1)
    def _():
        back, gram = back_ref[...].T, gram_ref[...]
        count = out_ref.shape[0]
        cut, small = back.shape[0] // count, gram.shape[0] // count
        for k in range(count):
            out_ref[k, :cut, :] = back[k * cut : (k + 1) * cut]
            out_ref[k, cut:, :] = gram[k * small : (k + 1) * small]


def range_kernel(
    core_ref, a_ref, both_ref, image_ref, keep_ref, send_ref, gram_ref, first_ref, wide_ref, third_ref
):
    step = pl.program_id(0)

    @pl.when(step == 0)
    def _():
        n = first_ref.shape[1]
        count = both_ref.shape[0]
        small = n // count
        cut = both_ref.shape[1] - small
        gram = jnp.concatenate([both_ref[k, cut:, :] for k in range(count)], axis=0)
        back = jnp.concatenate([both_ref[k, :cut, :] for k in range(count)], axis=0)
        unused, inverse = eliminate(gram)
        i1, i2, i3 = terms(inverse.T)
        wide = jnp.concatenate([i1, i2], axis=1)
        first_ref[...] = product_wide(image_ref[...], wide, i3)
        back = product_wide(back, wide, i3)
        gram_back = product(back.T, back)
        gram_ref[...] = gram_back
        send_ref[send_ref.shape[0] - 1] = gram_back
        b1, b2, b3 = terms(back)
        wide_ref[...] = jnp.concatenate([b1, b2], axis=1)
        third_ref[...] = b3

    value = product_wide(a_ref[...], wide_ref[...], third_ref[...])
    part_store(core_ref, value, keep_ref, send_ref.at[pl.ds(step, 1)])


def last_gram_kernel(parts_ref, range_ref, gram_ref):
    n = range_ref.shape[0]
    total = parts_ref[0]
    for k in range(1, parts_ref.shape[0]):
        total = total + parts_ref[k]
    unused, inverse = eliminate(total[n:])
    block = product(total[:n], inverse.T)
    range_ref[...] = block
    gram_ref[...] = product(block.T, block)


def basis_kernel(tokens, gram_ref, range_ref, basis_ref, triangle_ref):
    upper, inverse = eliminate(gram_ref[...])
    basis_ref[...] = product(range_ref[...], inverse.T)
    triangle_ref[...] = upper.T / jnp.sqrt(jnp.float32(tokens))


def shape(*sizes):
    return jax.ShapeDtypeStruct(sizes, jnp.float32)


def whole(*sizes):
    return pl.BlockSpec(sizes, lambda i, core: (0,) * len(sizes))


def image_parts(core, a, s):
    rows, depth = a.shape
    n, steps = s.shape[1], rows // ROWS
    block = pl.BlockSpec((1, ROWS // 2, n), lambda i, core: (i, 0, 0))
    return pl.pallas_call(
        image_kernel,
        out_shape=[shape(steps, ROWS // 2, n)] * 2,
        grid_spec=pltpu.PrefetchScalarGridSpec(
            num_scalar_prefetch=1,
            grid=(steps,),
            in_specs=[pl.BlockSpec((ROWS, depth), lambda i, core: (i, 0)), whole(depth, n)],
            out_specs=[block, block],
            scratch_shapes=[pltpu.VMEM((depth, 2 * n), jnp.bfloat16), pltpu.VMEM((depth, n), jnp.bfloat16)],
        ),
        compiler_params=BIG,
        name="image_parts",
    )(core, a, s)


def back_parts(core, a, mine, other, count):
    rows, depth = a.shape
    n, steps = mine.shape[2], rows // ROWS
    chunk = (depth + n) // count
    block = pl.BlockSpec((1, ROWS // 2, n), lambda i, core: (i, 0, 0))
    return pl.pallas_call(
        back_kernel,
        out_shape=shape(count, chunk, n),
        grid_spec=pltpu.PrefetchScalarGridSpec(
            num_scalar_prefetch=1,
            grid=(steps,),
            in_specs=[pl.BlockSpec((ROWS, depth), lambda i, core: (i, 0)), block, block],
            out_specs=whole(count, chunk, n),
            scratch_shapes=[pltpu.VMEM((n, depth), jnp.float32), pltpu.VMEM((n, n), jnp.float32)],
        ),
        compiler_params=BIG,
        name="back_parts",
    )(core, a, mine, other)


def range_parts(core, a, both, image_block):
    rows, depth = a.shape
    n, steps = both.shape[2], rows // ROWS
    block = pl.BlockSpec((1, ROWS // 2, n), lambda i, core: (i, 0, 0))
    return pl.pallas_call(
        range_kernel,
        out_shape=[shape(steps, ROWS // 2, n), shape(steps + 1, ROWS // 2, n), shape(n, n), shape(n, n)],
        grid_spec=pltpu.PrefetchScalarGridSpec(
            num_scalar_prefetch=1,
            grid=(steps,),
            in_specs=[pl.BlockSpec((ROWS, depth), lambda i, core: (i, 0)), whole(*both.shape), whole(n, n)],
            out_specs=[block, whole(steps + 1, ROWS // 2, n), whole(n, n), whole(n, n)],
            scratch_shapes=[pltpu.VMEM((depth, 2 * n), jnp.bfloat16), pltpu.VMEM((depth, n), jnp.bfloat16)],
        ),
        compiler_params=BIG,
        name="range_parts",
    )(core, a, both, image_block)


def last_gram(parts):
    n = parts.shape[2]
    return pl.pallas_call(
        last_gram_kernel, out_shape=[shape(n, n)] * 2, compiler_params=BIG, name="last_gram"
    )(parts)


def basis(gram, block, tokens):
    n = gram.shape[0]
    return pl.pallas_call(
        lambda *refs: basis_kernel(tokens, *refs),
        out_shape=[shape(n, n)] * 2,
        compiler_params=BIG,
        name="basis",
    )(gram, block)


def scatter_sum(parts, axis):
    return jnp.sum(lax.all_to_all(parts, axis, 0, 0), axis=0)


def gather(block, axis):
    count = lax.axis_size(axis)
    return lax.all_to_all(jnp.broadcast_to(block[None], (count,) + block.shape), axis, 0, 0)


def per_device(activations, sketch):
    width = sketch.shape[1]
    core = lax.axis_index("core").astype(jnp.int32).reshape(1)
    keep, send = image_parts(core, activations, sketch)
    image_block = scatter_sum(keep + lax.ppermute(send, "core", SWAP), PLANE)
    mine = gather(image_block, PLANE)
    other = lax.ppermute(mine, "core", SWAP)
    parts = back_parts(core, activations, mine, other, lax.axis_size(NEAR))
    sums = scatter_sum(parts, NEAR)
    sums = jnp.sum(gather(sums, "z_hi"), axis=0)
    both = gather(sums, NEAR)
    keep, send, gram_part, first_block = range_parts(core, activations, both, image_block)
    received = lax.ppermute(send, "core", SWAP)
    count = keep.shape[0]
    gram_part = jnp.broadcast_to(gram_part[None] + received[count:], (count, width, width))
    parts = jnp.concatenate([keep + received[:count], gram_part], axis=1)
    range_block, gram_part = last_gram(lax.all_to_all(parts, PLANE, 0, 0))
    gram_slice = scatter_sum(gram_part.reshape(lax.axis_size(CROSS), -1, width), CROSS)
    gram_slice = jnp.sum(gather(gram_slice, ("z_hi", "z_lo")), axis=0)
    gram_last = gather(gram_slice, CROSS).reshape(width, width)
    tokens = activations.shape[0] * lax.axis_size(("x_lo", "z_hi", "z_lo"))
    range_basis, triangle = basis(gram_last, range_block, tokens)
    return (first_block, range_basis, triangle)


def solution(mesh):
    fine = Mesh(mesh.devices.reshape(2, 4, 4, 4, 2, 2), ("x_lo", "z_hi", "z_lo", "y", "x_hi", "core"))
    tok, feat = ("x_lo", "z_hi", "z_lo"), ("y", "x_hi", "core")
    return jax.shard_map(
        per_device,
        mesh=fine,
        in_specs=(P(tok, feat), P(feat, None)),
        out_specs=(P(tok + feat, None), P(tok + feat, None), P()),
        check_vma=False,
    )
```

time: 224 us -> 198 us (0.88)
  blocking collectives: 103 us -> 135 us
  waiting for transfers between devices: 29 us -> 4.64 us
  matrix products: 22.4 us -> 0 us
  starting transfers between devices: 39.4 us -> 20.4 us
  Pallas kernels: 19 us -> 29.1 us
    all_to_all x2 -> x5, blocking collectives: 32.6 us -> 77.2 us  [gather(): lax.all_to_all(jnp.broadcast_to(block[None], (count,) + block.shape), axi...]
    all_to_all x4 -> x3, blocking collectives: 70.2 us -> 38.9 us  [scatter_sum(): return jnp.sum(lax.all_to_all(parts, axis, 0, 0), axis=0)]
    dot_general x10 -> x0, matrix products: 22.4 us -> none  [the longest x2 12 us: product(): jnp.dot(left_side, right_side, precision=TOP, preferred_element_type=jnp....]
    all_to_all x2 -> x0, waiting for transfers between devices: 18.8 us -> none  [gather(): lax.all_to_all(jnp.broadcast_to(block[None], (count,) + block.shape), axi...]
    all_to_all x0 -> x1, blocking collectives: none -> 18.8 us  [per_device(): range_block, gram_part = last_gram(lax.all_to_all(parts, PLANE, 0, 0))]
    all_to_all x2 -> x0, starting transfers between devices: 14.7 us -> none  [gather(): lax.all_to_all(jnp.broadcast_to(block[None], (count,) + block.shape), axi...]
    pallas_call x3 -> x5, Pallas kernels: 19 us -> 29.1 us  [the longest x1 9.9 us: range_parts(): pl.pallas_call(range_kernel, out_shape=[shape(steps, ROWS // 2, n), shape...]
    ppermute x4 -> x2, waiting for transfers between devices: 8.7 us -> 3.12 us  [the longest x1 1.61 us: per_device(): received = lax.ppermute(send, 'core', SWAP)]
  transfers between devices with their start and end apart: 7 -> 3, of which waited for: 6 -> 3; matrix products, arithmetic and copies ran while one was open for 1% -> 0% of each run, Pallas kernels for 3% -> 0%
where the time goes in v3:
time: 198 us
  blocking collectives  135 us (68%)
  Pallas kernels  29.1 us (15%)
  starting transfers between devices  20.4 us (10%)
  local copies, waits for them, and re-layouts  7.64 us (4%)
  waiting for transfers between devices  4.64 us (2%)
    all_to_all x5, blocking collectives, gather(): lax.all_to_all(jnp.broadcast_to(block[None], (count,) + block.shape), axi...  77.2 us
    all_to_all x3, blocking collectives, scatter_sum(): return jnp.sum(lax.all_to_all(parts, axis, 0, 0), axis=0)  38.9 us
    all_to_all x1, blocking collectives, per_device(): range_block, gram_part = last_gram(lax.all_to_all(parts, PLANE, 0, 0))  18.8 us
    pallas_call x1, Pallas kernels, range_parts(): pl.pallas_call(range_kernel, out_shape=[shape(steps, ROWS // 2, n), shape...  9.9 us
    ppermute x1, starting transfers between devices, per_device(): image_block = scatter_sum(keep + lax.ppermute(send, 'core', SWAP), PLANE)  8.72 us
    unnamed x8, local copies, waits for them, and re-layouts  7.51 us
    ppermute x1, starting transfers between devices, per_device(): received = lax.ppermute(send, 'core', SWAP)  7.3 us
    pallas_call x1, Pallas kernels, basis(): pl.pallas_call(lambda *refs: basis_kernel(tokens, *refs), out_shape=[shap...  5.58 us
  transfers between devices with their start and end apart: 3, of which 3 were waited for; matrix products, arithmetic and copies ran while one was open for 0% of the time, Pallas kernels for 0%

profile of v3, /device:TPU:1, one launch (start us, length us, event | category | flops | bytes accessed | tf_op | source)
XLA Modules:
  0.0 197.8 jit_solution(5933623201531145930)
XLA Ops:
  0.6 0.0 copy-start
  0.6 2.2 %copy-done = f32[2048,512]{1,0:T(8,128)S(1)} copy-done((f32[2048,512]{1,0:T(8,128)S(1)}, f32[2048,512]{1,0:T(8,128)}, u32[]{:S(2)}) %copy-start) | copy-done | bytes 4194328
  2.8 0.0 copy-start.3
  2.8 0.9 copy-done.3
  3.8 3.8 %image_parts.1 = (f32[8,128,128]{2,1,0:T(8,128)S(1)}, f32[8,128,128]{2,1,0:T(8,128)S(1)}) custom-call(s32[1]{0:T(128)} %bitcast.core_ref, f32[2048,512]{1,0:T(8,128)S(1)} %copy-done, f32[512,128]{1,0:T(8,128)S(1)} %copy-done.3), custom_call_target="tpu_custom_call" | custom-call | tf_op jit(solution)/shard_map/image_parts/pallas_call | solution.py:204
  7.6 8.7 %collective-permute-start = (f32[8,128,128]{2,1,0:T(8,128)S(1)}, f32[8,128,128]{2,1,0:T(8,128)S(1)}, u32[]{:S(2)}, u32[]{:S(2)}) collective-permute-start(f32[8,128,128]{2,1,0:T(8,128)S(1)} %get-tuple-element.14), channel_id=1, source_target_pairs={{0,1},{1,0},{2,3},{3,2},{4,5},{5,4},{6,7},{7,6},{8,9},{9,8},{10,11... | collective-permute-start | bytes 1572872 | tf_op jit(solution)/shard_map/ppermute | solution.py:288
  16.4 1.5 collective-permute-done
  17.9 0.1 add.9
  17.9 13.8 %all_to_all.45 = f32[8,128,128]{2,1,0:T(8,128)S(1)} all-to-all(f32[8,128,128]{2,1,0:T(8,128)S(1)} %add.9), channel_id=1, replica_groups=mesh['x_lo'=2,'z_hi'=4,'z_lo'=4,'y'=4,'x_hi'=2,'core'=2] {'y','x_hi'}, dimensions={0} | all-to-all | bytes 1048576 | tf_op jit(solution)/shard_map/all_to_all | solution.py:276
  31.8 12.5 %all_to_all.46.mine_ref = f32[8,128,128]{2,1,0:T(8,128)S(1)} all-to-all(f32[8,128,128]{2,1,0:T(8,128)S(1)} %broadcast_in_dim.16), channel_id=1, replica_groups=mesh['x_lo'=2,'z_hi'=4,'z_lo'=4,'y'=4,'x_hi'=2,'core'=2] {'y','x_hi'}, dimensions={0} | all-to-all | bytes 1048576 | tf_op jit(solution)/shard_map/all_to_all | solution.py:281
  44.2 4.4 %collective-permute-start.1 = (f32[8,128,128]{2,1,0:T(8,128)S(1)}, f32[8,128,128]{2,1,0:T(8,128)S(1)}, u32[]{:S(2)}, u32[]{:S(2)}) collective-permute-start(f32[8,128,128]{2,1,0:T(8,128)S(1)} %all_to_all.46.mine_ref), channel_id=1, source_target_pairs={{0,1},{1,0},{2,3},{3,2},{4,5},{5,4},{6,7},{7,6},{8,9},{9,8},{10,11... | collective-permute-start | bytes 1572872 | tf_op jit(solution)/shard_map/ppermute | solution.py:290
  48.6 1.5 collective-permute-done.1.other_ref
  50.1 0.0 copy-start.1
  50.1 2.2 %copy-done.1 = f32[2048,512]{1,0:T(8,128)S(1)} copy-done((f32[2048,512]{1,0:T(8,128)S(1)}, f32[2048,512]{1,0:T(8,128)}, u32[]{:S(2)}) %copy-start.1) | copy-done | bytes 4194328
  52.3 4.4 %back_parts.1 = f32[8,80,128]{2,1,0:T(8,128)S(1)} custom-call(s32[1]{0:T(128)} %bitcast.core_ref, f32[2048,512]{1,0:T(8,128)S(1)} %copy-done.1, f32[8,128,128]{2,1,0:T(8,128)S(1)} %all_to_all.46.mine_ref, f32[8,128,128]{2,1,0:T(8,128)S(1)} %collective-permute-done.1.other_ref), custom_call_target="tpu_custom_call" | custom-call | tf_op jit(solution)/shard_map/back_parts/pallas_call | solution.py:224
  56.7 13.4 %all_to_all.47 = f32[8,80,128]{2,1,0:T(8,128)S(1)} all-to-all(f32[8,80,128]{2,1,0:T(8,128)S(1)} %back_parts.1), channel_id=1, replica_groups=mesh['x_lo'=2,'z_hi'=4,'z_lo'=4,'y'=4,'x_hi'=2,'core'=2] {'x_lo','z_lo'}, dimensions={0} | all-to-all | bytes 655360 | tf_op jit(solution)/shard_map/all_to_all | solution.py:276
  70.2 26.6 %all_to_all.48 = f32[4,80,128]{2,1,0:T(8,128)S(1)} all-to-all(f32[4,80,128]{2,1,0:T(8,128)S(1)} %broadcast_in_dim.17), channel_id=1, replica_groups=mesh['x_lo'=2,'z_hi'=4,'z_lo'=4,'y'=4,'x_hi'=2,'core'=2] {'z_hi'}, dimensions={0} | all-to-all | bytes 327680 | tf_op jit(solution)/shard_map/all_to_all | solution.py:281
  96.8 10.4 %all_to_all.49.both_ref = f32[8,80,128]{2,1,0:T(8,128)S(1)} all-to-all(f32[8,80,128]{2,1,0:T(8,128)S(1)} %broadcast_in_dim.18), channel_id=1, replica_groups=mesh['x_lo'=2,'z_hi'=4,'z_lo'=4,'y'=4,'x_hi'=2,'core'=2] {'x_lo','z_lo'}, dimensions={0} | all-to-all | bytes 655360 | tf_op jit(solution)/shard_map/all_to_all | solution.py:281
  107.2 0.0 copy-start.2
  107.2 2.2 %copy-done.2 = f32[2048,512]{1,0:T(8,128)S(1)} copy-done((f32[2048,512]{1,0:T(8,128)S(1)}, f32[2048,512]{1,0:T(8,128)}, u32[]{:S(2)}) %copy-start.2) | copy-done | bytes 4194328
  109.4 9.9 %range_parts.1 = (f32[8,128,128]{2,1,0:T(8,128)S(1)}, f32[9,128,128]{2,1,0:T(8,128)S(1)}, f32[128,128]{1,0:T(8,128)S(1)}, f32[128,128]{1,0:T(8,128)}) custom-call(s32[1]{0:T(128)} %bitcast.core_ref, f32[2048,512]{1,0:T(8,128)S(1)} %copy-done.2, f32[8,80,128]{2,1,0:T(8,128)S(1)} %all_to_all.49.both_ref, f32[128,128]{1,0:T(8,128)S(1)} %reduce_sum.45.image_ref), custom_call_target="tpu_custom_call" | custom-call | tf_op jit(solution)/shard_map/range_parts/pallas_call | solution.py:243
  119.3 7.3 %collective-permute-start.2 = (f32[9,128,128]{2,1,0:T(8,128)S(1)}, f32[9,128,128]{2,1,0:T(8,128)S(1)}, u32[]{:S(2)}, u32[]{:S(2)}) collective-permute-start(f32[9,128,128]{2,1,0:T(8,128)S(1)} %get-tuple-element.17), channel_id=1, source_target_pairs={{0,1},{1,0},{2,3},{3,2},{4,5},{5,4},{6,7},{7,6},{8,9},{9,8},{10,11... | collective-permute-start | bytes 1769480 | tf_op jit(solution)/shard_map/ppermute | solution.py:296
  126.6 1.6 collective-permute-done.2
  128.2 0.1 slice_add_fusion
  128.4 0.1 pad_maximum_fusion
  128.4 18.8 %all_to_all.50.parts_ref = f32[8,256,128]{2,1,0:T(8,128)S(1)} all-to-all(f32[8,256,128]{2,1,0:T(8,128)S(1)} %pad_maximum_fusion), channel_id=1, replica_groups=mesh['x_lo'=2,'z_hi'=4,'z_lo'=4,'y'=4,'x_hi'=2,'core'=2] {'y','x_hi'}, dimensions={0} | all-to-all | bytes 2097152 | tf_op jit(solution)/shard_map/all_to_all | solution.py:300
  147.2 5.4 %last_gram.1 = (f32[128,128]{1,0:T(8,128)S(1)}, f32[128,128]{1,0:T(8,128)S(1)}) custom-call(f32[8,256,128]{2,1,0:T(8,128)S(1)} %all_to_all.50.parts_ref), custom_call_target="tpu_custom_call" | custom-call | tf_op jit(solution)/shard_map/last_gram/pallas_call | solution.py:260
  152.6 11.8 %all_to_all.51 = f32[32,4,128]{2,1,0:T(4,128)S(1)} all-to-all(f32[32,4,128]{2,1,0:T(4,128)S(1)} %bitcast.8), channel_id=1, replica_groups=mesh['x_lo'=2,'z_hi'=4,'z_lo'=4,'y'=4,'x_hi'=2,'core'=2] {'x_lo','y','x_..., dimensions={0} | all-to-all | bytes 131072 | tf_op jit(solution)/shard_map/all_to_all | solution.py:276
  164.4 15.5 %all_to_all.52 = f32[16,4,128]{2,1,0:T(4,128)S(1)} all-to-all(f32[16,4,128]{2,1,0:T(4,128)S(1)} %broadcast_in_dim.22), channel_id=1, replica_groups=mesh['x_lo'=2,'z_hi'=4,'z_lo'=4,'y'=4,'x_hi'=2,'core'=2] {'z_hi','z_lo'}, dimensions={0} | all-to-all | bytes 65536 | tf_op jit(solution)/shard_map/all_to_all | solution.py:281
  179.9 12.3 %all_to_all.53 = f32[32,4,128]{2,1,0:T(4,128)S(1)} all-to-all(f32[32,4,128]{2,1,0:T(4,128)S(1)} %broadcast_in_dim.23), channel_id=1, replica_groups=mesh['x_lo'=2,'z_hi'=4,'z_lo'=4,'y'=4,'x_hi'=2,'core'=2] {'x_lo','y','x_..., dimensions={0} | all-to-all | bytes 131072 | tf_op jit(solution)/shard_map/all_to_all | solution.py:281
  192.2 5.6 %basis.1 = (f32[128,128]{1,0:T(8,128)}, f32[128,128]{1,0:T(8,128)}) custom-call(f32[128,128]{1,0:T(8,128)S(1)} %bitcast.7, f32[128,128]{1,0:T(8,128)S(1)} %get-tuple-element.20.refs_1_), custom_call_target="tpu_custom_call" | custom-call | tf_op jit(solution)/shard_map/basis/pallas_call | solution.py:267
  (12 shorter events, 0.3 us)
Async XLA Ops:
  0.6 2.2 %copy-start = (f32[2048,512]{1,0:T(8,128)S(1)}, f32[2048,512]{1,0:T(8,128)}, u32[]{:S(2)}) copy-start(f32[2048,512]{1,0:T(8,128)} %a_ref.5) | copy-start | bytes 12582916
  2.8 0.9 copy-start.3
  7.6 10.2 %collective-permute-start = (f32[8,128,128]{2,1,0:T(8,128)S(1)}, f32[8,128,128]{2,1,0:T(8,128)S(1)}, u32[]{:S(2)}, u32[]{:S(2)}) collective-permute-start(f32[8,128,128]{2,1,0:T(8,128)S(1)} %get-tuple-element.14), channel_id=1, source_target_pairs={{0,1},{1,0},{2,3},{3,2},{4,5},{5,4},{6,7},{7,6},{8,9},{9,8},{10,11... | collective-permute-start | bytes 1572872 | tf_op jit(solution)/shard_map/ppermute | solution.py:288
  44.2 5.9 %collective-permute-start.1 = (f32[8,128,128]{2,1,0:T(8,128)S(1)}, f32[8,128,128]{2,1,0:T(8,128)S(1)}, u32[]{:S(2)}, u32[]{:S(2)}) collective-permute-start(f32[8,128,128]{2,1,0:T(8,128)S(1)} %all_to_all.46.mine_ref), channel_id=1, source_target_pairs={{0,1},{1,0},{2,3},{3,2},{4,5},{5,4},{6,7},{7,6},{8,9},{9,8},{10,11... | collective-permute-start | bytes 1572872 | tf_op jit(solution)/shard_map/ppermute | solution.py:290
  50.1 2.2 %copy-start.1 = (f32[2048,512]{1,0:T(8,128)S(1)}, f32[2048,512]{1,0:T(8,128)}, u32[]{:S(2)}) copy-start(f32[2048,512]{1,0:T(8,128)} %a_ref.5) | copy-start | bytes 12582916
  107.2 2.2 %copy-start.2 = (f32[2048,512]{1,0:T(8,128)S(1)}, f32[2048,512]{1,0:T(8,128)}, u32[]{:S(2)}) copy-start(f32[2048,512]{1,0:T(8,128)} %a_ref.5) | copy-start | bytes 12582916
  119.3 8.9 %collective-permute-start.2 = (f32[9,128,128]{2,1,0:T(8,128)S(1)}, f32[9,128,128]{2,1,0:T(8,128)S(1)}, u32[]{:S(2)}, u32[]{:S(2)}) collective-permute-start(f32[9,128,128]{2,1,0:T(8,128)S(1)} %get-tuple-element.17), channel_id=1, source_target_pairs={{0,1},{1,0},{2,3},{3,2},{4,5},{5,4},{6,7},{7,6},{8,9},{9,8},{10,11... | collective-permute-start | bytes 1769480 | tf_op jit(solution)/shard_map/ppermute | solution.py:296

commit v4 on v3

--- a/solution.py
+++ b/solution.py
@@ -11,7 +11,8 @@
 PLANE = ("y", "x_hi")
 NEAR = ("x_lo", "z_lo")
 CROSS = ("x_lo", "y", "x_hi", "core")
-BIG = pltpu.CompilerParams(vmem_limit_bytes=40 * 1024 * 1024)
+BIG = pltpu.CompilerParams(vmem_limit_bytes=61 * 1024 * 1024)
+SMALL = pltpu.CompilerParams(vmem_limit_bytes=32 * 1024 * 1024)
 
 
 def terms(value):
@@ -50,6 +51,12 @@
     q = dot(jnp.concatenate([l1, l2], axis=0), r2)
     low = (p[2 * n :] + q[n:]) + dot(l1, r3)
     return p[:n] + ((p[n : 2 * n] + q[:n]) + low)
+
+
+def tree(values):
+    while len(values) > 1:
+        values = [a + b for a, b in zip(values[::2], values[1::2])]
+    return values[0]
 
 
 def eliminate(gram):
@@ -64,33 +71,30 @@
         start = 8 * v
         rows = [jnp.broadcast_to(left[v][i : i + 1, :], tile) for i in range(PANEL)]
         more = [jnp.broadcast_to(right[v][i : i + 1, :], tile) for i in range(PANEL)]
-        columns = [
-            [jnp.broadcast_to(left[u][:, start + i : start + i + 1], tile) for u in range(v, count)]
-            for i in range(PANEL)
-        ]
         corner = [
             [jnp.broadcast_to(rows[i][:, start + m : start + m + 1], tile) for m in range(PANEL)]
             for i in range(PANEL)
         ]
-        factors = []
+        scales = []
         for i in range(PANEL):
-            inverse = 1.0 / corner[i][i]
-            factor = [c * inverse for c in columns[i]]
+            scales.append(1.0 / corner[i][i])
             for m in range(i + 1, PANEL):
-                weight = corner[i][m] * inverse
+                weight = corner[i][m] * scales[i]
                 for q in range(m, PANEL):
                     corner[m][q] = corner[m][q] - weight * corner[i][q]
                 rows[m] = rows[m] - weight * rows[i]
                 more[m] = more[m] - weight * more[i]
-                columns[m] = [c - f * corner[i][m] for c, f in zip(columns[m], factor)]
-            factor[0] = jnp.where(row > i, factor[0], 0.0)
-            factors.append(factor)
         for u in range(v, count):
-            a, b = left[u], right[u]
+            factors = []
             for i in range(PANEL):
-                a = a - factors[i][u - v] * rows[i]
-                b = b - factors[i][u - v] * more[i]
-            left[u], right[u] = a, b
+                column = jnp.broadcast_to(left[u][:, start + i : start + i + 1], tile)
+                for m in range(i):
+                    column = column - factors[m] * corner[m][i]
+                factors.append(column * scales[i])
+            if u == v:
+                factors = [jnp.where(row > i, factors[i], 0.0) for i in range(PANEL)]
+            left[u] = left[u] - tree([f * r for f, r in zip(factors, rows)])
+            right[u] = right[u] - tree([f * r for f, r in zip(factors, more)])
     upper, inverse = [], []
     for u in range(count):
         pivots = jnp.sum(jnp.where(lane == row + 8 * u, left[u], 0.0), axis=1, keepdims=True)
@@ -100,12 +104,33 @@
     return jnp.concatenate(upper, 0), jnp.concatenate(inverse, 0)
 
 
-def part_store(core_ref, value, keep_ref, send_ref):
+def iotas(gram):
+    return [lax.broadcasted_iota(jnp.int32, gram.shape, k) for k in range(2)]
+
+
+def pack(gram):
+    half = gram.shape[0] // 2
+    top, last = gram[:half], pltpu.roll(gram[half:], half, 1)
+    row, lane = iotas(top)
+    diagonal = jnp.sum(jnp.where(lane == row, last, 0.0), axis=0, keepdims=True)
+    return jnp.where(lane < row, last, top), jnp.broadcast_to(diagonal, (8, gram.shape[1]))
+
+
+def unpack(packed):
+    half = packed.shape[0] - 8
+    top, diagonal = packed[:half], packed[half : half + 1]
+    row, lane = iotas(top)
+    last = jnp.where(lane < row, top, jnp.where(lane == row, diagonal, 0.0))
+    whole = jnp.concatenate([jnp.where(lane < row, 0.0, top), pltpu.roll(last, half, 1)], axis=0)
+    row, lane = iotas(whole)
+    return jnp.where(row == lane, whole, whole + whole.T)
+
+
+def halves(core_ref, value):
     half = value.shape[0] // 2
     low, high = value[:half], value[half:]
     is_first = core_ref[0] == 0
-    keep_ref[...] = jnp.where(is_first, low, high)[None]
-    send_ref[...] = jnp.where(is_first, high, low)[None]
+    return jnp.where(is_first, low, high), jnp.where(is_first, high, low)
 
 
 def image_kernel(core_ref, a_ref, s_ref, keep_ref, send_ref, wide_ref, third_ref):
@@ -115,7 +140,7 @@
         wide_ref[...] = jnp.concatenate([s1, s2], axis=1)
         third_ref[...] = s3
 
-    part_store(core_ref, product_wide(a_ref[...], wide_ref[...], third_ref[...]), keep_ref, send_ref)
+    keep_ref[0], send_ref[0] = halves(core_ref, product_wide(a_ref[...], wide_ref[...], third_ref[...]))
 
 
 def back_kernel(core_ref, a_ref, mine_ref, other_ref, out_ref, back_ref, gram_ref):
@@ -161,15 +186,20 @@
         wide = jnp.concatenate([i1, i2], axis=1)
         first_ref[...] = product_wide(image_ref[...], wide, i3)
         back = product_wide(back, wide, i3)
-        gram_back = product(back.T, back)
-        gram_ref[...] = gram_back
-        send_ref[send_ref.shape[0] - 1] = gram_back
+        top, diagonal = pack(product(back.T, back))
+        edge = top.shape[0]
+        start = send_ref.shape[0] - edge - 8
+        gram_ref[:edge] = top
+        gram_ref[edge:] = diagonal
+        send_ref[start : start + edge] = top
+        send_ref[start + edge :] = diagonal
         b1, b2, b3 = terms(back)
         wide_ref[...] = jnp.concatenate([b1, b2], axis=1)
         third_ref[...] = b3
 
-    value = product_wide(a_ref[...], wide_ref[...], third_ref[...])
-    part_store(core_ref, value, keep_ref, send_ref.at[pl.ds(step, 1)])
+    keep, send = halves(core_ref, product_wide(a_ref[...], wide_ref[...], third_ref[...]))
+    keep_ref[0] = keep
+    send_ref[pl.ds(pl.multiple_of(step * keep.shape[0], keep.shape[0]), keep.shape[0])] = send
 
 
 def last_gram_kernel(parts_ref, range_ref, gram_ref):
@@ -177,7 +207,7 @@
     total = parts_ref[0]
     for k in range(1, parts_ref.shape[0]):
         total = total + parts_ref[k]
-    unused, inverse = eliminate(total[n:])
+    unused, inverse = eliminate(unpack(total[n:]))
     block = product(total[:n], inverse.T)
     range_ref[...] = block
     gram_ref[...] = product(block.T, block)
@@ -239,15 +269,16 @@
 def range_parts(core, a, both, image_block):
     rows, depth = a.shape
     n, steps = both.shape[2], rows // ROWS
+    packed = n // 2 + 8
     block = pl.BlockSpec((1, ROWS // 2, n), lambda i, core: (i, 0, 0))
     return pl.pallas_call(
         range_kernel,
-        out_shape=[shape(steps, ROWS // 2, n), shape(steps + 1, ROWS // 2, n), shape(n, n), shape(n, n)],
+        out_shape=[shape(steps, ROWS // 2, n), shape(rows // 2 + packed, n), shape(packed, n), shape(n, n)],
         grid_spec=pltpu.PrefetchScalarGridSpec(
             num_scalar_prefetch=1,
             grid=(steps,),
             in_specs=[pl.BlockSpec((ROWS, depth), lambda i, core: (i, 0)), whole(*both.shape), whole(n, n)],
-            out_specs=[block, whole(steps + 1, ROWS // 2, n), whole(n, n), whole(n, n)],
+            out_specs=[block, whole(rows // 2 + packed, n), whole(packed, n), whole(n, n)],
             scratch_shapes=[pltpu.VMEM((depth, 2 * n), jnp.bfloat16), pltpu.VMEM((depth, n), jnp.bfloat16)],
         ),
         compiler_params=BIG,
@@ -258,7 +289,7 @@
 def last_gram(parts):
     n = parts.shape[2]
     return pl.pallas_call(
-        last_gram_kernel, out_shape=[shape(n, n)] * 2, compiler_params=BIG, name="last_gram"
+        last_gram_kernel, out_shape=[shape(n, n)] * 2, compiler_params=SMALL, name="last_gram"
     )(parts)
 
 
@@ -267,7 +298,7 @@
     return pl.pallas_call(
         lambda *refs: basis_kernel(tokens, *refs),
         out_shape=[shape(n, n)] * 2,
-        compiler_params=BIG,
+        compiler_params=SMALL,
         name="basis",
     )(gram, block)
 
@@ -294,9 +325,10 @@
     both = gather(sums, NEAR)
     keep, send, gram_part, first_block = range_parts(core, activations, both, image_block)
     received = lax.ppermute(send, "core", SWAP)
-    count = keep.shape[0]
-    gram_part = jnp.broadcast_to(gram_part[None] + received[count:], (count, width, width))
-    parts = jnp.concatenate([keep + received[:count], gram_part], axis=1)
+    count, rows = keep.shape[:2]
+    gram_part = gram_part + received[count * rows :]
+    gram_part = jnp.broadcast_to(gram_part[None], (count,) + gram_part.shape)
+    parts = jnp.concatenate([keep + received[: count * rows].reshape(keep.shape), gram_part], axis=1)
     range_block, gram_part = last_gram(lax.all_to_all(parts, PLANE, 0, 0))
     gram_slice = scatter_sum(gram_part.reshape(lax.axis_size(CROSS), -1, width), CROSS)
     gram_slice = jnp.sum(gather(gram_slice, ("z_hi", "z_lo")), axis=0)

time: 198 us -> 204 us (1.030)
  Pallas kernels: 29.1 us -> 39.5 us
  local copies, waits for them, and re-layouts: 7.64 us -> 0.97 us
  other arithmetic: 0.33 us -> 3.21 us
    unnamed x8 -> x6, local copies, waits for them, and re-layouts: 7.51 us -> 0.82 us
    pallas_call x1, Pallas kernels: 3.84 us -> 7.7 us  [image_parts(): pl.pallas_call(image_kernel, out_shape=[shape(steps, ROWS // 2, n)] * 2,...]
    pallas_call x1, Pallas kernels: 4.39 us -> 7.98 us  [back_parts(): pl.pallas_call(back_kernel, out_shape=shape(count, chunk, n), grid_spec=p...]
    pallas_call x1, Pallas kernels: 9.9 us -> 13.5 us  [range_parts(): pl.pallas_call(range_kernel, out_shape=[shape(steps, ROWS // 2, n), shape...]
where the time goes in v4:
time: 204 us; the launch traced here: 203 us
  blocking collectives  133 us (65%)
  Pallas kernels  39.5 us (19%)
  starting transfers between devices  20.4 us (10%)
  waiting for transfers between devices  5.02 us (2%)
  other arithmetic  3.21 us (2%)
    all_to_all x5, blocking collectives, gather(): lax.all_to_all(jnp.broadcast_to(block[None], (count,) + block.shape), axi...  77.5 us
    all_to_all x3, blocking collectives, scatter_sum(): return jnp.sum(lax.all_to_all(parts, axis, 0, 0), axis=0)  38.6 us
    all_to_all x1, blocking collectives, per_device(): range_block, gram_part = last_gram(lax.all_to_all(parts, PLANE, 0, 0))  17 us
    pallas_call x1, Pallas kernels, range_parts(): pl.pallas_call(range_kernel, out_shape=[shape(steps, ROWS // 2, n), shape...  13.5 us
    ppermute x1, starting transfers between devices, per_device(): image_block = scatter_sum(keep + lax.ppermute(send, 'core', SWAP), PLANE)  8.77 us
    pallas_call x1, Pallas kernels, back_parts(): pl.pallas_call(back_kernel, out_shape=shape(count, chunk, n), grid_spec=p...  7.98 us
    pallas_call x1, Pallas kernels, image_parts(): pl.pallas_call(image_kernel, out_shape=[shape(steps, ROWS // 2, n)] * 2,...  7.7 us
    ppermute x1, starting transfers between devices, per_device(): received = lax.ppermute(send, 'core', SWAP)  7.2 us
  transfers between devices with their start and end apart: 3, of which 3 were waited for; matrix products, arithmetic and copies ran while one was open for 0% of the time, Pallas kernels for 0%

profile of v4, /device:TPU:1, one launch (start us, length us, event | category | flops | bytes accessed | tf_op | source)
XLA Modules:
  0.0 202.9 jit_solution(13555562047626337041)
XLA Ops:
  0.6 7.7 %image_parts.1 = (f32[8,128,128]{2,1,0:T(8,128)}, f32[8,128,128]{2,1,0:T(8,128)}) custom-call(s32[1]{0:T(128)} %bitcast.core_ref, f32[2048,512]{1,0:T(8,128)} %a_ref.5, f32[512,128]{1,0:T(8,128)} %s_ref.1), custom_call_target="tpu_custom_call" | custom-call | tf_op jit(solution)/shard_map/image_parts/pallas_call | solution.py:234
  8.3 8.8 %collective-permute-start = (f32[8,128,128]{2,1,0:T(8,128)}, f32[8,128,128]{2,1,0:T(8,128)S(1)}, u32[]{:S(2)}, u32[]{:S(2)}) collective-permute-start(f32[8,128,128]{2,1,0:T(8,128)} %get-tuple-element.14), channel_id=1, source_target_pairs={{0,1},{1,0},{2,3},{3,2},{4,5},{5,4},{6,7},{7,6},{8,9},{9,8},{10,11... | collective-permute-start | bytes 1572872 | tf_op jit(solution)/shard_map/ppermute | solution.py:319
  17.1 1.7 collective-permute-done
  18.8 1.1 add.9
  20.0 13.8 %all_to_all.45 = f32[8,128,128]{2,1,0:T(8,128)S(1)} all-to-all(f32[8,128,128]{2,1,0:T(8,128)S(1)} %add.9), channel_id=1, replica_groups=mesh['x_lo'=2,'z_hi'=4,'z_lo'=4,'y'=4,'x_hi'=2,'core'=2] {'y','x_hi'}, dimensions={0} | all-to-all | bytes 1048576 | tf_op jit(solution)/shard_map/all_to_all | solution.py:307
  33.7 0.0 copy-start.1
  33.8 12.5 %all_to_all.46.mine_ref = f32[8,128,128]{2,1,0:T(8,128)S(1)} all-to-all(f32[8,128,128]{2,1,0:T(8,128)S(1)} %broadcast_in_dim.12), channel_id=1, replica_groups=mesh['x_lo'=2,'z_hi'=4,'z_lo'=4,'y'=4,'x_hi'=2,'core'=2] {'y','x_hi'}, dimensions={0} | all-to-all | bytes 1048576 | tf_op jit(solution)/shard_map/all_to_all | solution.py:312
  46.3 0.0 copy-start
  46.3 4.4 %collective-permute-start.1 = (f32[8,128,128]{2,1,0:T(8,128)S(1)}, f32[8,128,128]{2,1,0:T(8,128)S(1)}, u32[]{:S(2)}, u32[]{:S(2)}) collective-permute-start(f32[8,128,128]{2,1,0:T(8,128)S(1)} %all_to_all.46.mine_ref), channel_id=1, source_target_pairs={{0,1},{1,0},{2,3},{3,2},{4,5},{5,4},{6,7},{7,6},{8,9},{9,8},{10,11... | collective-permute-start | bytes 1572872 | tf_op jit(solution)/shard_map/ppermute | solution.py:321
  50.7 1.5 collective-permute-done.1.other_ref
  52.2 0.0 copy-done
  52.2 0.0 copy-start.2
  52.2 0.8 copy-done.2
  53.0 8.0 %back_parts.1 = f32[8,80,128]{2,1,0:T(8,128)} custom-call(s32[1]{0:T(128)} %bitcast.core_ref, f32[2048,512]{1,0:T(8,128)} %a_ref.5, f32[8,128,128]{2,1,0:T(8,128)} %copy-done, f32[8,128,128]{2,1,0:T(8,128)} %copy-done.2), custom_call_target="tpu_custom_call" | custom-call | tf_op jit(solution)/shard_map/back_parts/pallas_call | solution.py:254
  61.0 13.6 %all_to_all.47 = f32[8,80,128]{2,1,0:T(8,128)S(1)} all-to-all(f32[8,80,128]{2,1,0:T(8,128)} %back_parts.1), channel_id=1, replica_groups=mesh['x_lo'=2,'z_hi'=4,'z_lo'=4,'y'=4,'x_hi'=2,'core'=2] {'x_lo','z_lo'}, dimensions={0} | all-to-all | bytes 655360 | tf_op jit(solution)/shard_map/all_to_all | solution.py:307
  74.6 0.0 copy-done.1
  74.7 27.1 %all_to_all.48 = f32[4,80,128]{2,1,0:T(8,128)S(1)} all-to-all(f32[4,80,128]{2,1,0:T(8,128)S(1)} %broadcast_in_dim.13), channel_id=1, replica_groups=mesh['x_lo'=2,'z_hi'=4,'z_lo'=4,'y'=4,'x_hi'=2,'core'=2] {'z_hi'}, dimensions={0} | all-to-all | bytes 327680 | tf_op jit(solution)/shard_map/all_to_all | solution.py:312
  101.8 11.1 %all_to_all.49.both_ref = f32[8,80,128]{2,1,0:T(8,128)} all-to-all(f32[8,80,128]{2,1,0:T(8,128)S(1)} %broadcast_in_dim.14), channel_id=1, replica_groups=mesh['x_lo'=2,'z_hi'=4,'z_lo'=4,'y'=4,'x_hi'=2,'core'=2] {'x_lo','z_lo'}, dimensions={0} | all-to-all | bytes 655360 | tf_op jit(solution)/shard_map/all_to_all | solution.py:312
  112.9 13.5 %range_parts.1 = (f32[8,128,128]{2,1,0:T(8,128)}, f32[1096,128]{1,0:T(8,128)}, f32[72,128]{1,0:T(8,128)}, f32[128,128]{1,0:T(8,128)}) custom-call(s32[1]{0:T(128)} %bitcast.core_ref, f32[2048,512]{1,0:T(8,128)} %a_ref.5, f32[8,80,128]{2,1,0:T(8,128)} %all_to_all.49.both_ref, f32[128,128]{1,0:T(8,128)} %copy-done.1), custom_call_target="tpu_custom_call" | custom-call | tf_op jit(solution)/shard_map/range_parts/pallas_call | solution.py:274
  126.3 7.2 %collective-permute-start.2 = (f32[1096,128]{1,0:T(8,128)}, f32[1096,128]{1,0:T(8,128)S(1)}, u32[]{:S(2)}, u32[]{:S(2)}) collective-permute-start(f32[1096,128]{1,0:T(8,128)} %get-tuple-element.17), channel_id=1, source_target_pairs={{0,1},{1,0},{2,3},{3,2},{4,5},{5,4},{6,7},{7,6},{8,9},{9,8},{10,11... | collective-permute-start | bytes 1683464 | tf_op jit(solution)/shard_map/ppermute | solution.py:327
  133.6 1.8 collective-permute-done.2
  135.4 1.1 add.10
  136.5 0.8 slice_add_fusion
  137.3 0.1 pad_maximum_fusion
  137.4 17.0 %all_to_all.50.parts_ref = f32[8,200,128]{2,1,0:T(8,128)S(1)} all-to-all(f32[8,200,128]{2,1,0:T(8,128)S(1)} %pad_maximum_fusion), channel_id=1, replica_groups=mesh['x_lo'=2,'z_hi'=4,'z_lo'=4,'y'=4,'x_hi'=2,'core'=2] {'y','x_hi'}, dimensions={0} | all-to-all | bytes 1638400 | tf_op jit(solution)/shard_map/all_to_all | solution.py:332
  154.4 5.2 %last_gram.1 = (f32[128,128]{1,0:T(8,128)S(1)}, f32[128,128]{1,0:T(8,128)S(1)}) custom-call(f32[8,200,128]{2,1,0:T(8,128)S(1)} %all_to_all.50.parts_ref), custom_call_target="tpu_custom_call" | custom-call | tf_op jit(solution)/shard_map/last_gram/pallas_call | solution.py:291
  159.5 11.2 %all_to_all.51 = f32[32,4,128]{2,1,0:T(4,128)S(1)} all-to-all(f32[32,4,128]{2,1,0:T(4,128)S(1)} %bitcast.5), channel_id=1, replica_groups=mesh['x_lo'=2,'z_hi'=4,'z_lo'=4,'y'=4,'x_hi'=2,'core'=2] {'x_lo','y','x_..., dimensions={0} | all-to-all | bytes 131072 | tf_op jit(solution)/shard_map/all_to_all | solution.py:307
  170.8 14.6 %all_to_all.52 = f32[16,4,128]{2,1,0:T(4,128)S(1)} all-to-all(f32[16,4,128]{2,1,0:T(4,128)S(1)} %broadcast_in_dim.16), channel_id=1, replica_groups=mesh['x_lo'=2,'z_hi'=4,'z_lo'=4,'y'=4,'x_hi'=2,'core'=2] {'z_hi','z_lo'}, dimensions={0} | all-to-all | bytes 65536 | tf_op jit(solution)/shard_map/all_to_all | solution.py:312
  185.4 12.3 %all_to_all.53 = f32[32,4,128]{2,1,0:T(4,128)S(1)} all-to-all(f32[32,4,128]{2,1,0:T(4,128)S(1)} %broadcast_in_dim.17), channel_id=1, replica_groups=mesh['x_lo'=2,'z_hi'=4,'z_lo'=4,'y'=4,'x_hi'=2,'core'=2] {'x_lo','y','x_..., dimensions={0} | all-to-all | bytes 131072 | tf_op jit(solution)/shard_map/all_to_all | solution.py:312
  197.7 5.2 %basis.1 = (f32[128,128]{1,0:T(8,128)}, f32[128,128]{1,0:T(8,128)}) custom-call(f32[128,128]{1,0:T(8,128)S(1)} %bitcast.4, f32[128,128]{1,0:T(8,128)S(1)} %get-tuple-element.20.refs_1_), custom_call_target="tpu_custom_call" | custom-call | tf_op jit(solution)/shard_map/basis/pallas_call | solution.py:298
  (12 shorter events, 0.3 us)
Async XLA Ops:
  8.3 10.5 %collective-permute-start = (f32[8,128,128]{2,1,0:T(8,128)}, f32[8,128,128]{2,1,0:T(8,128)S(1)}, u32[]{:S(2)}, u32[]{:S(2)}) collective-permute-start(f32[8,128,128]{2,1,0:T(8,128)} %get-tuple-element.14), channel_id=1, source_target_pairs={{0,1},{1,0},{2,3},{3,2},{4,5},{5,4},{6,7},{7,6},{8,9},{9,8},{10,11... | collective-permute-start | bytes 1572872 | tf_op jit(solution)/shard_map/ppermute | solution.py:319
  33.7 40.9 %copy-start.1 = (f32[128,128]{1,0:T(8,128)}, f32[128,128]{1,0:T(8,128)S(1)}, u32[]{:S(2)}) copy-start(f32[128,128]{1,0:T(8,128)S(1)} %reduce_sum.45.image_ref) | copy-start | bytes 196612
  46.3 5.9 %copy-start = (f32[8,128,128]{2,1,0:T(8,128)}, f32[8,128,128]{2,1,0:T(8,128)S(1)}, u32[]{:S(2)}) copy-start(f32[8,128,128]{2,1,0:T(8,128)S(1)} %all_to_all.46.mine_ref) | copy-start | bytes 1572868
  46.3 5.9 %collective-permute-start.1 = (f32[8,128,128]{2,1,0:T(8,128)S(1)}, f32[8,128,128]{2,1,0:T(8,128)S(1)}, u32[]{:S(2)}, u32[]{:S(2)}) collective-permute-start(f32[8,128,128]{2,1,0:T(8,128)S(1)} %all_to_all.46.mine_ref), channel_id=1, source_target_pairs={{0,1},{1,0},{2,3},{3,2},{4,5},{5,4},{6,7},{7,6},{8,9},{9,8},{10,11... | collective-permute-start | bytes 1572872 | tf_op jit(solution)/shard_map/ppermute | solution.py:321
  52.2 0.8 copy-start.2
  126.3 9.0 %collective-permute-start.2 = (f32[1096,128]{1,0:T(8,128)}, f32[1096,128]{1,0:T(8,128)S(1)}, u32[]{:S(2)}, u32[]{:S(2)}) collective-permute-start(f32[1096,128]{1,0:T(8,128)} %get-tuple-element.17), channel_id=1, source_target_pairs={{0,1},{1,0},{2,3},{3,2},{4,5},{5,4},{6,7},{7,6},{8,9},{9,8},{10,11... | collective-permute-start | bytes 1683464 | tf_op jit(solution)/shard_map/ppermute | solution.py:327

commit v5 on v4

--- a/solution.py
+++ b/solution.py
@@ -11,8 +11,7 @@
 PLANE = ("y", "x_hi")
 NEAR = ("x_lo", "z_lo")
 CROSS = ("x_lo", "y", "x_hi", "core")
-BIG = pltpu.CompilerParams(vmem_limit_bytes=61 * 1024 * 1024)
-SMALL = pltpu.CompilerParams(vmem_limit_bytes=32 * 1024 * 1024)
+PARAMS = pltpu.CompilerParams(vmem_limit_bytes=32 * 1024 * 1024)
 
 
 def terms(value):
@@ -133,73 +132,82 @@
     return jnp.where(is_first, low, high), jnp.where(is_first, high, low)
 
 
-def image_kernel(core_ref, a_ref, s_ref, keep_ref, send_ref, wide_ref, third_ref):
-    @pl.when(pl.program_id(0) == 0)
-    def _():
-        s1, s2, s3 = terms(s_ref[...])
-        wide_ref[...] = jnp.concatenate([s1, s2], axis=1)
-        third_ref[...] = s3
-
-    keep_ref[0], send_ref[0] = halves(core_ref, product_wide(a_ref[...], wide_ref[...], third_ref[...]))
-
-
-def back_kernel(core_ref, a_ref, mine_ref, other_ref, out_ref, back_ref, gram_ref):
-    step = pl.program_id(0)
-
-    @pl.when(step == 0)
-    def _():
-        back_ref[...] = jnp.zeros_like(back_ref)
-        gram_ref[...] = jnp.zeros_like(gram_ref)
-
+def start_copies(a_ref, held_ref, semaphores):
+    copies = []
+    for i in range(a_ref.shape[0] // ROWS):
+        rows = pl.ds(i * ROWS, ROWS)
+        copies.append(pltpu.make_async_copy(a_ref.at[rows], held_ref.at[rows], semaphores.at[i]))
+        copies[i].start()
+    return copies
+
+
+def image_kernel(
+    core_ref, a_ref, s_ref, keep_ref, send_ref, held_ref, sketch_ref, sketch_semaphore, semaphores
+):
+    sketch_copy = pltpu.make_async_copy(s_ref, sketch_ref, sketch_semaphore)
+    sketch_copy.start()
+    copies = start_copies(a_ref, held_ref, semaphores)
+    sketch_copy.wait()
+    s1, s2, s3 = terms(sketch_ref[...])
+    wide = jnp.concatenate([s1, s2], axis=1)
+    for i, copy in enumerate(copies):
+        copy.wait()
+        value = product_wide(held_ref[i * ROWS : (i + 1) * ROWS], wide, s3)
+        keep_ref[i], send_ref[i] = halves(core_ref, value)
+
+
+def back_kernel(core_ref, a_ref, mine_ref, other_ref, out_ref, held_ref, back_ref, gram_ref, semaphores):
+    copies = start_copies(a_ref, held_ref, semaphores)
     is_first = core_ref[0] == 0
-    mine, other = mine_ref[0], other_ref[0]
-    y = jnp.concatenate([jnp.where(is_first, mine, other), jnp.where(is_first, other, mine)], axis=0)
-    turned = y.T
-    back_ref[...] += product_tall(turned, a_ref[...])
-    gram_ref[...] += product_tall(turned, y)
-
-    @pl.when(step == pl.num_programs(0) - 1)
-    def _():
-        back, gram = back_ref[...].T, gram_ref[...]
-        count = out_ref.shape[0]
-        cut, small = back.shape[0] // count, gram.shape[0] // count
-        for k in range(count):
-            out_ref[k, :cut, :] = back[k * cut : (k + 1) * cut]
-            out_ref[k, cut:, :] = gram[k * small : (k + 1) * small]
+    for i, copy in enumerate(copies):
+        mine, other = mine_ref[i], other_ref[i]
+        y = jnp.concatenate([jnp.where(is_first, mine, other), jnp.where(is_first, other, mine)], axis=0)
+        turned = y.T
+        gram = product_tall(turned, y)
+        copy.wait()
+        back = product_tall(turned, held_ref[i * ROWS : (i + 1) * ROWS])
+        if i == 0:
+            back_ref[...], gram_ref[...] = back, gram
+        else:
+            back_ref[...] += back
+            gram_ref[...] += gram
+    back, gram = back_ref[...].T, gram_ref[...]
+    count = out_ref.shape[0]
+    cut, small = back.shape[0] // count, gram.shape[0] // count
+    for k in range(count):
+        out_ref[k, :cut, :] = back[k * cut : (k + 1) * cut]
+        out_ref[k, cut:, :] = gram[k * small : (k + 1) * small]
 
 
 def range_kernel(
-    core_ref, a_ref, both_ref, image_ref, keep_ref, send_ref, gram_ref, first_ref, wide_ref, third_ref
+    core_ref, a_ref, both_ref, image_ref, keep_ref, send_ref, gram_ref, first_ref, held_ref, semaphores
 ):
-    step = pl.program_id(0)
-
-    @pl.when(step == 0)
-    def _():
-        n = first_ref.shape[1]
-        count = both_ref.shape[0]
-        small = n // count
-        cut = both_ref.shape[1] - small
-        gram = jnp.concatenate([both_ref[k, cut:, :] for k in range(count)], axis=0)
-        back = jnp.concatenate([both_ref[k, :cut, :] for k in range(count)], axis=0)
-        unused, inverse = eliminate(gram)
-        i1, i2, i3 = terms(inverse.T)
-        wide = jnp.concatenate([i1, i2], axis=1)
-        first_ref[...] = product_wide(image_ref[...], wide, i3)
-        back = product_wide(back, wide, i3)
-        top, diagonal = pack(product(back.T, back))
-        edge = top.shape[0]
-        start = send_ref.shape[0] - edge - 8
-        gram_ref[:edge] = top
-        gram_ref[edge:] = diagonal
-        send_ref[start : start + edge] = top
-        send_ref[start + edge :] = diagonal
-        b1, b2, b3 = terms(back)
-        wide_ref[...] = jnp.concatenate([b1, b2], axis=1)
-        third_ref[...] = b3
-
-    keep, send = halves(core_ref, product_wide(a_ref[...], wide_ref[...], third_ref[...]))
-    keep_ref[0] = keep
-    send_ref[pl.ds(pl.multiple_of(step * keep.shape[0], keep.shape[0]), keep.shape[0])] = send
+    copies = start_copies(a_ref, held_ref, semaphores)
+    n = first_ref.shape[1]
+    count = both_ref.shape[0]
+    small = n // count
+    cut = both_ref.shape[1] - small
+    gram = jnp.concatenate([both_ref[k, cut:, :] for k in range(count)], axis=0)
+    back = jnp.concatenate([both_ref[k, :cut, :] for k in range(count)], axis=0)
+    unused, inverse = eliminate(gram)
+    i1, i2, i3 = terms(inverse.T)
+    wide = jnp.concatenate([i1, i2], axis=1)
+    first_ref[...] = product_wide(image_ref[...], wide, i3)
+    back = product_wide(back, wide, i3)
+    top, diagonal = pack(product(back.T, back))
+    edge = top.shape[0]
+    start = send_ref.shape[0] - edge - 8
+    gram_ref[:edge] = top
+    gram_ref[edge:] = diagonal
+    send_ref[start : start + edge] = top
+    send_ref[start + edge :] = diagonal
+    b1, b2, b3 = terms(back)
+    wide = jnp.concatenate([b1, b2], axis=1)
+    half = ROWS // 2
+    for i, copy in enumerate(copies):
+        copy.wait()
+        value = product_wide(held_ref[i * ROWS : (i + 1) * ROWS], wide, b3)
+        keep_ref[i], send_ref[i * half : (i + 1) * half] = halves(core_ref, value)
 
 
 def last_gram_kernel(parts_ref, range_ref, gram_ref):
@@ -223,73 +231,44 @@
     return jax.ShapeDtypeStruct(sizes, jnp.float32)
 
 
-def whole(*sizes):
-    return pl.BlockSpec(sizes, lambda i, core: (0,) * len(sizes))
+def reading(kernel, a, others, out_shape, scratch, name):
+    places = [pltpu.SMEM, pltpu.HBM] + others
+    return pl.pallas_call(
+        kernel,
+        out_shape=out_shape,
+        in_specs=[pl.BlockSpec(memory_space=place) for place in places],
+        scratch_shapes=[pltpu.VMEM(a.shape, jnp.float32)]
+        + scratch
+        + [pltpu.SemaphoreType.DMA((a.shape[0] // ROWS,))],
+        compiler_params=PARAMS,
+        name=name,
+    )
 
 
 def image_parts(core, a, s):
-    rows, depth = a.shape
-    n, steps = s.shape[1], rows // ROWS
-    block = pl.BlockSpec((1, ROWS // 2, n), lambda i, core: (i, 0, 0))
-    return pl.pallas_call(
-        image_kernel,
-        out_shape=[shape(steps, ROWS // 2, n)] * 2,
-        grid_spec=pltpu.PrefetchScalarGridSpec(
-            num_scalar_prefetch=1,
-            grid=(steps,),
-            in_specs=[pl.BlockSpec((ROWS, depth), lambda i, core: (i, 0)), whole(depth, n)],
-            out_specs=[block, block],
-            scratch_shapes=[pltpu.VMEM((depth, 2 * n), jnp.bfloat16), pltpu.VMEM((depth, n), jnp.bfloat16)],
-        ),
-        compiler_params=BIG,
-        name="image_parts",
-    )(core, a, s)
+    parts = shape(a.shape[0] // ROWS, ROWS // 2, s.shape[1])
+    scratch = [pltpu.VMEM(s.shape, jnp.float32), pltpu.SemaphoreType.DMA]
+    return reading(image_kernel, a, [pltpu.HBM], [parts, parts], scratch, "image_parts")(core, a, s)
 
 
 def back_parts(core, a, mine, other, count):
-    rows, depth = a.shape
-    n, steps = mine.shape[2], rows // ROWS
-    chunk = (depth + n) // count
-    block = pl.BlockSpec((1, ROWS // 2, n), lambda i, core: (i, 0, 0))
-    return pl.pallas_call(
-        back_kernel,
-        out_shape=shape(count, chunk, n),
-        grid_spec=pltpu.PrefetchScalarGridSpec(
-            num_scalar_prefetch=1,
-            grid=(steps,),
-            in_specs=[pl.BlockSpec((ROWS, depth), lambda i, core: (i, 0)), block, block],
-            out_specs=whole(count, chunk, n),
-            scratch_shapes=[pltpu.VMEM((n, depth), jnp.float32), pltpu.VMEM((n, n), jnp.float32)],
-        ),
-        compiler_params=BIG,
-        name="back_parts",
-    )(core, a, mine, other)
+    n, depth = mine.shape[2], a.shape[1]
+    scratch = [pltpu.VMEM((n, depth), jnp.float32), pltpu.VMEM((n, n), jnp.float32)]
+    out_shape = shape(count, (depth + n) // count, n)
+    return reading(back_kernel, a, [pltpu.VMEM] * 2, out_shape, scratch, "back_parts")(core, a, mine, other)
 
 
 def range_parts(core, a, both, image_block):
-    rows, depth = a.shape
-    n, steps = both.shape[2], rows // ROWS
+    rows, n = a.shape[0], both.shape[2]
     packed = n // 2 + 8
-    block = pl.BlockSpec((1, ROWS // 2, n), lambda i, core: (i, 0, 0))
-    return pl.pallas_call(
-        range_kernel,
-        out_shape=[shape(steps, ROWS // 2, n), shape(rows // 2 + packed, n), shape(packed, n), shape(n, n)],
-        grid_spec=pltpu.PrefetchScalarGridSpec(
-            num_scalar_prefetch=1,
-            grid=(steps,),
-            in_specs=[pl.BlockSpec((ROWS, depth), lambda i, core: (i, 0)), whole(*both.shape), whole(n, n)],
-            out_specs=[block, whole(rows // 2 + packed, n), whole(packed, n), whole(n, n)],
-            scratch_shapes=[pltpu.VMEM((depth, 2 * n), jnp.bfloat16), pltpu.VMEM((depth, n), jnp.bfloat16)],
-        ),
-        compiler_params=BIG,
-        name="range_parts",
-    )(core, a, both, image_block)
+    out_shape = [shape(rows // ROWS, ROWS // 2, n), shape(rows // 2 + packed, n), shape(packed, n), shape(n, n)]
+    return reading(range_kernel, a, [pltpu.VMEM] * 2, out_shape, [], "range_parts")(core, a, both, image_block)
 
 
 def last_gram(parts):
     n = parts.shape[2]
     return pl.pallas_call(
-        last_gram_kernel, out_shape=[shape(n, n)] * 2, compiler_params=SMALL, name="last_gram"
+        last_gram_kernel, out_shape=[shape(n, n)] * 2, compiler_params=PARAMS, name="last_gram"
     )(parts)
 
 
@@ -298,7 +277,7 @@
     return pl.pallas_call(
         lambda *refs: basis_kernel(tokens, *refs),
         out_shape=[shape(n, n)] * 2,
-        compiler_params=SMALL,
+        compiler_params=PARAMS,
         name="basis",
     )(gram, block)
 
@@ -315,6 +294,8 @@
 def per_device(activations, sketch):
     width = sketch.shape[1]
     core = lax.axis_index("core").astype(jnp.int32).reshape(1)
+    activations = pltpu.with_memory_space_constraint(activations, pltpu.HBM)
+    sketch = pltpu.with_memory_space_constraint(sketch, pltpu.HBM)
     keep, send = image_parts(core, activations, sketch)
     image_block = scatter_sum(keep + lax.ppermute(send, "core", SWAP), PLANE)
     mine = gather(image_block, PLANE)

time: 204 us -> 191 us (0.936)
  Pallas kernels: 39.5 us -> 31 us
  other arithmetic: 3.21 us -> 0.31 us
    pallas_call x3, Pallas kernels: 29.1 us -> 20.7 us  [the longest x1 9.73 us: range_parts(): reading(range_kernel, a, [pltpu.VMEM] * 2, out_shape, [], 'range_parts')]
where the time goes in v5:
time: 191 us; the launch traced here: 190 us
  blocking collectives  133 us (70%)
  Pallas kernels  31 us (16%)
  starting transfers between devices  20.5 us (11%)
  waiting for transfers between devices  4.6 us (2%)
    all_to_all x5, blocking collectives, gather(): lax.all_to_all(jnp.broadcast_to(block[None], (count,) + block.shape), axi...  77.1 us
    all_to_all x3, blocking collectives, scatter_sum(): return jnp.sum(lax.all_to_all(parts, axis, 0, 0), axis=0)  38.8 us
    all_to_all x1, blocking collectives, per_device(): range_block, gram_part = last_gram(lax.all_to_all(parts, PLANE, 0, 0))  17.1 us
    pallas_call x1, Pallas kernels, range_parts(): reading(range_kernel, a, [pltpu.VMEM] * 2, out_shape, [], 'range_parts')  9.73 us
    ppermute x1, starting transfers between devices, per_device(): image_block = scatter_sum(keep + lax.ppermute(send, 'core', SWAP), PLANE)  8.78 us
    ppermute x1, starting transfers between devices, per_device(): received = lax.ppermute(send, 'core', SWAP)  7.35 us
    pallas_call x1, Pallas kernels, image_parts(): reading(image_kernel, a, [pltpu.HBM], [parts, parts], scratch, 'image_par...  5.87 us
    pallas_call x1, Pallas kernels, last_gram(): pl.pallas_call(last_gram_kernel, out_shape=[shape(n, n)] * 2, compiler_pa...  5.17 us
  transfers between devices with their start and end apart: 3, of which 3 were waited for; matrix products, arithmetic and copies ran while one was open for 0% of the time, Pallas kernels for 0%

profile of v5, /device:TPU:1, one launch (start us, length us, event | category | flops | bytes accessed | tf_op | source)
XLA Modules:
  0.0 190.3 jit_solution(10626998348487100664)
XLA Ops:
  0.6 5.9 %image_parts.1 = (f32[8,128,128]{2,1,0:T(8,128)S(1)}, f32[8,128,128]{2,1,0:T(8,128)S(1)}) custom-call(s32[1]{0:T(128)} %bitcast.core_ref, f32[2048,512]{1,0:T(8,128)} %a_ref.5, f32[512,128]{1,0:T(8,128)} %s_ref.1), custom_call_target="tpu_custom_call" | custom-call | tf_op jit(solution)/shard_map/image_parts/pallas_call | solution.py:251
  6.5 8.8 %collective-permute-start = (f32[8,128,128]{2,1,0:T(8,128)S(1)}, f32[8,128,128]{2,1,0:T(8,128)S(1)}, u32[]{:S(2)}, u32[]{:S(2)}) collective-permute-start(f32[8,128,128]{2,1,0:T(8,128)S(1)} %get-tuple-element.14), channel_id=1, source_target_pairs={{0,1},{1,0},{2,3},{3,2},{4,5},{5,4},{6,7},{7,6},{8,9},{9,8},{10,11... | collective-permute-start | bytes 1572872 | tf_op jit(solution)/shard_map/ppermute | solution.py:300
  15.3 1.5 collective-permute-done
  16.8 0.1 add.9
  16.9 13.8 %all_to_all.45 = f32[8,128,128]{2,1,0:T(8,128)S(1)} all-to-all(f32[8,128,128]{2,1,0:T(8,128)S(1)} %add.9), channel_id=1, replica_groups=mesh['x_lo'=2,'z_hi'=4,'z_lo'=4,'y'=4,'x_hi'=2,'core'=2] {'y','x_hi'}, dimensions={0} | all-to-all | bytes 1048576 | tf_op jit(solution)/shard_map/all_to_all | solution.py:286
  30.7 12.5 %all_to_all.46.mine_ref = f32[8,128,128]{2,1,0:T(8,128)S(1)} all-to-all(f32[8,128,128]{2,1,0:T(8,128)S(1)} %broadcast_in_dim.12), channel_id=1, replica_groups=mesh['x_lo'=2,'z_hi'=4,'z_lo'=4,'y'=4,'x_hi'=2,'core'=2] {'y','x_hi'}, dimensions={0} | all-to-all | bytes 1048576 | tf_op jit(solution)/shard_map/all_to_all | solution.py:291
  43.2 4.4 %collective-permute-start.1 = (f32[8,128,128]{2,1,0:T(8,128)S(1)}, f32[8,128,128]{2,1,0:T(8,128)S(1)}, u32[]{:S(2)}, u32[]{:S(2)}) collective-permute-start(f32[8,128,128]{2,1,0:T(8,128)S(1)} %all_to_all.46.mine_ref), channel_id=1, source_target_pairs={{0,1},{1,0},{2,3},{3,2},{4,5},{5,4},{6,7},{7,6},{8,9},{9,8},{10,11... | collective-permute-start | bytes 1572872 | tf_op jit(solution)/shard_map/ppermute | solution.py:302
  47.6 1.5 collective-permute-done.1.other_ref
  49.1 5.1 %back_parts.1 = f32[8,80,128]{2,1,0:T(8,128)S(1)} custom-call(s32[1]{0:T(128)} %bitcast.core_ref, f32[2048,512]{1,0:T(8,128)} %a_ref.5, f32[8,128,128]{2,1,0:T(8,128)S(1)} %all_to_all.46.mine_ref, f32[8,128,128]{2,1,0:T(8,128)S(1)} %collective-permute-done.1.other_ref), custom_call_target="tpu_custom_call" | custom-call | tf_op jit(solution)/shard_map/back_parts/pallas_call | solution.py:258
  54.2 13.5 %all_to_all.47 = f32[8,80,128]{2,1,0:T(8,128)S(1)} all-to-all(f32[8,80,128]{2,1,0:T(8,128)S(1)} %back_parts.1), channel_id=1, replica_groups=mesh['x_lo'=2,'z_hi'=4,'z_lo'=4,'y'=4,'x_hi'=2,'core'=2] {'x_lo','z_lo'}, dimensions={0} | all-to-all | bytes 655360 | tf_op jit(solution)/shard_map/all_to_all | solution.py:286
  67.7 26.5 %all_to_all.48 = f32[4,80,128]{2,1,0:T(8,128)S(1)} all-to-all(f32[4,80,128]{2,1,0:T(8,128)S(1)} %broadcast_in_dim.13), channel_id=1, replica_groups=mesh['x_lo'=2,'z_hi'=4,'z_lo'=4,'y'=4,'x_hi'=2,'core'=2] {'z_hi'}, dimensions={0} | all-to-all | bytes 327680 | tf_op jit(solution)/shard_map/all_to_all | solution.py:291
  94.3 10.4 %all_to_all.49.both_ref = f32[8,80,128]{2,1,0:T(8,128)S(1)} all-to-all(f32[8,80,128]{2,1,0:T(8,128)S(1)} %broadcast_in_dim.14), channel_id=1, replica_groups=mesh['x_lo'=2,'z_hi'=4,'z_lo'=4,'y'=4,'x_hi'=2,'core'=2] {'x_lo','z_lo'}, dimensions={0} | all-to-all | bytes 655360 | tf_op jit(solution)/shard_map/all_to_all | solution.py:291
  104.7 9.7 %range_parts.1 = (f32[8,128,128]{2,1,0:T(8,128)S(1)}, f32[1096,128]{1,0:T(8,128)S(1)}, f32[72,128]{1,0:T(8,128)S(1)}, f32[128,128]{1,0:T(8,128)}) custom-call(s32[1]{0:T(128)} %bitcast.core_ref, f32[2048,512]{1,0:T(8,128)} %a_ref.5, f32[8,80,128]{2,1,0:T(8,128)S(1)} %all_to_all.49.both_ref, f32[128,128]{1,0:T(8,128)S(1)} %reduce_sum.45.image_ref), custom_call_target="tpu_custom_call" | custom-call | tf_op jit(solution)/shard_map/range_parts/pallas_call | solution.py:265
  114.4 7.4 %collective-permute-start.2 = (f32[1096,128]{1,0:T(8,128)S(1)}, f32[1096,128]{1,0:T(8,128)S(1)}, u32[]{:S(2)}, u32[]{:S(2)}) collective-permute-start(f32[1096,128]{1,0:T(8,128)S(1)} %get-tuple-element.17), channel_id=1, source_target_pairs={{0,1},{1,0},{2,3},{3,2},{4,5},{5,4},{6,7},{7,6},{8,9},{9,8},{10,11... | collective-permute-start | bytes 1683464 | tf_op jit(solution)/shard_map/ppermute | solution.py:308
  121.8 1.6 collective-permute-done.2
  123.4 0.1 add.10
  123.5 0.1 pad_maximum_fusion
  123.5 17.1 %all_to_all.50.parts_ref = f32[8,200,128]{2,1,0:T(8,128)S(1)} all-to-all(f32[8,200,128]{2,1,0:T(8,128)S(1)} %pad_maximum_fusion), channel_id=1, replica_groups=mesh['x_lo'=2,'z_hi'=4,'z_lo'=4,'y'=4,'x_hi'=2,'core'=2] {'y','x_hi'}, dimensions={0} | all-to-all | bytes 1638400 | tf_op jit(solution)/shard_map/all_to_all | solution.py:313
  140.7 5.2 %last_gram.1 = (f32[128,128]{1,0:T(8,128)S(1)}, f32[128,128]{1,0:T(8,128)S(1)}) custom-call(f32[8,200,128]{2,1,0:T(8,128)S(1)} %all_to_all.50.parts_ref), custom_call_target="tpu_custom_call" | custom-call | tf_op jit(solution)/shard_map/last_gram/pallas_call | solution.py:270
  145.8 11.5 %all_to_all.51 = f32[32,4,128]{2,1,0:T(4,128)S(1)} all-to-all(f32[32,4,128]{2,1,0:T(4,128)S(1)} %bitcast.5), channel_id=1, replica_groups=mesh['x_lo'=2,'z_hi'=4,'z_lo'=4,'y'=4,'x_hi'=2,'core'=2] {'x_lo','y','x_..., dimensions={0} | all-to-all | bytes 131072 | tf_op jit(solution)/shard_map/all_to_all | solution.py:286
  157.4 15.4 %all_to_all.52 = f32[16,4,128]{2,1,0:T(4,128)S(1)} all-to-all(f32[16,4,128]{2,1,0:T(4,128)S(1)} %broadcast_in_dim.16), channel_id=1, replica_groups=mesh['x_lo'=2,'z_hi'=4,'z_lo'=4,'y'=4,'x_hi'=2,'core'=2] {'z_hi','z_lo'}, dimensions={0} | all-to-all | bytes 65536 | tf_op jit(solution)/shard_map/all_to_all | solution.py:291
  172.9 12.3 %all_to_all.53 = f32[32,4,128]{2,1,0:T(4,128)S(1)} all-to-all(f32[32,4,128]{2,1,0:T(4,128)S(1)} %broadcast_in_dim.17), channel_id=1, replica_groups=mesh['x_lo'=2,'z_hi'=4,'z_lo'=4,'y'=4,'x_hi'=2,'core'=2] {'x_lo','y','x_..., dimensions={0} | all-to-all | bytes 131072 | tf_op jit(solution)/shard_map/all_to_all | solution.py:291
  185.2 5.2 %basis.1 = (f32[128,128]{1,0:T(8,128)}, f32[128,128]{1,0:T(8,128)}) custom-call(f32[128,128]{1,0:T(8,128)S(1)} %bitcast.4, f32[128,128]{1,0:T(8,128)S(1)} %get-tuple-element.20.refs_1_), custom_call_target="tpu_custom_call" | custom-call | tf_op jit(solution)/shard_map/basis/pallas_call | solution.py:277
  (13 shorter events, 0.3 us)
Async XLA Ops:
  6.5 10.3 %collective-permute-start = (f32[8,128,128]{2,1,0:T(8,128)S(1)}, f32[8,128,128]{2,1,0:T(8,128)S(1)}, u32[]{:S(2)}, u32[]{:S(2)}) collective-permute-start(f32[8,128,128]{2,1,0:T(8,128)S(1)} %get-tuple-element.14), channel_id=1, source_target_pairs={{0,1},{1,0},{2,3},{3,2},{4,5},{5,4},{6,7},{7,6},{8,9},{9,8},{10,11... | collective-permute-start | bytes 1572872 | tf_op jit(solution)/shard_map/ppermute | solution.py:300
  43.2 5.9 %collective-permute-start.1 = (f32[8,128,128]{2,1,0:T(8,128)S(1)}, f32[8,128,128]{2,1,0:T(8,128)S(1)}, u32[]{:S(2)}, u32[]{:S(2)}) collective-permute-start(f32[8,128,128]{2,1,0:T(8,128)S(1)} %all_to_all.46.mine_ref), channel_id=1, source_target_pairs={{0,1},{1,0},{2,3},{3,2},{4,5},{5,4},{6,7},{7,6},{8,9},{9,8},{10,11... | collective-permute-start | bytes 1572872 | tf_op jit(solution)/shard_map/ppermute | solution.py:302
  114.4 8.9 %collective-permute-start.2 = (f32[1096,128]{1,0:T(8,128)S(1)}, f32[1096,128]{1,0:T(8,128)S(1)}, u32[]{:S(2)}, u32[]{:S(2)}) collective-permute-start(f32[1096,128]{1,0:T(8,128)S(1)} %get-tuple-element.17), channel_id=1, source_target_pairs={{0,1},{1,0},{2,3},{3,2},{4,5},{5,4},{6,7},{7,6},{8,9},{9,8},{10,11... | collective-permute-start | bytes 1683464 | tf_op jit(solution)/shard_map/ppermute | solution.py:308

commit v6 on v5

--- a/solution.py
+++ b/solution.py
@@ -8,6 +8,8 @@
 PANEL = 8
 SWAP = [(0, 1), (1, 0)]
 ROWS = 256
+BLOCK = 1024
+FIRST_PANEL = 5
 PLANE = ("y", "x_hi")
 NEAR = ("x_lo", "z_lo")
 CROSS = ("x_lo", "y", "x_hi", "core")
@@ -58,7 +60,7 @@
     return values[0]
 
 
-def eliminate(gram):
+def eliminate(gram, between=lambda panel: None):
     n = gram.shape[0]
     count = n // 8
     tile = (8, n)
@@ -94,6 +96,7 @@
                 factors = [jnp.where(row > i, factors[i], 0.0) for i in range(PANEL)]
             left[u] = left[u] - tree([f * r for f, r in zip(factors, rows)])
             right[u] = right[u] - tree([f * r for f, r in zip(factors, more)])
+        between(v)
     upper, inverse = [], []
     for u in range(count):
         pivots = jnp.sum(jnp.where(lane == row + 8 * u, left[u], 0.0), axis=1, keepdims=True)
@@ -126,16 +129,17 @@
 
 
 def halves(core_ref, value):
-    half = value.shape[0] // 2
-    low, high = value[:half], value[half:]
+    half = ROWS // 2
     is_first = core_ref[0] == 0
-    return jnp.where(is_first, low, high), jnp.where(is_first, high, low)
+    for start in range(0, value.shape[0], ROWS):
+        low, high = value[start : start + half], value[start + half : start + ROWS]
+        yield jnp.where(is_first, low, high), jnp.where(is_first, high, low)
 
 
 def start_copies(a_ref, held_ref, semaphores):
     copies = []
-    for i in range(a_ref.shape[0] // ROWS):
-        rows = pl.ds(i * ROWS, ROWS)
+    for i in range(a_ref.shape[0] // BLOCK):
+        rows = pl.ds(i * BLOCK, BLOCK)
         copies.append(pltpu.make_async_copy(a_ref.at[rows], held_ref.at[rows], semaphores.at[i]))
         copies[i].start()
     return copies
@@ -152,20 +156,24 @@
     wide = jnp.concatenate([s1, s2], axis=1)
     for i, copy in enumerate(copies):
         copy.wait()
-        value = product_wide(held_ref[i * ROWS : (i + 1) * ROWS], wide, s3)
-        keep_ref[i], send_ref[i] = halves(core_ref, value)
+        value = product_wide(held_ref[i * BLOCK : (i + 1) * BLOCK], wide, s3)
+        for k, (keep, send) in enumerate(halves(core_ref, value), i * (BLOCK // ROWS)):
+            keep_ref[k], send_ref[k] = keep, send
 
 
 def back_kernel(core_ref, a_ref, mine_ref, other_ref, out_ref, held_ref, back_ref, gram_ref, semaphores):
     copies = start_copies(a_ref, held_ref, semaphores)
     is_first = core_ref[0] == 0
     for i, copy in enumerate(copies):
-        mine, other = mine_ref[i], other_ref[i]
-        y = jnp.concatenate([jnp.where(is_first, mine, other), jnp.where(is_first, other, mine)], axis=0)
+        pieces = []
+        for k in range(i * (BLOCK // ROWS), (i + 1) * (BLOCK // ROWS)):
+            mine, other = mine_ref[k], other_ref[k]
+            pieces += [jnp.where(is_first, mine, other), jnp.where(is_first, other, mine)]
+        y = jnp.concatenate(pieces, axis=0)
         turned = y.T
         gram = product_tall(turned, y)
         copy.wait()
-        back = product_tall(turned, held_ref[i * ROWS : (i + 1) * ROWS])
+        back = product_tall(turned, held_ref[i * BLOCK : (i + 1) * BLOCK])
         if i == 0:
             back_ref[...], gram_ref[...] = back, gram
         else:
@@ -180,7 +188,7 @@
 
 
 def range_kernel(
-    core_ref, a_ref, both_ref, image_ref, keep_ref, send_ref, gram_ref, first_ref, held_ref, semaphores
+    core_ref, a_ref, both_ref, image_ref, keep_ref, send_ref, gram_ref, first_ref, turn_ref, held_ref, semaphores
 ):
     copies = start_copies(a_ref, held_ref, semaphores)
     n = first_ref.shape[1]
@@ -189,10 +197,25 @@
     cut = both_ref.shape[1] - small
     gram = jnp.concatenate([both_ref[k, cut:, :] for k in range(count)], axis=0)
     back = jnp.concatenate([both_ref[k, :cut, :] for k in range(count)], axis=0)
-    unused, inverse = eliminate(gram)
-    i1, i2, i3 = terms(inverse.T)
+    scale = lax.rsqrt(gram[:1, :1])
+    b1, b2, b3 = terms(back * scale)
+    beside = jnp.concatenate([b1, b2], axis=1)
+    half = ROWS // 2
+
+    def between(panel):
+        if panel == FIRST_PANEL:
+            for copy in copies:
+                copy.wait()
+        k = panel - FIRST_PANEL
+        if 0 <= k < a_ref.shape[0] // ROWS:
+            value = product_wide(held_ref[k * ROWS : (k + 1) * ROWS], beside, b3)
+            ((keep, send),) = halves(core_ref, value)
+            keep_ref[k], send_ref[k * half : (k + 1) * half] = keep, send
+
+    unused, inverse = eliminate(gram, between)
+    turn = inverse.T
+    i1, i2, i3 = terms(turn)
     wide = jnp.concatenate([i1, i2], axis=1)
-    first_ref[...] = product_wide(image_ref[...], wide, i3)
     back = product_wide(back, wide, i3)
     top, diagonal = pack(product(back.T, back))
     edge = top.shape[0]
@@ -201,22 +224,23 @@
     gram_ref[edge:] = diagonal
     send_ref[start : start + edge] = top
     send_ref[start + edge :] = diagonal
-    b1, b2, b3 = terms(back)
-    wide = jnp.concatenate([b1, b2], axis=1)
-    half = ROWS // 2
-    for i, copy in enumerate(copies):
-        copy.wait()
-        value = product_wide(held_ref[i * ROWS : (i + 1) * ROWS], wide, b3)
-        keep_ref[i], send_ref[i * half : (i + 1) * half] = halves(core_ref, value)
-
-
-def last_gram_kernel(parts_ref, range_ref, gram_ref):
+    first_ref[...] = product_wide(image_ref[...], wide, i3)
+    turn_ref[...] = turn * (gram[:1, :1] * scale)
+
+
+def last_gram_kernel(parts_ref, turn_ref, range_ref, gram_ref):
     n = range_ref.shape[0]
     total = parts_ref[0]
     for k in range(1, parts_ref.shape[0]):
         total = total + parts_ref[k]
-    unused, inverse = eliminate(unpack(total[n:]))
-    block = product(total[:n], inverse.T)
+    rows = []
+
+    def between(panel):
+        if panel == 2:
+            rows.append(product(total[:n], turn_ref[...]))
+
+    unused, inverse = eliminate(unpack(total[n:]), between)
+    block = product(rows[0], inverse.T)
     range_ref[...] = block
     gram_ref[...] = product(block.T, block)
 
@@ -239,7 +263,7 @@
         in_specs=[pl.BlockSpec(memory_space=place) for place in places],
         scratch_shapes=[pltpu.VMEM(a.shape, jnp.float32)]
         + scratch
-        + [pltpu.SemaphoreType.DMA((a.shape[0] // ROWS,))],
+        + [pltpu.SemaphoreType.DMA((a.shape[0] // BLOCK,))],
         compiler_params=PARAMS,
         name=name,
     )
@@ -261,15 +285,16 @@
 def range_parts(core, a, both, image_block):
     rows, n = a.shape[0], both.shape[2]
     packed = n // 2 + 8
-    out_shape = [shape(rows // ROWS, ROWS // 2, n), shape(rows // 2 + packed, n), shape(packed, n), shape(n, n)]
+    out_shape = [shape(rows // ROWS, ROWS // 2, n), shape(rows // 2 + packed, n), shape(packed, n)]
+    out_shape += [shape(n, n)] * 2
     return reading(range_kernel, a, [pltpu.VMEM] * 2, out_shape, [], "range_parts")(core, a, both, image_block)
 
 
-def last_gram(parts):
+def last_gram(parts, turn):
     n = parts.shape[2]
     return pl.pallas_call(
         last_gram_kernel, out_shape=[shape(n, n)] * 2, compiler_params=PARAMS, name="last_gram"
-    )(parts)
+    )(parts, turn)
 
 
 def basis(gram, block, tokens):
@@ -304,13 +329,13 @@
     sums = scatter_sum(parts, NEAR)
     sums = jnp.sum(gather(sums, "z_hi"), axis=0)
     both = gather(sums, NEAR)
-    keep, send, gram_part, first_block = range_parts(core, activations, both, image_block)
+    keep, send, gram_part, first_block, turn = range_parts(core, activations, both, image_block)
     received = lax.ppermute(send, "core", SWAP)
     count, rows = keep.shape[:2]
     gram_part = gram_part + received[count * rows :]
     gram_part = jnp.broadcast_to(gram_part[None], (count,) + gram_part.shape)
     parts = jnp.concatenate([keep + received[: count * rows].reshape(keep.shape), gram_part], axis=1)
-    range_block, gram_part = last_gram(lax.all_to_all(parts, PLANE, 0, 0))
+    range_block, gram_part = last_gram(lax.all_to_all(parts, PLANE, 0, 0), turn)
     gram_slice = scatter_sum(gram_part.reshape(lax.axis_size(CROSS), -1, width), CROSS)
     gram_slice = jnp.sum(gather(gram_slice, ("z_hi", "z_lo")), axis=0)
     gram_last = gather(gram_slice, CROSS).reshape(width, width)

time: 191 us -> 187 us (0.979)
  Pallas kernels: 31 us -> 27.4 us
where the time goes in v6:
time: 187 us; the launch traced here: 186 us
  blocking collectives  133 us (71%)
  Pallas kernels  27.4 us (15%)
  starting transfers between devices  20.7 us (11%)
  waiting for transfers between devices  4.42 us (2%)
    all_to_all x5, blocking collectives, gather(): lax.all_to_all(jnp.broadcast_to(block[None], (count,) + block.shape), axi...  76.9 us
    all_to_all x3, blocking collectives, scatter_sum(): return jnp.sum(lax.all_to_all(parts, axis, 0, 0), axis=0)  38.7 us
    all_to_all x1, blocking collectives, per_device(): range_block, gram_part = last_gram(lax.all_to_all(parts, PLANE, 0, 0), turn)  17.1 us
    ppermute x1, starting transfers between devices, per_device(): image_block = scatter_sum(keep + lax.ppermute(send, 'core', SWAP), PLANE)  8.79 us
    pallas_call x1, Pallas kernels, range_parts(): reading(range_kernel, a, [pltpu.VMEM] * 2, out_shape, [], 'range_parts')  8.62 us
    ppermute x1, starting transfers between devices, per_device(): received = lax.ppermute(send, 'core', SWAP)  7.49 us
    pallas_call x1, Pallas kernels, last_gram(): pl.pallas_call(last_gram_kernel, out_shape=[shape(n, n)] * 2, compiler_pa...  5.21 us
    pallas_call x1, Pallas kernels, basis(): pl.pallas_call(lambda *refs: basis_kernel(tokens, *refs), out_shape=[shap...  5.16 us
  transfers between devices with their start and end apart: 3, of which 3 were waited for; matrix products, arithmetic and copies ran while one was open for 0% of the time, Pallas kernels for 0%

profile of v6, /device:TPU:1, one launch (start us, length us, event | category | flops | bytes accessed | tf_op | source)
XLA Modules:
  0.0 186.4 jit_solution(622414184375600901)
XLA Ops:
  0.6 4.2 %image_parts.1 = (f32[8,128,128]{2,1,0:T(8,128)S(1)}, f32[8,128,128]{2,1,0:T(8,128)S(1)}) custom-call(s32[1]{0:T(128)} %bitcast.core_ref, f32[2048,512]{1,0:T(8,128)} %a_ref.5, f32[512,128]{1,0:T(8,128)} %s_ref.1), custom_call_target="tpu_custom_call" | custom-call | tf_op jit(solution)/shard_map/image_parts/pallas_call | solution.py:275
  4.9 8.8 %collective-permute-start = (f32[8,128,128]{2,1,0:T(8,128)S(1)}, f32[8,128,128]{2,1,0:T(8,128)S(1)}, u32[]{:S(2)}, u32[]{:S(2)}) collective-permute-start(f32[8,128,128]{2,1,0:T(8,128)S(1)} %get-tuple-element.15), channel_id=1, source_target_pairs={{0,1},{1,0},{2,3},{3,2},{4,5},{5,4},{6,7},{7,6},{8,9},{9,8},{10,11... | collective-permute-start | bytes 1572872 | tf_op jit(solution)/shard_map/ppermute | solution.py:325
  13.7 1.5 collective-permute-done
  15.2 0.1 add.9
  15.2 13.8 %all_to_all.45 = f32[8,128,128]{2,1,0:T(8,128)S(1)} all-to-all(f32[8,128,128]{2,1,0:T(8,128)S(1)} %add.9), channel_id=1, replica_groups=mesh['x_lo'=2,'z_hi'=4,'z_lo'=4,'y'=4,'x_hi'=2,'core'=2] {'y','x_hi'}, dimensions={0} | all-to-all | bytes 1048576 | tf_op jit(solution)/shard_map/all_to_all | solution.py:311
  29.1 12.5 %all_to_all.46.mine_ref = f32[8,128,128]{2,1,0:T(8,128)S(1)} all-to-all(f32[8,128,128]{2,1,0:T(8,128)S(1)} %broadcast_in_dim.12), channel_id=1, replica_groups=mesh['x_lo'=2,'z_hi'=4,'z_lo'=4,'y'=4,'x_hi'=2,'core'=2] {'y','x_hi'}, dimensions={0} | all-to-all | bytes 1048576 | tf_op jit(solution)/shard_map/all_to_all | solution.py:316
  41.5 4.4 %collective-permute-start.1 = (f32[8,128,128]{2,1,0:T(8,128)S(1)}, f32[8,128,128]{2,1,0:T(8,128)S(1)}, u32[]{:S(2)}, u32[]{:S(2)}) collective-permute-start(f32[8,128,128]{2,1,0:T(8,128)S(1)} %all_to_all.46.mine_ref), channel_id=1, source_target_pairs={{0,1},{1,0},{2,3},{3,2},{4,5},{5,4},{6,7},{7,6},{8,9},{9,8},{10,11... | collective-permute-start | bytes 1572872 | tf_op jit(solution)/shard_map/ppermute | solution.py:327
  45.9 1.5 collective-permute-done.1.other_ref
  47.4 4.2 %back_parts.1 = f32[8,80,128]{2,1,0:T(8,128)S(1)} custom-call(s32[1]{0:T(128)} %bitcast.core_ref, f32[2048,512]{1,0:T(8,128)} %a_ref.5, f32[8,128,128]{2,1,0:T(8,128)S(1)} %all_to_all.46.mine_ref, f32[8,128,128]{2,1,0:T(8,128)S(1)} %collective-permute-done.1.other_ref), custom_call_target="tpu_custom_call" | custom-call | tf_op jit(solution)/shard_map/back_parts/pallas_call | solution.py:282
  51.7 13.4 %all_to_all.47 = f32[8,80,128]{2,1,0:T(8,128)S(1)} all-to-all(f32[8,80,128]{2,1,0:T(8,128)S(1)} %back_parts.1), channel_id=1, replica_groups=mesh['x_lo'=2,'z_hi'=4,'z_lo'=4,'y'=4,'x_hi'=2,'core'=2] {'x_lo','z_lo'}, dimensions={0} | all-to-all | bytes 655360 | tf_op jit(solution)/shard_map/all_to_all | solution.py:311
  65.1 26.6 %all_to_all.48 = f32[4,80,128]{2,1,0:T(8,128)S(1)} all-to-all(f32[4,80,128]{2,1,0:T(8,128)S(1)} %broadcast_in_dim.13), channel_id=1, replica_groups=mesh['x_lo'=2,'z_hi'=4,'z_lo'=4,'y'=4,'x_hi'=2,'core'=2] {'z_hi'}, dimensions={0} | all-to-all | bytes 327680 | tf_op jit(solution)/shard_map/all_to_all | solution.py:316
  91.8 10.4 %all_to_all.49.both_ref = f32[8,80,128]{2,1,0:T(8,128)S(1)} all-to-all(f32[8,80,128]{2,1,0:T(8,128)S(1)} %broadcast_in_dim.14), channel_id=1, replica_groups=mesh['x_lo'=2,'z_hi'=4,'z_lo'=4,'y'=4,'x_hi'=2,'core'=2] {'x_lo','z_lo'}, dimensions={0} | all-to-all | bytes 655360 | tf_op jit(solution)/shard_map/all_to_all | solution.py:316
  102.2 8.6 %range_parts.1 = (f32[8,128,128]{2,1,0:T(8,128)S(1)}, f32[1096,128]{1,0:T(8,128)S(1)}, f32[72,128]{1,0:T(8,128)S(1)}, f32[128,128]{1,0:T(8,128)}, f32[128,128]{1,0:T(8,128)S(1)}) custom-call(s32[1]{0:T(128)} %bitcast.core_ref, f32[2048,512]{1,0:T(8,128)} %a_ref.5, f32[8,80,128]{2,1,0:T(8,128)S(1)} %all_to_all.49.both_ref, f32[128,128]{1,0:T(8,128)S(1)} %reduce_sum.45.image_ref), custom_call_target="tpu_custom_call" | custom-call | tf_op jit(solution)/shard_map/range_parts/pallas_call | solution.py:290
  110.8 7.5 %collective-permute-start.2 = (f32[1096,128]{1,0:T(8,128)S(1)}, f32[1096,128]{1,0:T(8,128)S(1)}, u32[]{:S(2)}, u32[]{:S(2)}) collective-permute-start(f32[1096,128]{1,0:T(8,128)S(1)} %get-tuple-element.18), channel_id=1, source_target_pairs={{0,1},{1,0},{2,3},{3,2},{4,5},{5,4},{6,7},{7,6},{8,9},{9,8},{10,11... | collective-permute-start | bytes 1683464 | tf_op jit(solution)/shard_map/ppermute | solution.py:333
  118.3 1.4 collective-permute-done.2
  119.7 0.1 add.10
  119.8 0.1 pad_maximum_fusion
  119.9 17.1 %all_to_all.50.parts_ref = f32[8,200,128]{2,1,0:T(8,128)S(1)} all-to-all(f32[8,200,128]{2,1,0:T(8,128)S(1)} %pad_maximum_fusion), channel_id=1, replica_groups=mesh['x_lo'=2,'z_hi'=4,'z_lo'=4,'y'=4,'x_hi'=2,'core'=2] {'y','x_hi'}, dimensions={0} | all-to-all | bytes 1638400 | tf_op jit(solution)/shard_map/all_to_all | solution.py:338
  137.0 5.2 %last_gram.1 = (f32[128,128]{1,0:T(8,128)S(1)}, f32[128,128]{1,0:T(8,128)S(1)}) custom-call(f32[8,200,128]{2,1,0:T(8,128)S(1)} %all_to_all.50.parts_ref, f32[128,128]{1,0:T(8,128)S(1)} %get-tuple-element.20.turn_ref), custom_call_target="tpu_custom_call" | custom-call | tf_op jit(solution)/shard_map/last_gram/pallas_call | solution.py:295
  142.2 11.5 %all_to_all.51 = f32[32,4,128]{2,1,0:T(4,128)S(1)} all-to-all(f32[32,4,128]{2,1,0:T(4,128)S(1)} %bitcast.5), channel_id=1, replica_groups=mesh['x_lo'=2,'z_hi'=4,'z_lo'=4,'y'=4,'x_hi'=2,'core'=2] {'x_lo','y','x_..., dimensions={0} | all-to-all | bytes 131072 | tf_op jit(solution)/shard_map/all_to_all | solution.py:311
  153.8 15.1 %all_to_all.52 = f32[16,4,128]{2,1,0:T(4,128)S(1)} all-to-all(f32[16,4,128]{2,1,0:T(4,128)S(1)} %broadcast_in_dim.16), channel_id=1, replica_groups=mesh['x_lo'=2,'z_hi'=4,'z_lo'=4,'y'=4,'x_hi'=2,'core'=2] {'z_hi','z_lo'}, dimensions={0} | all-to-all | bytes 65536 | tf_op jit(solution)/shard_map/all_to_all | solution.py:316
  169.0 12.3 %all_to_all.53 = f32[32,4,128]{2,1,0:T(4,128)S(1)} all-to-all(f32[32,4,128]{2,1,0:T(4,128)S(1)} %broadcast_in_dim.17), channel_id=1, replica_groups=mesh['x_lo'=2,'z_hi'=4,'z_lo'=4,'y'=4,'x_hi'=2,'core'=2] {'x_lo','y','x_..., dimensions={0} | all-to-all | bytes 131072 | tf_op jit(solution)/shard_map/all_to_all | solution.py:316
  181.3 5.2 %basis.1 = (f32[128,128]{1,0:T(8,128)}, f32[128,128]{1,0:T(8,128)}) custom-call(f32[128,128]{1,0:T(8,128)S(1)} %bitcast.4, f32[128,128]{1,0:T(8,128)S(1)} %get-tuple-element.22.refs_1_), custom_call_target="tpu_custom_call" | custom-call | tf_op jit(solution)/shard_map/basis/pallas_call | solution.py:302
  (13 shorter events, 0.3 us)
Async XLA Ops:
  4.9 10.3 %collective-permute-start = (f32[8,128,128]{2,1,0:T(8,128)S(1)}, f32[8,128,128]{2,1,0:T(8,128)S(1)}, u32[]{:S(2)}, u32[]{:S(2)}) collective-permute-start(f32[8,128,128]{2,1,0:T(8,128)S(1)} %get-tuple-element.15), channel_id=1, source_target_pairs={{0,1},{1,0},{2,3},{3,2},{4,5},{5,4},{6,7},{7,6},{8,9},{9,8},{10,11... | collective-permute-start | bytes 1572872 | tf_op jit(solution)/shard_map/ppermute | solution.py:325
  41.5 5.9 %collective-permute-start.1 = (f32[8,128,128]{2,1,0:T(8,128)S(1)}, f32[8,128,128]{2,1,0:T(8,128)S(1)}, u32[]{:S(2)}, u32[]{:S(2)}) collective-permute-start(f32[8,128,128]{2,1,0:T(8,128)S(1)} %all_to_all.46.mine_ref), channel_id=1, source_target_pairs={{0,1},{1,0},{2,3},{3,2},{4,5},{5,4},{6,7},{7,6},{8,9},{9,8},{10,11... | collective-permute-start | bytes 1572872 | tf_op jit(solution)/shard_map/ppermute | solution.py:327
  110.8 8.9 %collective-permute-start.2 = (f32[1096,128]{1,0:T(8,128)S(1)}, f32[1096,128]{1,0:T(8,128)S(1)}, u32[]{:S(2)}, u32[]{:S(2)}) collective-permute-start(f32[1096,128]{1,0:T(8,128)S(1)} %get-tuple-element.18), channel_id=1, source_target_pairs={{0,1},{1,0},{2,3},{3,2},{4,5},{5,4},{6,7},{7,6},{8,9},{9,8},{10,11... | collective-permute-start | bytes 1683464 | tf_op jit(solution)/shard_map/ppermute | solution.py:333

commit v7 on v6

--- a/solution.py
+++ b/solution.py
@@ -60,7 +60,7 @@
     return values[0]
 
 
-def eliminate(gram, between=lambda panel: None):
+def eliminate(gram, left_ref, right_ref, between=lambda panel: None):
     n = gram.shape[0]
     count = n // 8
     tile = (8, n)
@@ -68,10 +68,11 @@
     lane = lax.broadcasted_iota(jnp.int32, tile, 1)
     left = [gram[8 * u : 8 * u + 8, :] for u in range(count)]
     right = [jnp.where(lane == row + 8 * u, 1.0, 0.0).astype(jnp.float32) for u in range(count)]
+    left_ref[:8], right_ref[:8] = left[0], right[0]
     for v in range(count):
         start = 8 * v
-        rows = [jnp.broadcast_to(left[v][i : i + 1, :], tile) for i in range(PANEL)]
-        more = [jnp.broadcast_to(right[v][i : i + 1, :], tile) for i in range(PANEL)]
+        rows = [left_ref[pl.ds(start + i, 8, stride=0), :] for i in range(PANEL)]
+        more = [right_ref[pl.ds(start + i, 8, stride=0), :] for i in range(PANEL)]
         corner = [
             [jnp.broadcast_to(rows[i][:, start + m : start + m + 1], tile) for m in range(PANEL)]
             for i in range(PANEL)
@@ -85,17 +86,21 @@
                     corner[m][q] = corner[m][q] - weight * corner[i][q]
                 rows[m] = rows[m] - weight * rows[i]
                 more[m] = more[m] - weight * more[i]
-        for u in range(v, count):
+        for u in range(v + 1, count):
             factors = []
             for i in range(PANEL):
                 column = jnp.broadcast_to(left[u][:, start + i : start + i + 1], tile)
                 for m in range(i):
                     column = column - factors[m] * corner[m][i]
                 factors.append(column * scales[i])
-            if u == v:
-                factors = [jnp.where(row > i, factors[i], 0.0) for i in range(PANEL)]
             left[u] = left[u] - tree([f * r for f, r in zip(factors, rows)])
             right[u] = right[u] - tree([f * r for f, r in zip(factors, more)])
+            if u == v + 1:
+                left_ref[8 * u : 8 * u + 8], right_ref[8 * u : 8 * u + 8] = left[u], right[u]
+        left[v], right[v] = rows[-1], more[-1]
+        for i in range(PANEL - 1):
+            left[v] = jnp.where(row == i, rows[i], left[v])
+            right[v] = jnp.where(row == i, more[i], right[v])
         between(v)
     upper, inverse = [], []
     for u in range(count):
@@ -188,7 +193,19 @@
 
 
 def range_kernel(
-    core_ref, a_ref, both_ref, image_ref, keep_ref, send_ref, gram_ref, first_ref, turn_ref, held_ref, semaphores
+    core_ref,
+    a_ref,
+    both_ref,
+    image_ref,
+    keep_ref,
+    send_ref,
+    gram_ref,
+    first_ref,
+    turn_ref,
+    held_ref,
+    left_ref,
+    right_ref,
+    semaphores,
 ):
     copies = start_copies(a_ref, held_ref, semaphores)
     n = first_ref.shape[1]
@@ -212,7 +229,7 @@
             ((keep, send),) = halves(core_ref, value)
             keep_ref[k], send_ref[k * half : (k + 1) * half] = keep, send
 
-    unused, inverse = eliminate(gram, between)
+    unused, inverse = eliminate(gram, left_ref, right_ref, between)
     turn = inverse.T
     i1, i2, i3 = terms(turn)
     wide = jnp.concatenate([i1, i2], axis=1)
@@ -228,7 +245,7 @@
     turn_ref[...] = turn * (gram[:1, :1] * scale)
 
 
-def last_gram_kernel(parts_ref, turn_ref, range_ref, gram_ref):
+def last_gram_kernel(parts_ref, turn_ref, range_ref, gram_ref, left_ref, right_ref):
     n = range_ref.shape[0]
     total = parts_ref[0]
     for k in range(1, parts_ref.shape[0]):
@@ -239,16 +256,20 @@
         if panel == 2:
             rows.append(product(total[:n], turn_ref[...]))
 
-    unused, inverse = eliminate(unpack(total[n:]), between)
+    unused, inverse = eliminate(unpack(total[n:]), left_ref, right_ref, between)
     block = product(rows[0], inverse.T)
     range_ref[...] = block
     gram_ref[...] = product(block.T, block)
 
 
-def basis_kernel(tokens, gram_ref, range_ref, basis_ref, triangle_ref):
-    upper, inverse = eliminate(gram_ref[...])
+def basis_kernel(tokens, gram_ref, range_ref, basis_ref, triangle_ref, left_ref, right_ref):
+    upper, inverse = eliminate(gram_ref[...], left_ref, right_ref)
     basis_ref[...] = product(range_ref[...], inverse.T)
     triangle_ref[...] = upper.T / jnp.sqrt(jnp.float32(tokens))
+
+
+def spread(n):
+    return [pltpu.VMEM((n + 8, n), jnp.float32)] * 2
 
 
 def shape(*sizes):
@@ -287,13 +308,17 @@
     packed = n // 2 + 8
     out_shape = [shape(rows // ROWS, ROWS // 2, n), shape(rows // 2 + packed, n), shape(packed, n)]
     out_shape += [shape(n, n)] * 2
-    return reading(range_kernel, a, [pltpu.VMEM] * 2, out_shape, [], "range_parts")(core, a, both, image_block)
+    return reading(range_kernel, a, [pltpu.VMEM] * 2, out_shape, spread(n), "range_parts")(core, a, both, image_block)
 
 
 def last_gram(parts, turn):
     n = parts.shape[2]
     return pl.pallas_call(
-        last_gram_kernel, out_shape=[shape(n, n)] * 2, compiler_params=PARAMS, name="last_gram"
+        last_gram_kernel,
+        out_shape=[shape(n, n)] * 2,
+        scratch_shapes=spread(n),
+        compiler_params=PARAMS,
+        name="last_gram",
     )(parts, turn)
 
 
@@ -302,6 +327,7 @@
     return pl.pallas_call(
         lambda *refs: basis_kernel(tokens, *refs),
         out_shape=[shape(n, n)] * 2,
+        scratch_shapes=spread(n),
         compiler_params=PARAMS,
         name="basis",
     )(gram, block)

time: 187 us -> 183 us (0.979)
  Pallas kernels: 27.4 us -> 23.9 us
    pallas_call x2, Pallas kernels: 13.8 us -> 11.2 us  [the longest x1 6.61 us: range_parts(): reading(range_kernel, a, [pltpu.VMEM] * 2, out_shape, spread(n), 'range_p...]
where the time goes in v7:
time: 183 us
  blocking collectives  133 us (73%)
  Pallas kernels  23.9 us (13%)
  starting transfers between devices  20.7 us (11%)
  waiting for transfers between devices  4.42 us (2%)
    all_to_all x5, blocking collectives, gather(): lax.all_to_all(jnp.broadcast_to(block[None], (count,) + block.shape), axi...  76.9 us
    all_to_all x3, blocking collectives, scatter_sum(): return jnp.sum(lax.all_to_all(parts, axis, 0, 0), axis=0)  38.7 us
    all_to_all x1, blocking collectives, per_device(): range_block, gram_part = last_gram(lax.all_to_all(parts, PLANE, 0, 0), turn)  17.1 us
    ppermute x1, starting transfers between devices, per_device(): image_block = scatter_sum(keep + lax.ppermute(send, 'core', SWAP), PLANE)  8.79 us
    ppermute x1, starting transfers between devices, per_device(): received = lax.ppermute(send, 'core', SWAP)  7.49 us
    pallas_call x1, Pallas kernels, range_parts(): reading(range_kernel, a, [pltpu.VMEM] * 2, out_shape, spread(n), 'range_p...  6.61 us
    pallas_call x1, Pallas kernels, last_gram(): pl.pallas_call(last_gram_kernel, out_shape=[shape(n, n)] * 2, scratch_sha...  4.58 us
    ppermute x1, starting transfers between devices, per_device(): other = lax.ppermute(mine, 'core', SWAP)  4.39 us
  transfers between devices with their start and end apart: 3, of which 3 were waited for; matrix products, arithmetic and copies ran while one was open for 0% of the time, Pallas kernels for 0%

profile of v7, /device:TPU:1, one launch (start us, length us, event | category | flops | bytes accessed | tf_op | source)
XLA Modules:
  0.0 183.0 jit_solution(3209710240483992639)
XLA Ops:
  0.6 4.2 %image_parts.1 = (f32[8,128,128]{2,1,0:T(8,128)S(1)}, f32[8,128,128]{2,1,0:T(8,128)S(1)}) custom-call(s32[1]{0:T(128)} %bitcast.core_ref, f32[2048,512]{1,0:T(8,128)} %a_ref.5, f32[512,128]{1,0:T(8,128)} %s_ref.1), custom_call_target="tpu_custom_call" | custom-call | tf_op jit(solution)/shard_map/image_parts/pallas_call | solution.py:296
  4.9 8.8 %collective-permute-start = (f32[8,128,128]{2,1,0:T(8,128)S(1)}, f32[8,128,128]{2,1,0:T(8,128)S(1)}, u32[]{:S(2)}, u32[]{:S(2)}) collective-permute-start(f32[8,128,128]{2,1,0:T(8,128)S(1)} %get-tuple-element.15), channel_id=1, source_target_pairs={{0,1},{1,0},{2,3},{3,2},{4,5},{5,4},{6,7},{7,6},{8,9},{9,8},{10,11... | collective-permute-start | bytes 1572872 | tf_op jit(solution)/shard_map/ppermute | solution.py:351
  13.7 1.5 collective-permute-done
  15.2 0.1 add.9
  15.2 13.8 %all_to_all.45 = f32[8,128,128]{2,1,0:T(8,128)S(1)} all-to-all(f32[8,128,128]{2,1,0:T(8,128)S(1)} %add.9), channel_id=1, replica_groups=mesh['x_lo'=2,'z_hi'=4,'z_lo'=4,'y'=4,'x_hi'=2,'core'=2] {'y','x_hi'}, dimensions={0} | all-to-all | bytes 1048576 | tf_op jit(solution)/shard_map/all_to_all | solution.py:337
  29.1 12.5 %all_to_all.46.mine_ref = f32[8,128,128]{2,1,0:T(8,128)S(1)} all-to-all(f32[8,128,128]{2,1,0:T(8,128)S(1)} %broadcast_in_dim.12), channel_id=1, replica_groups=mesh['x_lo'=2,'z_hi'=4,'z_lo'=4,'y'=4,'x_hi'=2,'core'=2] {'y','x_hi'}, dimensions={0} | all-to-all | bytes 1048576 | tf_op jit(solution)/shard_map/all_to_all | solution.py:342
  41.5 4.4 %collective-permute-start.1 = (f32[8,128,128]{2,1,0:T(8,128)S(1)}, f32[8,128,128]{2,1,0:T(8,128)S(1)}, u32[]{:S(2)}, u32[]{:S(2)}) collective-permute-start(f32[8,128,128]{2,1,0:T(8,128)S(1)} %all_to_all.46.mine_ref), channel_id=1, source_target_pairs={{0,1},{1,0},{2,3},{3,2},{4,5},{5,4},{6,7},{7,6},{8,9},{9,8},{10,11... | collective-permute-start | bytes 1572872 | tf_op jit(solution)/shard_map/ppermute | solution.py:353
  45.9 1.5 collective-permute-done.1.other_ref
  47.4 4.2 %back_parts.1 = f32[8,80,128]{2,1,0:T(8,128)S(1)} custom-call(s32[1]{0:T(128)} %bitcast.core_ref, f32[2048,512]{1,0:T(8,128)} %a_ref.5, f32[8,128,128]{2,1,0:T(8,128)S(1)} %all_to_all.46.mine_ref, f32[8,128,128]{2,1,0:T(8,128)S(1)} %collective-permute-done.1.other_ref), custom_call_target="tpu_custom_call" | custom-call | tf_op jit(solution)/shard_map/back_parts/pallas_call | solution.py:303
  51.7 13.4 %all_to_all.47 = f32[8,80,128]{2,1,0:T(8,128)S(1)} all-to-all(f32[8,80,128]{2,1,0:T(8,128)S(1)} %back_parts.1), channel_id=1, replica_groups=mesh['x_lo'=2,'z_hi'=4,'z_lo'=4,'y'=4,'x_hi'=2,'core'=2] {'x_lo','z_lo'}, dimensions={0} | all-to-all | bytes 655360 | tf_op jit(solution)/shard_map/all_to_all | solution.py:337
  65.1 26.6 %all_to_all.48 = f32[4,80,128]{2,1,0:T(8,128)S(1)} all-to-all(f32[4,80,128]{2,1,0:T(8,128)S(1)} %broadcast_in_dim.13), channel_id=1, replica_groups=mesh['x_lo'=2,'z_hi'=4,'z_lo'=4,'y'=4,'x_hi'=2,'core'=2] {'z_hi'}, dimensions={0} | all-to-all | bytes 327680 | tf_op jit(solution)/shard_map/all_to_all | solution.py:342
  91.8 10.4 %all_to_all.49.both_ref = f32[8,80,128]{2,1,0:T(8,128)S(1)} all-to-all(f32[8,80,128]{2,1,0:T(8,128)S(1)} %broadcast_in_dim.14), channel_id=1, replica_groups=mesh['x_lo'=2,'z_hi'=4,'z_lo'=4,'y'=4,'x_hi'=2,'core'=2] {'x_lo','z_lo'}, dimensions={0} | all-to-all | bytes 655360 | tf_op jit(solution)/shard_map/all_to_all | solution.py:342
  102.2 6.6 %range_parts.1 = (f32[8,128,128]{2,1,0:T(8,128)S(1)}, f32[1096,128]{1,0:T(8,128)S(1)}, f32[72,128]{1,0:T(8,128)S(1)}, f32[128,128]{1,0:T(8,128)}, f32[128,128]{1,0:T(8,128)S(1)}) custom-call(s32[1]{0:T(128)} %bitcast.core_ref, f32[2048,512]{1,0:T(8,128)} %a_ref.5, f32[8,80,128]{2,1,0:T(8,128)S(1)} %all_to_all.49.both_ref, f32[128,128]{1,0:T(8,128)S(1)} %reduce_sum.45.image_ref), custom_call_target="tpu_custom_call" | custom-call | tf_op jit(solution)/shard_map/range_parts/pallas_call | solution.py:311
  108.8 7.5 %collective-permute-start.2 = (f32[1096,128]{1,0:T(8,128)S(1)}, f32[1096,128]{1,0:T(8,128)S(1)}, u32[]{:S(2)}, u32[]{:S(2)}) collective-permute-start(f32[1096,128]{1,0:T(8,128)S(1)} %get-tuple-element.18), channel_id=1, source_target_pairs={{0,1},{1,0},{2,3},{3,2},{4,5},{5,4},{6,7},{7,6},{8,9},{9,8},{10,11... | collective-permute-start | bytes 1683464 | tf_op jit(solution)/shard_map/ppermute | solution.py:359
  116.3 1.4 collective-permute-done.2
  117.7 0.1 add.10
  117.8 0.1 pad_maximum_fusion
  117.9 17.1 %all_to_all.50.parts_ref = f32[8,200,128]{2,1,0:T(8,128)S(1)} all-to-all(f32[8,200,128]{2,1,0:T(8,128)S(1)} %pad_maximum_fusion), channel_id=1, replica_groups=mesh['x_lo'=2,'z_hi'=4,'z_lo'=4,'y'=4,'x_hi'=2,'core'=2] {'y','x_hi'}, dimensions={0} | all-to-all | bytes 1638400 | tf_op jit(solution)/shard_map/all_to_all | solution.py:364
  135.0 4.6 %last_gram.1 = (f32[128,128]{1,0:T(8,128)S(1)}, f32[128,128]{1,0:T(8,128)S(1)}) custom-call(f32[8,200,128]{2,1,0:T(8,128)S(1)} %all_to_all.50.parts_ref, f32[128,128]{1,0:T(8,128)S(1)} %get-tuple-element.20.turn_ref), custom_call_target="tpu_custom_call" | custom-call | tf_op jit(solution)/shard_map/last_gram/pallas_call | solution.py:316
  139.6 11.5 %all_to_all.51 = f32[32,4,128]{2,1,0:T(4,128)S(1)} all-to-all(f32[32,4,128]{2,1,0:T(4,128)S(1)} %bitcast.5), channel_id=1, replica_groups=mesh['x_lo'=2,'z_hi'=4,'z_lo'=4,'y'=4,'x_hi'=2,'core'=2] {'x_lo','y','x_..., dimensions={0} | all-to-all | bytes 131072 | tf_op jit(solution)/shard_map/all_to_all | solution.py:337
  151.2 15.1 %all_to_all.52 = f32[16,4,128]{2,1,0:T(4,128)S(1)} all-to-all(f32[16,4,128]{2,1,0:T(4,128)S(1)} %broadcast_in_dim.16), channel_id=1, replica_groups=mesh['x_lo'=2,'z_hi'=4,'z_lo'=4,'y'=4,'x_hi'=2,'core'=2] {'z_hi','z_lo'}, dimensions={0} | all-to-all | bytes 65536 | tf_op jit(solution)/shard_map/all_to_all | solution.py:342
  166.3 12.3 %all_to_all.53 = f32[32,4,128]{2,1,0:T(4,128)S(1)} all-to-all(f32[32,4,128]{2,1,0:T(4,128)S(1)} %broadcast_in_dim.17), channel_id=1, replica_groups=mesh['x_lo'=2,'z_hi'=4,'z_lo'=4,'y'=4,'x_hi'=2,'core'=2] {'x_lo','y','x_..., dimensions={0} | all-to-all | bytes 131072 | tf_op jit(solution)/shard_map/all_to_all | solution.py:342
  178.6 4.3 %basis.1 = (f32[128,128]{1,0:T(8,128)}, f32[128,128]{1,0:T(8,128)}) custom-call(f32[128,128]{1,0:T(8,128)S(1)} %bitcast.4, f32[128,128]{1,0:T(8,128)S(1)} %get-tuple-element.22.refs_1_), custom_call_target="tpu_custom_call" | custom-call | tf_op jit(solution)/shard_map/basis/pallas_call | solution.py:327
  (13 shorter events, 0.3 us)
Async XLA Ops:
  4.9 10.3 %collective-permute-start = (f32[8,128,128]{2,1,0:T(8,128)S(1)}, f32[8,128,128]{2,1,0:T(8,128)S(1)}, u32[]{:S(2)}, u32[]{:S(2)}) collective-permute-start(f32[8,128,128]{2,1,0:T(8,128)S(1)} %get-tuple-element.15), channel_id=1, source_target_pairs={{0,1},{1,0},{2,3},{3,2},{4,5},{5,4},{6,7},{7,6},{8,9},{9,8},{10,11... | collective-permute-start | bytes 1572872 | tf_op jit(solution)/shard_map/ppermute | solution.py:351
  41.5 5.9 %collective-permute-start.1 = (f32[8,128,128]{2,1,0:T(8,128)S(1)}, f32[8,128,128]{2,1,0:T(8,128)S(1)}, u32[]{:S(2)}, u32[]{:S(2)}) collective-permute-start(f32[8,128,128]{2,1,0:T(8,128)S(1)} %all_to_all.46.mine_ref), channel_id=1, source_target_pairs={{0,1},{1,0},{2,3},{3,2},{4,5},{5,4},{6,7},{7,6},{8,9},{9,8},{10,11... | collective-permute-start | bytes 1572872 | tf_op jit(solution)/shard_map/ppermute | solution.py:353
  108.8 8.9 %collective-permute-start.2 = (f32[1096,128]{1,0:T(8,128)S(1)}, f32[1096,128]{1,0:T(8,128)S(1)}, u32[]{:S(2)}, u32[]{:S(2)}) collective-permute-start(f32[1096,128]{1,0:T(8,128)S(1)} %get-tuple-element.18), channel_id=1, source_target_pairs={{0,1},{1,0},{2,3},{3,2},{4,5},{5,4},{6,7},{7,6},{8,9},{9,8},{10,11... | collective-permute-start | bytes 1683464 | tf_op jit(solution)/shard_map/ppermute | solution.py:359

commit v8 on v7

--- a/solution.py
+++ b/solution.py
@@ -9,7 +9,7 @@
 SWAP = [(0, 1), (1, 0)]
 ROWS = 256
 BLOCK = 1024
-FIRST_PANEL = 5
+FIRST_PANEL = 8
 PLANE = ("y", "x_hi")
 NEAR = ("x_lo", "z_lo")
 CROSS = ("x_lo", "y", "x_hi", "core")
@@ -61,6 +61,7 @@
 
 
 def eliminate(gram, left_ref, right_ref, between=lambda panel: None):
+    corner_ref = left_ref.at[pl.ds(gram.shape[0] + 8, 72)]
     n = gram.shape[0]
     count = n // 8
     tile = (8, n)
@@ -73,10 +74,9 @@
         start = 8 * v
         rows = [left_ref[pl.ds(start + i, 8, stride=0), :] for i in range(PANEL)]
         more = [right_ref[pl.ds(start + i, 8, stride=0), :] for i in range(PANEL)]
-        corner = [
-            [jnp.broadcast_to(rows[i][:, start + m : start + m + 1], tile) for m in range(PANEL)]
-            for i in range(PANEL)
-        ]
+        for m in range(PANEL):
+            corner_ref[8 * m : 8 * m + 8] = jnp.broadcast_to(left[v][:, start + m : start + m + 1], tile)
+        corner = [[corner_ref[pl.ds(8 * m + i, 8, stride=0), :] for m in range(PANEL)] for i in range(PANEL)]
         scales = []
         for i in range(PANEL):
             scales.append(1.0 / corner[i][i])
@@ -196,11 +196,9 @@
     core_ref,
     a_ref,
     both_ref,
-    image_ref,
     keep_ref,
     send_ref,
     gram_ref,
-    first_ref,
     turn_ref,
     held_ref,
     left_ref,
@@ -208,7 +206,7 @@
     semaphores,
 ):
     copies = start_copies(a_ref, held_ref, semaphores)
-    n = first_ref.shape[1]
+    n = both_ref.shape[2]
     count = both_ref.shape[0]
     small = n // count
     cut = both_ref.shape[1] - small
@@ -241,11 +239,10 @@
     gram_ref[edge:] = diagonal
     send_ref[start : start + edge] = top
     send_ref[start + edge :] = diagonal
-    first_ref[...] = product_wide(image_ref[...], wide, i3)
-    turn_ref[...] = turn * (gram[:1, :1] * scale)
-
-
-def last_gram_kernel(parts_ref, turn_ref, range_ref, gram_ref, left_ref, right_ref):
+    turn_ref[0], turn_ref[1] = turn, turn * (gram[:1, :1] * scale)
+
+
+def last_gram_kernel(parts_ref, turn_ref, image_ref, range_ref, gram_ref, first_ref, left_ref, right_ref):
     n = range_ref.shape[0]
     total = parts_ref[0]
     for k in range(1, parts_ref.shape[0]):
@@ -254,7 +251,9 @@
 
     def between(panel):
         if panel == 2:
-            rows.append(product(total[:n], turn_ref[...]))
+            rows.append(product(total[:n], turn_ref[1]))
+        if panel == 4:
+            first_ref[...] = product(image_ref[...], turn_ref[0])
 
     unused, inverse = eliminate(unpack(total[n:]), left_ref, right_ref, between)
     block = product(rows[0], inverse.T)
@@ -269,7 +268,7 @@
 
 
 def spread(n):
-    return [pltpu.VMEM((n + 8, n), jnp.float32)] * 2
+    return [pltpu.VMEM((n + 80, n), jnp.float32), pltpu.VMEM((n + 8, n), jnp.float32)]
 
 
 def shape(*sizes):
@@ -303,23 +302,23 @@
     return reading(back_kernel, a, [pltpu.VMEM] * 2, out_shape, scratch, "back_parts")(core, a, mine, other)
 
 
-def range_parts(core, a, both, image_block):
+def range_parts(core, a, both):
     rows, n = a.shape[0], both.shape[2]
     packed = n // 2 + 8
     out_shape = [shape(rows // ROWS, ROWS // 2, n), shape(rows // 2 + packed, n), shape(packed, n)]
-    out_shape += [shape(n, n)] * 2
-    return reading(range_kernel, a, [pltpu.VMEM] * 2, out_shape, spread(n), "range_parts")(core, a, both, image_block)
-
-
-def last_gram(parts, turn):
+    out_shape += [shape(2, n, n)]
+    return reading(range_kernel, a, [pltpu.VMEM], out_shape, spread(n), "range_parts")(core, a, both)
+
+
+def last_gram(parts, turn, image_block):
     n = parts.shape[2]
     return pl.pallas_call(
         last_gram_kernel,
-        out_shape=[shape(n, n)] * 2,
+        out_shape=[shape(n, n)] * 3,
         scratch_shapes=spread(n),
         compiler_params=PARAMS,
         name="last_gram",
-    )(parts, turn)
+    )(parts, turn, image_block)
 
 
 def basis(gram, block, tokens):
@@ -355,13 +354,14 @@
     sums = scatter_sum(parts, NEAR)
     sums = jnp.sum(gather(sums, "z_hi"), axis=0)
     both = gather(sums, NEAR)
-    keep, send, gram_part, first_block, turn = range_parts(core, activations, both, image_block)
+    keep, send, gram_part, turn = range_parts(core, activations, both)
     received = lax.ppermute(send, "core", SWAP)
     count, rows = keep.shape[:2]
     gram_part = gram_part + received[count * rows :]
     gram_part = jnp.broadcast_to(gram_part[None], (count,) + gram_part.shape)
     parts = jnp.concatenate([keep + received[: count * rows].reshape(keep.shape), gram_part], axis=1)
-    range_block, gram_part = last_gram(lax.all_to_all(parts, PLANE, 0, 0), turn)
+    parts = lax.all_to_all(parts, PLANE, 0, 0)
+    range_block, gram_part, first_block = last_gram(parts, turn, image_block)
     gram_slice = scatter_sum(gram_part.reshape(lax.axis_size(CROSS), -1, width), CROSS)
     gram_slice = jnp.sum(gather(gram_slice, ("z_hi", "z_lo")), axis=0)
     gram_last = gather(gram_slice, CROSS).reshape(width, width)

time: 183 us -> 183 us (level)
  no operation moved by 1% of the time
where the time goes in v8:
time: 183 us; the launch traced here: 182 us
  blocking collectives  133 us (73%)
  Pallas kernels  23.1 us (13%)
  starting transfers between devices  20.5 us (11%)
  waiting for transfers between devices  4.6 us (3%)
    all_to_all x5, blocking collectives, gather(): lax.all_to_all(jnp.broadcast_to(block[None], (count,) + block.shape), axi...  76.9 us
    all_to_all x3, blocking collectives, scatter_sum(): return jnp.sum(lax.all_to_all(parts, axis, 0, 0), axis=0)  38.7 us
    all_to_all x1, blocking collectives, per_device(): parts = lax.all_to_all(parts, PLANE, 0, 0)  17.3 us
    ppermute x1, starting transfers between devices, per_device(): image_block = scatter_sum(keep + lax.ppermute(send, 'core', SWAP), PLANE)  8.79 us
    ppermute x1, starting transfers between devices, per_device(): received = lax.ppermute(send, 'core', SWAP)  7.31 us
    pallas_call x1, Pallas kernels, range_parts(): reading(range_kernel, a, [pltpu.VMEM], out_shape, spread(n), 'range_parts')  5.69 us
    pallas_call x1, Pallas kernels, last_gram(): pl.pallas_call(last_gram_kernel, out_shape=[shape(n, n)] * 3, scratch_sha...  4.63 us
    ppermute x1, starting transfers between devices, per_device(): other = lax.ppermute(mine, 'core', SWAP)  4.39 us
  transfers between devices with their start and end apart: 3, of which 3 were waited for; matrix products, arithmetic and copies ran while one was open for 0% of the time, Pallas kernels for 0%

profile of v8, /device:TPU:1, one launch (start us, length us, event | category | flops | bytes accessed | tf_op | source)
XLA Modules:
  0.0 182.3 jit_solution(16927613410431571504)
XLA Ops:
  0.6 4.2 %image_parts.1 = (f32[8,128,128]{2,1,0:T(8,128)S(1)}, f32[8,128,128]{2,1,0:T(8,128)S(1)}) custom-call(s32[1]{0:T(128)} %bitcast.core_ref, f32[2048,512]{1,0:T(8,128)} %a_ref.5, f32[512,128]{1,0:T(8,128)} %s_ref.1), custom_call_target="tpu_custom_call" | custom-call | tf_op jit(solution)/shard_map/image_parts/pallas_call | solution.py:295
  4.9 8.8 %collective-permute-start = (f32[8,128,128]{2,1,0:T(8,128)S(1)}, f32[8,128,128]{2,1,0:T(8,128)S(1)}, u32[]{:S(2)}, u32[]{:S(2)}) collective-permute-start(f32[8,128,128]{2,1,0:T(8,128)S(1)} %get-tuple-element.15), channel_id=1, source_target_pairs={{0,1},{1,0},{2,3},{3,2},{4,5},{5,4},{6,7},{7,6},{8,9},{9,8},{10,11... | collective-permute-start | bytes 1572872 | tf_op jit(solution)/shard_map/ppermute | solution.py:350
  13.7 1.5 collective-permute-done
  15.2 0.1 add.9
  15.2 13.8 %all_to_all.45 = f32[8,128,128]{2,1,0:T(8,128)S(1)} all-to-all(f32[8,128,128]{2,1,0:T(8,128)S(1)} %add.9), channel_id=1, replica_groups=mesh['x_lo'=2,'z_hi'=4,'z_lo'=4,'y'=4,'x_hi'=2,'core'=2] {'y','x_hi'}, dimensions={0} | all-to-all | bytes 1048576 | tf_op jit(solution)/shard_map/all_to_all | solution.py:336
  29.1 12.5 %all_to_all.46.mine_ref = f32[8,128,128]{2,1,0:T(8,128)S(1)} all-to-all(f32[8,128,128]{2,1,0:T(8,128)S(1)} %broadcast_in_dim.12), channel_id=1, replica_groups=mesh['x_lo'=2,'z_hi'=4,'z_lo'=4,'y'=4,'x_hi'=2,'core'=2] {'y','x_hi'}, dimensions={0} | all-to-all | bytes 1048576 | tf_op jit(solution)/shard_map/all_to_all | solution.py:341
  41.5 4.4 %collective-permute-start.1 = (f32[8,128,128]{2,1,0:T(8,128)S(1)}, f32[8,128,128]{2,1,0:T(8,128)S(1)}, u32[]{:S(2)}, u32[]{:S(2)}) collective-permute-start(f32[8,128,128]{2,1,0:T(8,128)S(1)} %all_to_all.46.mine_ref), channel_id=1, source_target_pairs={{0,1},{1,0},{2,3},{3,2},{4,5},{5,4},{6,7},{7,6},{8,9},{9,8},{10,11... | collective-permute-start | bytes 1572872 | tf_op jit(solution)/shard_map/ppermute | solution.py:352
  45.9 1.5 collective-permute-done.1.other_ref
  47.4 4.2 %back_parts.1 = f32[8,80,128]{2,1,0:T(8,128)S(1)} custom-call(s32[1]{0:T(128)} %bitcast.core_ref, f32[2048,512]{1,0:T(8,128)} %a_ref.5, f32[8,128,128]{2,1,0:T(8,128)S(1)} %all_to_all.46.mine_ref, f32[8,128,128]{2,1,0:T(8,128)S(1)} %collective-permute-done.1.other_ref), custom_call_target="tpu_custom_call" | custom-call | tf_op jit(solution)/shard_map/back_parts/pallas_call | solution.py:302
  51.7 13.4 %all_to_all.47 = f32[8,80,128]{2,1,0:T(8,128)S(1)} all-to-all(f32[8,80,128]{2,1,0:T(8,128)S(1)} %back_parts.1), channel_id=1, replica_groups=mesh['x_lo'=2,'z_hi'=4,'z_lo'=4,'y'=4,'x_hi'=2,'core'=2] {'x_lo','z_lo'}, dimensions={0} | all-to-all | bytes 655360 | tf_op jit(solution)/shard_map/all_to_all | solution.py:336
  65.1 26.6 %all_to_all.48 = f32[4,80,128]{2,1,0:T(8,128)S(1)} all-to-all(f32[4,80,128]{2,1,0:T(8,128)S(1)} %broadcast_in_dim.13), channel_id=1, replica_groups=mesh['x_lo'=2,'z_hi'=4,'z_lo'=4,'y'=4,'x_hi'=2,'core'=2] {'z_hi'}, dimensions={0} | all-to-all | bytes 327680 | tf_op jit(solution)/shard_map/all_to_all | solution.py:341
  91.8 10.4 %all_to_all.49.both_ref = f32[8,80,128]{2,1,0:T(8,128)S(1)} all-to-all(f32[8,80,128]{2,1,0:T(8,128)S(1)} %broadcast_in_dim.14), channel_id=1, replica_groups=mesh['x_lo'=2,'z_hi'=4,'z_lo'=4,'y'=4,'x_hi'=2,'core'=2] {'x_lo','z_lo'}, dimensions={0} | all-to-all | bytes 655360 | tf_op jit(solution)/shard_map/all_to_all | solution.py:341
  102.2 5.7 %range_parts.1 = (f32[8,128,128]{2,1,0:T(8,128)S(1)}, f32[1096,128]{1,0:T(8,128)S(1)}, f32[72,128]{1,0:T(8,128)S(1)}, f32[2,128,128]{2,1,0:T(8,128)S(1)}) custom-call(s32[1]{0:T(128)} %bitcast.core_ref, f32[2048,512]{1,0:T(8,128)} %a_ref.5, f32[8,80,128]{2,1,0:T(8,128)S(1)} %all_to_all.49.both_ref), custom_call_target="tpu_custom_call" | custom-call | tf_op jit(solution)/shard_map/range_parts/pallas_call | solution.py:310
  107.9 7.3 %collective-permute-start.2 = (f32[1096,128]{1,0:T(8,128)S(1)}, f32[1096,128]{1,0:T(8,128)S(1)}, u32[]{:S(2)}, u32[]{:S(2)}) collective-permute-start(f32[1096,128]{1,0:T(8,128)S(1)} %get-tuple-element.17), channel_id=1, source_target_pairs={{0,1},{1,0},{2,3},{3,2},{4,5},{5,4},{6,7},{7,6},{8,9},{9,8},{10,11... | collective-permute-start | bytes 1683464 | tf_op jit(solution)/shard_map/ppermute | solution.py:358
  115.2 1.6 collective-permute-done.2
  116.8 0.1 add.10
  116.9 0.1 pad_maximum_fusion
  117.0 17.3 %all_to_all.50.parts_ref = f32[8,200,128]{2,1,0:T(8,128)S(1)} all-to-all(f32[8,200,128]{2,1,0:T(8,128)S(1)} %pad_maximum_fusion), channel_id=1, replica_groups=mesh['x_lo'=2,'z_hi'=4,'z_lo'=4,'y'=4,'x_hi'=2,'core'=2] {'y','x_hi'}, dimensions={0} | all-to-all | bytes 1638400 | tf_op jit(solution)/shard_map/all_to_all | solution.py:363
  134.3 4.6 %last_gram.1 = (f32[128,128]{1,0:T(8,128)S(1)}, f32[128,128]{1,0:T(8,128)S(1)}, f32[128,128]{1,0:T(8,128)}) custom-call(f32[8,200,128]{2,1,0:T(8,128)S(1)} %all_to_all.50.parts_ref, f32[2,128,128]{2,1,0:T(8,128)S(1)} %get-tuple-element.19.turn_ref, f32[128,128]{1,0:T(8,128)S(1)} %reduce_sum.45.image_ref), custom_call_target="tpu_custom_call" | custom-call | tf_op jit(solution)/shard_map/last_gram/pallas_call | solution.py:315
  138.9 11.5 %all_to_all.51 = f32[32,4,128]{2,1,0:T(4,128)S(1)} all-to-all(f32[32,4,128]{2,1,0:T(4,128)S(1)} %bitcast.5), channel_id=1, replica_groups=mesh['x_lo'=2,'z_hi'=4,'z_lo'=4,'y'=4,'x_hi'=2,'core'=2] {'x_lo','y','x_..., dimensions={0} | all-to-all | bytes 131072 | tf_op jit(solution)/shard_map/all_to_all | solution.py:336
  150.5 15.1 %all_to_all.52 = f32[16,4,128]{2,1,0:T(4,128)S(1)} all-to-all(f32[16,4,128]{2,1,0:T(4,128)S(1)} %broadcast_in_dim.16), channel_id=1, replica_groups=mesh['x_lo'=2,'z_hi'=4,'z_lo'=4,'y'=4,'x_hi'=2,'core'=2] {'z_hi','z_lo'}, dimensions={0} | all-to-all | bytes 65536 | tf_op jit(solution)/shard_map/all_to_all | solution.py:341
  165.6 12.3 %all_to_all.53 = f32[32,4,128]{2,1,0:T(4,128)S(1)} all-to-all(f32[32,4,128]{2,1,0:T(4,128)S(1)} %broadcast_in_dim.17), channel_id=1, replica_groups=mesh['x_lo'=2,'z_hi'=4,'z_lo'=4,'y'=4,'x_hi'=2,'core'=2] {'x_lo','y','x_..., dimensions={0} | all-to-all | bytes 131072 | tf_op jit(solution)/shard_map/all_to_all | solution.py:341
  177.9 4.4 %basis.1 = (f32[128,128]{1,0:T(8,128)}, f32[128,128]{1,0:T(8,128)}) custom-call(f32[128,128]{1,0:T(8,128)S(1)} %bitcast.4, f32[128,128]{1,0:T(8,128)S(1)} %get-tuple-element.22.refs_1_), custom_call_target="tpu_custom_call" | custom-call | tf_op jit(solution)/shard_map/basis/pallas_call | solution.py:326
  (13 shorter events, 0.3 us)
Async XLA Ops:
  4.9 10.3 %collective-permute-start = (f32[8,128,128]{2,1,0:T(8,128)S(1)}, f32[8,128,128]{2,1,0:T(8,128)S(1)}, u32[]{:S(2)}, u32[]{:S(2)}) collective-permute-start(f32[8,128,128]{2,1,0:T(8,128)S(1)} %get-tuple-element.15), channel_id=1, source_target_pairs={{0,1},{1,0},{2,3},{3,2},{4,5},{5,4},{6,7},{7,6},{8,9},{9,8},{10,11... | collective-permute-start | bytes 1572872 | tf_op jit(solution)/shard_map/ppermute | solution.py:350
  41.5 5.9 %collective-permute-start.1 = (f32[8,128,128]{2,1,0:T(8,128)S(1)}, f32[8,128,128]{2,1,0:T(8,128)S(1)}, u32[]{:S(2)}, u32[]{:S(2)}) collective-permute-start(f32[8,128,128]{2,1,0:T(8,128)S(1)} %all_to_all.46.mine_ref), channel_id=1, source_target_pairs={{0,1},{1,0},{2,3},{3,2},{4,5},{5,4},{6,7},{7,6},{8,9},{9,8},{10,11... | collective-permute-start | bytes 1572872 | tf_op jit(solution)/shard_map/ppermute | solution.py:352
  107.9 8.9 %collective-permute-start.2 = (f32[1096,128]{1,0:T(8,128)S(1)}, f32[1096,128]{1,0:T(8,128)S(1)}, u32[]{:S(2)}, u32[]{:S(2)}) collective-permute-start(f32[1096,128]{1,0:T(8,128)S(1)} %get-tuple-element.17), channel_id=1, source_target_pairs={{0,1},{1,0},{2,3},{3,2},{4,5},{5,4},{6,7},{7,6},{8,9},{9,8},{10,11... | collective-permute-start | bytes 1683464 | tf_op jit(solution)/shard_map/ppermute | solution.py:358

commit v9 on v8

--- a/solution.py
+++ b/solution.py
@@ -11,8 +11,8 @@
 BLOCK = 1024
 FIRST_PANEL = 8
 PLANE = ("y", "x_hi")
-NEAR = ("x_lo", "z_lo")
-CROSS = ("x_lo", "y", "x_hi", "core")
+NEAR = ("z_lo", "x_lo")
+CROSS = ("core", "x_hi", "y", "x_lo")
 PARAMS = pltpu.CompilerParams(vmem_limit_bytes=32 * 1024 * 1024)
 
 

time: 183 us -> 183 us (level)
  no operation moved by 1% of the time
where the time goes in v9:
time: 183 us; the launch traced here: 182 us
  blocking collectives  133 us (73%)
  Pallas kernels  23.1 us (13%)
  starting transfers between devices  20.4 us (11%)
  waiting for transfers between devices  4.6 us (3%)
    all_to_all x5, blocking collectives, gather(): lax.all_to_all(jnp.broadcast_to(block[None], (count,) + block.shape), axi...  76.9 us
    all_to_all x3, blocking collectives, scatter_sum(): return jnp.sum(lax.all_to_all(parts, axis, 0, 0), axis=0)  38.4 us
    all_to_all x1, blocking collectives, per_device(): parts = lax.all_to_all(parts, PLANE, 0, 0)  17.3 us
    ppermute x1, starting transfers between devices, per_device(): image_block = scatter_sum(keep + lax.ppermute(send, 'core', SWAP), PLANE)  8.79 us
    ppermute x1, starting transfers between devices, per_device(): received = lax.ppermute(send, 'core', SWAP)  7.26 us
    pallas_call x1, Pallas kernels, range_parts(): reading(range_kernel, a, [pltpu.VMEM], out_shape, spread(n), 'range_parts')  5.69 us
    pallas_call x1, Pallas kernels, last_gram(): pl.pallas_call(last_gram_kernel, out_shape=[shape(n, n)] * 3, scratch_sha...  4.63 us
    ppermute x1, starting transfers between devices, per_device(): other = lax.ppermute(mine, 'core', SWAP)  4.39 us
  transfers between devices with their start and end apart: 3, of which 3 were waited for; matrix products, arithmetic and copies ran while one was open for 0% of the time, Pallas kernels for 0%

profile of v9, /device:TPU:1, one launch (start us, length us, event | category | flops | bytes accessed | tf_op | source)
XLA Modules:
  0.0 182.1 jit_solution(15308131379255340733)
XLA Ops:
  0.6 4.2 %image_parts.1 = (f32[8,128,128]{2,1,0:T(8,128)S(1)}, f32[8,128,128]{2,1,0:T(8,128)S(1)}) custom-call(s32[1]{0:T(128)} %bitcast.core_ref, f32[2048,512]{1,0:T(8,128)} %a_ref.5, f32[512,128]{1,0:T(8,128)} %s_ref.1), custom_call_target="tpu_custom_call" | custom-call | tf_op jit(solution)/shard_map/image_parts/pallas_call | solution.py:295
  4.9 8.8 %collective-permute-start = (f32[8,128,128]{2,1,0:T(8,128)S(1)}, f32[8,128,128]{2,1,0:T(8,128)S(1)}, u32[]{:S(2)}, u32[]{:S(2)}) collective-permute-start(f32[8,128,128]{2,1,0:T(8,128)S(1)} %get-tuple-element.15), channel_id=1, source_target_pairs={{0,1},{1,0},{2,3},{3,2},{4,5},{5,4},{6,7},{7,6},{8,9},{9,8},{10,11... | collective-permute-start | bytes 1572872 | tf_op jit(solution)/shard_map/ppermute | solution.py:350
  13.7 1.5 collective-permute-done
  15.2 0.1 add.9
  15.2 13.8 %all_to_all.45 = f32[8,128,128]{2,1,0:T(8,128)S(1)} all-to-all(f32[8,128,128]{2,1,0:T(8,128)S(1)} %add.9), channel_id=1, replica_groups=mesh['x_lo'=2,'z_hi'=4,'z_lo'=4,'y'=4,'x_hi'=2,'core'=2] {'y','x_hi'}, dimensions={0} | all-to-all | bytes 1048576 | tf_op jit(solution)/shard_map/all_to_all | solution.py:336
  29.1 12.5 %all_to_all.46.mine_ref = f32[8,128,128]{2,1,0:T(8,128)S(1)} all-to-all(f32[8,128,128]{2,1,0:T(8,128)S(1)} %broadcast_in_dim.12), channel_id=1, replica_groups=mesh['x_lo'=2,'z_hi'=4,'z_lo'=4,'y'=4,'x_hi'=2,'core'=2] {'y','x_hi'}, dimensions={0} | all-to-all | bytes 1048576 | tf_op jit(solution)/shard_map/all_to_all | solution.py:341
  41.5 4.4 %collective-permute-start.1 = (f32[8,128,128]{2,1,0:T(8,128)S(1)}, f32[8,128,128]{2,1,0:T(8,128)S(1)}, u32[]{:S(2)}, u32[]{:S(2)}) collective-permute-start(f32[8,128,128]{2,1,0:T(8,128)S(1)} %all_to_all.46.mine_ref), channel_id=1, source_target_pairs={{0,1},{1,0},{2,3},{3,2},{4,5},{5,4},{6,7},{7,6},{8,9},{9,8},{10,11... | collective-permute-start | bytes 1572872 | tf_op jit(solution)/shard_map/ppermute | solution.py:352
  45.9 1.5 collective-permute-done.1.other_ref
  47.4 4.2 %back_parts.1 = f32[8,80,128]{2,1,0:T(8,128)S(1)} custom-call(s32[1]{0:T(128)} %bitcast.core_ref, f32[2048,512]{1,0:T(8,128)} %a_ref.5, f32[8,128,128]{2,1,0:T(8,128)S(1)} %all_to_all.46.mine_ref, f32[8,128,128]{2,1,0:T(8,128)S(1)} %collective-permute-done.1.other_ref), custom_call_target="tpu_custom_call" | custom-call | tf_op jit(solution)/shard_map/back_parts/pallas_call | solution.py:302
  51.7 13.2 %all_to_all.47 = f32[8,80,128]{2,1,0:T(8,128)S(1)} all-to-all(f32[8,80,128]{2,1,0:T(8,128)S(1)} %back_parts.1), channel_id=1, replica_groups=mesh['x_lo'=2,'z_hi'=4,'z_lo'=4,'y'=4,'x_hi'=2,'core'=2] {'z_lo','x_lo'}, dimensions={0} | all-to-all | bytes 655360 | tf_op jit(solution)/shard_map/all_to_all | solution.py:336
  64.9 26.5 %all_to_all.48 = f32[4,80,128]{2,1,0:T(8,128)S(1)} all-to-all(f32[4,80,128]{2,1,0:T(8,128)S(1)} %broadcast_in_dim.13), channel_id=1, replica_groups=mesh['x_lo'=2,'z_hi'=4,'z_lo'=4,'y'=4,'x_hi'=2,'core'=2] {'z_hi'}, dimensions={0} | all-to-all | bytes 327680 | tf_op jit(solution)/shard_map/all_to_all | solution.py:341
  91.5 10.5 %all_to_all.49.both_ref = f32[8,80,128]{2,1,0:T(8,128)S(1)} all-to-all(f32[8,80,128]{2,1,0:T(8,128)S(1)} %broadcast_in_dim.14), channel_id=1, replica_groups=mesh['x_lo'=2,'z_hi'=4,'z_lo'=4,'y'=4,'x_hi'=2,'core'=2] {'z_lo','x_lo'}, dimensions={0} | all-to-all | bytes 655360 | tf_op jit(solution)/shard_map/all_to_all | solution.py:341
  101.9 5.7 %range_parts.1 = (f32[8,128,128]{2,1,0:T(8,128)S(1)}, f32[1096,128]{1,0:T(8,128)S(1)}, f32[72,128]{1,0:T(8,128)S(1)}, f32[2,128,128]{2,1,0:T(8,128)S(1)}) custom-call(s32[1]{0:T(128)} %bitcast.core_ref, f32[2048,512]{1,0:T(8,128)} %a_ref.5, f32[8,80,128]{2,1,0:T(8,128)S(1)} %all_to_all.49.both_ref), custom_call_target="tpu_custom_call" | custom-call | tf_op jit(solution)/shard_map/range_parts/pallas_call | solution.py:310
  107.6 7.3 %collective-permute-start.2 = (f32[1096,128]{1,0:T(8,128)S(1)}, f32[1096,128]{1,0:T(8,128)S(1)}, u32[]{:S(2)}, u32[]{:S(2)}) collective-permute-start(f32[1096,128]{1,0:T(8,128)S(1)} %get-tuple-element.17), channel_id=1, source_target_pairs={{0,1},{1,0},{2,3},{3,2},{4,5},{5,4},{6,7},{7,6},{8,9},{9,8},{10,11... | collective-permute-start | bytes 1683464 | tf_op jit(solution)/shard_map/ppermute | solution.py:358
  114.9 1.6 collective-permute-done.2
  116.5 0.1 add.10
  116.6 0.1 pad_maximum_fusion
  116.7 17.3 %all_to_all.50.parts_ref = f32[8,200,128]{2,1,0:T(8,128)S(1)} all-to-all(f32[8,200,128]{2,1,0:T(8,128)S(1)} %pad_maximum_fusion), channel_id=1, replica_groups=mesh['x_lo'=2,'z_hi'=4,'z_lo'=4,'y'=4,'x_hi'=2,'core'=2] {'y','x_hi'}, dimensions={0} | all-to-all | bytes 1638400 | tf_op jit(solution)/shard_map/all_to_all | solution.py:363
  134.0 4.6 %last_gram.1 = (f32[128,128]{1,0:T(8,128)S(1)}, f32[128,128]{1,0:T(8,128)S(1)}, f32[128,128]{1,0:T(8,128)}) custom-call(f32[8,200,128]{2,1,0:T(8,128)S(1)} %all_to_all.50.parts_ref, f32[2,128,128]{2,1,0:T(8,128)S(1)} %get-tuple-element.19.turn_ref, f32[128,128]{1,0:T(8,128)S(1)} %reduce_sum.45.image_ref), custom_call_target="tpu_custom_call" | custom-call | tf_op jit(solution)/shard_map/last_gram/pallas_call | solution.py:315
  138.6 11.4 %all_to_all.51 = f32[32,4,128]{2,1,0:T(4,128)S(1)} all-to-all(f32[32,4,128]{2,1,0:T(4,128)S(1)} %bitcast.5), channel_id=1, replica_groups=mesh['x_lo'=2,'z_hi'=4,'z_lo'=4,'y'=4,'x_hi'=2,'core'=2] {'core','x_hi',..., dimensions={0} | all-to-all | bytes 131072 | tf_op jit(solution)/shard_map/all_to_all | solution.py:336
  150.1 15.2 %all_to_all.52 = f32[16,4,128]{2,1,0:T(4,128)S(1)} all-to-all(f32[16,4,128]{2,1,0:T(4,128)S(1)} %broadcast_in_dim.16), channel_id=1, replica_groups=mesh['x_lo'=2,'z_hi'=4,'z_lo'=4,'y'=4,'x_hi'=2,'core'=2] {'z_hi','z_lo'}, dimensions={0} | all-to-all | bytes 65536 | tf_op jit(solution)/shard_map/all_to_all | solution.py:341
  165.4 12.3 %all_to_all.53 = f32[32,4,128]{2,1,0:T(4,128)S(1)} all-to-all(f32[32,4,128]{2,1,0:T(4,128)S(1)} %broadcast_in_dim.17), channel_id=1, replica_groups=mesh['x_lo'=2,'z_hi'=4,'z_lo'=4,'y'=4,'x_hi'=2,'core'=2] {'core','x_hi',..., dimensions={0} | all-to-all | bytes 131072 | tf_op jit(solution)/shard_map/all_to_all | solution.py:341
  177.7 4.4 %basis.1 = (f32[128,128]{1,0:T(8,128)}, f32[128,128]{1,0:T(8,128)}) custom-call(f32[128,128]{1,0:T(8,128)S(1)} %bitcast.4, f32[128,128]{1,0:T(8,128)S(1)} %get-tuple-element.22.refs_1_), custom_call_target="tpu_custom_call" | custom-call | tf_op jit(solution)/shard_map/basis/pallas_call | solution.py:326
  (13 shorter events, 0.3 us)
Async XLA Ops:
  4.9 10.3 %collective-permute-start = (f32[8,128,128]{2,1,0:T(8,128)S(1)}, f32[8,128,128]{2,1,0:T(8,128)S(1)}, u32[]{:S(2)}, u32[]{:S(2)}) collective-permute-start(f32[8,128,128]{2,1,0:T(8,128)S(1)} %get-tuple-element.15), channel_id=1, source_target_pairs={{0,1},{1,0},{2,3},{3,2},{4,5},{5,4},{6,7},{7,6},{8,9},{9,8},{10,11... | collective-permute-start | bytes 1572872 | tf_op jit(solution)/shard_map/ppermute | solution.py:350
  41.5 5.9 %collective-permute-start.1 = (f32[8,128,128]{2,1,0:T(8,128)S(1)}, f32[8,128,128]{2,1,0:T(8,128)S(1)}, u32[]{:S(2)}, u32[]{:S(2)}) collective-permute-start(f32[8,128,128]{2,1,0:T(8,128)S(1)} %all_to_all.46.mine_ref), channel_id=1, source_target_pairs={{0,1},{1,0},{2,3},{3,2},{4,5},{5,4},{6,7},{7,6},{8,9},{9,8},{10,11... | collective-permute-start | bytes 1572872 | tf_op jit(solution)/shard_map/ppermute | solution.py:352
  107.6 8.8 %collective-permute-start.2 = (f32[1096,128]{1,0:T(8,128)S(1)}, f32[1096,128]{1,0:T(8,128)S(1)}, u32[]{:S(2)}, u32[]{:S(2)}) collective-permute-start(f32[1096,128]{1,0:T(8,128)S(1)} %get-tuple-element.17), channel_id=1, source_target_pairs={{0,1},{1,0},{2,3},{3,2},{4,5},{5,4},{6,7},{7,6},{8,9},{9,8},{10,11... | collective-permute-start | bytes 1683464 | tf_op jit(solution)/shard_map/ppermute | solution.py:358
